TPU v7x, 32 devices: a whole 2x2x4 slice. The times are simulated.
32 devices in a mesh: section: 2 (over core), dp: 4 (over y, x), tensor: 4 (over z).
Axes of the slice: x: 2, y: 2, z: 4, core: 2. Of those that a mesh axis runs over, the one named last changes fastest.
Arguments:
- inputs: bfloat16 [8192, 1024], P('dp'), may hold values from -6 to 6
- out_grad: bfloat16 [8192, 1024], P('dp'), may hold values from -6 to 6
- w_query: bfloat16 [2, 1024, 1024], P('section', None, 'tensor'), may hold values from -0.1875 to 0.1875
- w_latent: bfloat16 [2, 1024, 512], P('section'), may hold values from -0.1875 to 0.1875
- w_key_up: bfloat16 [2, 256, 1024], P('section', None, 'tensor'), may hold values from -0.375 to 0.375
- w_value_up: bfloat16 [2, 256, 1024], P('section', None, 'tensor'), may hold values from -0.375 to 0.375
- w_out: bfloat16 [2, 1024, 1024], P('section', 'tensor'), may hold values from -3 to 3
- w_gate: bfloat16 [2, 1024, 2816], P('section', None, 'tensor'), may hold values from -0.1875 to 0.1875
- w_up: bfloat16 [2, 1024, 2816], P('section', None, 'tensor'), may hold values from -0.1875 to 0.1875
- w_down: bfloat16 [2, 2816, 1024], P('section', 'tensor'), may hold values from -0.109375 to 0.109375
- norm_attn: float32 [2, 1024], P('section'), may hold values from 0.1 to 1.9
- norm_mlp: float32 [2, 1024], P('section'), may hold values from 0.1 to 1.9
Outputs:
- layer_out: bfloat16 [2, 8192, 1024], P('section', 'dp')
- input_grad: bfloat16 [2, 8192, 1024], P('section', 'dp')
- grad_query: float32 [2, 1024, 1024], P('section', None, 'tensor')
- grad_latent: float32 [2, 1024, 512], P('section', 'tensor')
- grad_key_up: float32 [2, 256, 1024], P('section', None, 'tensor')
- grad_value_up: float32 [2, 256, 1024], P('section', None, 'tensor')
- grad_out: float32 [2, 1024, 1024], P('section', 'tensor')
- grad_gate: float32 [2, 1024, 2816], P('section', None, 'tensor')
- grad_up: float32 [2, 1024, 2816], P('section', None, 'tensor')
- grad_down: float32 [2, 2816, 1024], P('section', 'tensor')
- grad_norm_attn: float32 [2, 1024], P('section', 'tensor')
- grad_norm_mlp: float32 [2, 1024], P('section', 'tensor')
All inputs are finite; a program needn't handle non-finite values.
Results may differ from a plain program's by a relative error of at most 0.035.
Values may be sent and summed in bfloat16 or wider, within the bound.
A program may use at most 256 MiB of HBM per device.

v0:
```python
import functools
import math

import jax
import jax.numpy as jnp
from jax import lax
from jax.experimental import pallas as pl
from jax.experimental.pallas import tpu as pltpu
from jax.sharding import PartitionSpec as P

QH = 16
HD = 64
KVH = 2
LH = 256
LEN = 1024
EPS = 1e-05
F32 = jnp.float32
BF16 = jnp.bfloat16
SEC, DP, TEN = "section", "dp", "tensor"
LOG2_SCALE = HD**-0.5 * math.log2(math.e)
KEY_ROWS = 256


def mm(left, right, left_dim=1, right_dim=0):
    dims = (((left_dim,), (right_dim,)), ((), ()))
    return lax.dot_general(left, right, dims, preferred_element_type=F32)


def head_masks(width):
    if width == HD:
        return [None]
    lane = lax.broadcasted_iota(jnp.int32, (1, width), 1)
    return [lane // HD == j for j in range(width // HD)]


def keep_head(block, mask):
    return block if mask is None else jnp.where(mask, block, jnp.zeros_like(block))


def attend_kernel(q_ref, k_ref, v_ref, o_ref, norm_ref):
    width = q_ref.shape[1]
    masks = head_masks(width)
    rows = KEY_ROWS
    place_k = lax.broadcasted_iota(jnp.int32, (rows, rows), 0)
    place_q = lax.broadcasted_iota(jnp.int32, (rows, rows), 1)
    for start in range(0, LEN, rows):
        query = q_ref[start : start + rows, :]
        total = None
        for j, mask in enumerate(masks):
            query_j = keep_head(query, mask)
            scores = mm(k_ref[start : start + rows, :], query_j, 1, 1) * LOG2_SCALE
            scores = jnp.where(place_k <= place_q, scores, -jnp.inf)
            largest = jnp.max(scores, axis=0, keepdims=True)
            if start:
                before = mm(k_ref[0:start, :], query_j, 1, 1) * LOG2_SCALE
                largest = jnp.maximum(largest, jnp.max(before, axis=0, keepdims=True))
            weight = jnp.exp2(scores - largest)
            norm = jnp.sum(weight, axis=0, keepdims=True)
            value = keep_head(v_ref[start : start + rows, :], mask)
            out = mm(value, weight.astype(BF16), 0, 0)
            if start:
                weight = jnp.exp2(before - largest)
                norm = norm + jnp.sum(weight, axis=0, keepdims=True)
                value = keep_head(v_ref[0:start, :], mask)
                out = out + mm(value, weight.astype(BF16), 0, 0)
            out = out / norm
            total = out if total is None else total + out
            norm_ref[0, j : j + 1, start : start + rows] = largest + jnp.log2(norm)
        o_ref[start : start + rows, :] = total.T.astype(BF16)


def attend_forward(queries, keys, values):
    rows, columns = queries.shape
    width = min(2 * HD, columns)
    heads = width // HD
    spec = pl.BlockSpec((rows, width), lambda i: (0, i))
    return pl.pallas_call(
        attend_kernel,
        grid=(columns // width,),
        in_specs=[spec] * 3,
        out_specs=[spec, pl.BlockSpec((1, heads, rows), lambda i: (i, 0, 0))],
        out_shape=[
            jax.ShapeDtypeStruct((rows, columns), BF16),
            jax.ShapeDtypeStruct((columns // width, heads, rows), F32),
        ],
        compiler_params=pltpu.CompilerParams(vmem_limit_bytes=40 * 2**20),
        cost_estimate=pl.CostEstimate(
            flops=rows * rows * columns * 8, bytes_accessed=rows * columns * 8, transcendentals=0
        ),
    )(queries, keys, values)


def attend_back_kernel(q_ref, k_ref, v_ref, o_ref, g_ref, norm_ref, dq_ref, dk_ref, dv_ref, acc):
    width = q_ref.shape[1]
    masks = head_masks(width)
    rows = KEY_ROWS
    place_k = lax.broadcasted_iota(jnp.int32, (rows, rows), 0)
    place_q = lax.broadcasted_iota(jnp.int32, (rows, rows), 1)
    product = g_ref[...].astype(F32) * o_ref[...].astype(F32)
    product = product.T
    acc[...] = jnp.zeros_like(acc)
    deltas = [
        jnp.sum(product[j * HD : (j + 1) * HD, :], axis=0, keepdims=True)
        for j in range(len(masks))
    ]
    for start in range(0, LEN, rows):
        end = start + rows
        key = k_ref[start:end, :]
        value = v_ref[start:end, :]
        grad_key = grad_value = None
        for j, mask in enumerate(masks):
            query_j = keep_head(q_ref[start:, :], mask)
            grad_j = keep_head(g_ref[start:, :], mask)
            scores = mm(key, query_j, 1, 1) * LOG2_SCALE
            probs = jnp.exp2(scores - norm_ref[0, j : j + 1, start:])
            first = jnp.where(place_k <= place_q, probs[:, :rows], 0.0)
            probs = first if end == LEN else jnp.concatenate([first, probs[:, rows:]], axis=1)
            grad_probs = mm(value, grad_j, 1, 1)
            grad_scores = (probs * (grad_probs - deltas[j][:, start:])).astype(BF16)
            value_term = mm(probs.astype(BF16), grad_j)
            key_term = mm(grad_scores, query_j)
            grad_key = key_term if grad_key is None else grad_key + key_term
            grad_value = value_term if grad_value is None else grad_value + value_term
            acc[:, start:] += mm(keep_head(key, mask), grad_scores, 0, 0)
        dk_ref[start:end, :] = (grad_key * HD**-0.5).astype(BF16)
        dv_ref[start:end, :] = grad_value.astype(BF16)
    dq_ref[...] = (acc[...].T * HD**-0.5).astype(BF16)


def attend_backward(queries, keys, values, heads_out, grad_heads, norms):
    rows, columns = queries.shape
    width = min(2 * HD, columns)
    heads = width // HD
    spec = pl.BlockSpec((rows, width), lambda i: (0, i))
    shape = jax.ShapeDtypeStruct((rows, columns), BF16)
    return pl.pallas_call(
        attend_back_kernel,
        grid=(columns // width,),
        in_specs=[spec] * 5 + [pl.BlockSpec((1, heads, rows), lambda i: (i, 0, 0))],
        out_specs=[spec] * 3,
        out_shape=[shape] * 3,
        scratch_shapes=[pltpu.VMEM((width, rows), F32)],
        compiler_params=pltpu.CompilerParams(vmem_limit_bytes=40 * 2**20),
        cost_estimate=pl.CostEstimate(
            flops=rows * rows * columns * 20, bytes_accessed=rows * columns * 16, transcendentals=0
        ),
    )(queries, keys, values, heads_out, grad_heads, norms)


def rms_scale(features):
    return features * lax.rsqrt(jnp.mean(features * features, axis=-1, keepdims=True) + EPS)


def norm_backward(source, gain, upstream):
    inverse = lax.rsqrt(jnp.mean(source * source, axis=-1, keepdims=True) + EPS)
    normed = source * inverse
    scaled = upstream * gain
    grad_source = inverse * (scaled - normed * jnp.mean(scaled * normed, axis=-1, keepdims=True))
    return grad_source, jnp.sum(upstream * normed, axis=0)


class Place:
    def __init__(self):
        self.count = lax.axis_size(TEN)
        self.team = self.count // 2
        self.z = lax.axis_index(TEN)
        self.core = lax.axis_index(SEC)
        self.dp = lax.axis_index(DP)
        self.sequence = self.z // self.team
        self.first = self.core == 0

    def swap(self, block):
        return lax.ppermute(block, SEC, [(0, 1), (1, 0)])

    def opposite(self, block, cores=(0, 1)):
        n, t = self.count, self.team
        route = [(c * n + z, c * n + (z + t) % n) for c in cores for z in range(n)]
        return lax.ppermute(block, (SEC, TEN), route)

    def across(self, block, cores=(0, 1)):
        n, t = self.count, self.team
        route = [(c * n + z, (1 - c) * n + (z + t) % n) for c in cores for z in range(n)]
        return lax.ppermute(block, (SEC, TEN), route)

    def team_sum(self, block):
        n, t = self.count, self.team
        parts = [block]
        for step in range(1, t):
            route = [(z, z // t * t + (z - step) % t) for z in range(n)]
            parts.append(lax.ppermute(block, TEN, route))
        if t == 2:
            return parts[0].astype(F32) + parts[1].astype(F32)
        stacked = jnp.roll(jnp.stack(parts), self.z % t, axis=0)
        return jnp.sum(stacked.astype(F32), axis=0)

    def own_half(self, block):
        half = block.shape[0] // 2
        return lax.dynamic_slice_in_dim(block, self.core * half, half, 0)

    def other_half(self, block):
        half = block.shape[0] // 2
        return lax.dynamic_slice_in_dim(block, (1 - self.core) * half, half, 0)

    def reduce(self, partial):
        got = self.swap(self.other_half(partial.astype(BF16)))
        mine = self.own_half(partial) + got.astype(F32)
        return self.team_sum(mine.astype(BF16))

    def join(self, own):
        other = self.swap(own)
        return jnp.concatenate(
            [jnp.where(self.first, own, other), jnp.where(self.first, other, own)], axis=0
        )


def pack_columns(matrix, width):
    return [matrix[:, i : i + width] for i in range(0, matrix.shape[1], width)]


def pack_attention(query, key_up, value_up, out):
    width = query.shape[1]
    return jnp.concatenate([query, key_up, value_up] + pack_columns(out, width), axis=0)


def unpack_attention(packed, model):
    width = packed.shape[1]
    query = packed[:model]
    key_up = packed[model : model + LH]
    value_up = packed[model + LH : model + 2 * LH]
    rest = packed[model + 2 * LH :]
    out = jnp.concatenate([rest[i : i + width] for i in range(0, rest.shape[0], width)], axis=1)
    return query, key_up, value_up, out


CHUNKS = 2


def chunk(block, index):
    rows = block.shape[0] // CHUNKS
    return block[index * rows : (index + 1) * rows]


def layer_forward(at, source, weights):
    w_query, w_key_up, w_value_up, w_out, w_gate, w_up, w_down, w_latent, gain_attn, gain_mlp = weights
    attn_in = (rms_scale(source.astype(F32)) * gain_attn).astype(BF16)
    queries = mm(attn_in, w_query).astype(BF16)
    latents = mm(attn_in, w_latent).astype(BF16)
    keys = mm(latents, w_key_up).astype(BF16)
    values = mm(latents, w_value_up).astype(BF16)
    heads_out, norms = attend_forward(queries, keys, values)
    residuals, mlp_ins, gates, ups, hiddens, outputs = [], [], [], [], [], []
    for i in range(CHUNKS):
        attended = at.reduce(mm(chunk(heads_out, i), w_out))
        residual = at.own_half(chunk(source, i)).astype(F32) + attended
        residuals.append(residual)
        mlp_ins.append(at.join((rms_scale(residual) * gain_mlp).astype(BF16)))
    for i in range(CHUNKS):
        gate = mm(mlp_ins[i], w_gate)
        up = mm(mlp_ins[i], w_up)
        hidden = (jax.nn.silu(gate) * up).astype(BF16)
        output = residuals[i] + at.reduce(mm(hidden, w_down))
        outputs.append(at.join(output.astype(BF16)))
        gates.append(gate)
        ups.append(up)
        hiddens.append(hidden)
    whole = functools.partial(jnp.concatenate, axis=0)
    kept = (
        source,
        attn_in,
        queries,
        latents,
        keys,
        values,
        heads_out,
        norms,
        residuals,
        whole(mlp_ins),
        whole(gates),
        whole(ups),
        whole(hiddens),
    )
    return whole(outputs), kept


def layer_backward(at, kept, upstream, weights):
    w_query, w_key_up, w_value_up, w_out, w_gate, w_up, w_down, w_latent, gain_attn, gain_mlp = weights
    source, attn_in, queries, latents, keys, values, heads_out, norms, residuals, mlp_in, gate, up, hidden = kept
    grad_hidden = mm(upstream, w_down, 1, 1)
    sigmoid = jax.nn.sigmoid(gate)
    d_gate = (grad_hidden * up * sigmoid * (1.0 + gate * (1.0 - sigmoid))).astype(BF16)
    d_up = (grad_hidden * gate * sigmoid).astype(BF16)
    d_residuals, gain_mlp_grad = [], 0.0
    joined = []
    for i in range(CHUNKS):
        term = mm(chunk(d_gate, i), w_gate, 1, 1) + mm(chunk(d_up, i), w_up, 1, 1)
        part, gain_part = norm_backward(residuals[i], gain_mlp, at.reduce(term))
        d_residual = at.own_half(chunk(upstream, i)).astype(F32) + part
        d_residuals.append(d_residual)
        gain_mlp_grad = gain_mlp_grad + gain_part
        joined.append(at.join(d_residual.astype(BF16)))
    g_down = mm(hidden, upstream, 0, 0).astype(BF16)
    g_gate = mm(mlp_in, d_gate, 0, 0).astype(BF16)
    g_up = mm(mlp_in, d_up, 0, 0).astype(BF16)
    res_grad = jnp.concatenate(joined, axis=0)
    d_heads = mm(res_grad, w_out, 1, 1).astype(BF16)
    d_queries, d_keys, d_values = attend_backward(queries, keys, values, heads_out, d_heads, norms)
    d_latents = (mm(d_keys, w_key_up, 1, 1) + mm(d_values, w_value_up, 1, 1)).astype(BF16)
    grads, gain_attn_grad = [], 0.0
    for i in range(CHUNKS):
        term = mm(chunk(d_queries, i), w_query, 1, 1) + mm(chunk(d_latents, i), w_latent, 1, 1)
        part, gain_part = norm_backward(
            at.own_half(chunk(source, i)).astype(F32), gain_attn, at.reduce(term)
        )
        gain_attn_grad = gain_attn_grad + gain_part
        grads.append(at.join((d_residuals[i] + part).astype(BF16)))
    g_out = mm(heads_out, res_grad, 0, 0).astype(BF16)
    g_query = mm(attn_in, d_queries, 0, 0).astype(BF16)
    g_key_up = mm(latents, d_keys, 0, 0).astype(BF16)
    g_value_up = mm(latents, d_values, 0, 0).astype(BF16)
    g_latent = mm(attn_in, d_latents, 0, 0).astype(BF16)
    attention = pack_attention(g_query, g_key_up, g_value_up, g_out)
    return jnp.concatenate(grads, axis=0), (
        (attention, g_gate, g_up, g_down),
        g_latent,
        (gain_attn_grad, gain_mlp_grad),
    )


def local(
    inputs,
    out_grad,
    w_query,
    w_latent,
    w_key_up,
    w_value_up,
    w_out,
    w_gate,
    w_up,
    w_down,
    norm_attn,
    norm_mlp,
):
    at = Place()
    model = inputs.shape[1]
    heads = w_query.shape[2] // HD
    dp_count = lax.axis_size(DP)

    def group_of(shard):
        return shard * heads // (QH // KVH)

    opposite_z = (at.z + at.team) % at.count

    def latent_of(shard):
        return lax.dynamic_slice_in_dim(w_latent[0], group_of(shard) * LH, LH, 1)

    def fetch(matrix):
        rows = matrix.shape[0] // dp_count
        piece = lax.dynamic_slice_in_dim(matrix, at.dp * rows, rows, 0)
        return lax.all_gather(at.across(piece), DP, axis=0, tiled=True)

    own_packed = pack_attention(w_query[0], w_key_up[0], w_value_up[0], w_out[0])
    far_attention = unpack_attention(fetch(own_packed), model)
    far_latent = at.swap(latent_of(opposite_z))
    far_gains = at.swap(jnp.concatenate([norm_attn, norm_mlp], axis=0))
    far = far_attention + (fetch(w_gate[0]), fetch(w_up[0]), fetch(w_down[0]))
    far = far + (far_latent, far_gains[0], far_gains[1])
    own = (w_query[0], w_key_up[0], w_value_up[0], w_out[0], w_gate[0], w_up[0], w_down[0])
    own = own + (latent_of(at.z), norm_attn[0], norm_mlp[0])
    weights = [
        tuple(jnp.where(at.first, a, b) for a, b in zip(own, far)),
        tuple(jnp.where(at.first, b, a) for a, b in zip(own, far)),
    ]

    def sequence_rows(block):
        return lax.dynamic_slice_in_dim(block, at.sequence * LEN, LEN, 0)

    source = sequence_rows(inputs)
    first_out, first_kept = layer_forward(at, source, weights[0])
    second_out, second_kept = layer_forward(at, first_out, weights[1])
    second_grad, second_totals = layer_backward(at, second_kept, sequence_rows(out_grad), weights[1])
    first_grad, first_totals = layer_backward(at, first_kept, second_grad, weights[0])

    def both_sequences(mine, other):
        top = at.sequence == 0
        return jnp.concatenate([jnp.where(top, mine, other), jnp.where(top, other, mine)], axis=0)[None]

    layer_mine = jnp.where(at.first, first_out, second_out)
    layer_out = both_sequences(layer_mine, at.opposite(layer_mine))
    grad_mine = jnp.where(at.first, first_grad, second_grad)
    grad_far = at.opposite(second_grad, (1,)) + at.opposite(first_grad, (0,))
    input_grad = both_sequences(grad_mine, grad_far)

    def scatter(matrix):
        return lax.psum_scatter(matrix, DP, scatter_dimension=0, tiled=True)

    totals = []
    for one, two in zip(first_totals[0], second_totals[0]):
        one, two = scatter(one), scatter(two)
        far_part = at.across(two, (0,)) + at.across(one, (1,))
        mine = jnp.where(at.first, one, two).astype(F32) + far_part.astype(F32)
        totals.append(lax.all_gather(mine.astype(BF16), DP, axis=0, tiled=True).astype(F32))
    g_query, g_key_up, g_value_up, g_out = unpack_attention(totals[0], model)

    def latent_rows(mine, shard):
        wide = lax.dynamic_update_slice_in_dim(
            jnp.zeros((model, KVH * LH), BF16), mine, group_of(shard) * LH, 1
        )
        return lax.psum_scatter(wide, TEN, scatter_dimension=0, tiled=True)

    one = latent_rows(first_totals[1], jnp.where(at.first, at.z, opposite_z))
    two = latent_rows(second_totals[1], jnp.where(at.first, opposite_z, at.z))
    mine = jnp.where(at.first, one, two) + at.swap(jnp.where(at.first, two, one))
    g_latent = lax.psum(mine, DP).astype(F32)
    gains = lax.psum(jnp.stack(first_totals[2] + second_totals[2]), (SEC, DP, TEN)) / at.team
    gains = jnp.where(at.first, gains[:2], gains[2:])
    width = model // at.count
    gains = lax.dynamic_slice_in_dim(gains, at.z * width, width, 1)
    return (
        layer_out,
        input_grad,
        g_query[None],
        g_latent[None],
        g_key_up[None],
        g_value_up[None],
        g_out[None],
        totals[1][None],
        totals[2][None],
        totals[3][None],
        gains[0:1],
        gains[1:2],
    )


def solution(mesh):
    columns = P(SEC, None, TEN)
    rows = P(SEC, TEN, None)
    return jax.shard_map(
        local,
        mesh=mesh,
        in_specs=(
            P(DP, None),
            P(DP, None),
            columns,
            P(SEC, None, None),
            columns,
            columns,
            rows,
            columns,
            columns,
            rows,
            P(SEC, None),
            P(SEC, None),
        ),
        out_specs=(
            P(SEC, DP, None),
            P(SEC, DP, None),
            columns,
            rows,
            columns,
            columns,
            rows,
            columns,
            columns,
            rows,
            P(SEC, TEN),
            P(SEC, TEN),
        ),
        check_vma=False,
    )
```

profile of v0, /device:TPU:0, one launch (start us, length us, event | category | flops | bytes accessed | tf_op | source)
XLA Modules:
  0.0 843.3 jit_solution(4375599953197127407)
XLA Ops:
  15.8 14.5 %collective-permute-done.1 = bf16[640,256]{1,0:T(8,128)(2,1)S(1)} collective-permute-done((bf16[640,256]{1,0:T(8,128)(2,1)S(1)}, bf16[640,256]{1,0:T(8,128)(2,1)S(1)}, u32[]{:S(2)}, u32[]{:S(2)}) %collective-permute-start.1) | collective-permute-done | bytes 327712 | tf_op jit(solution)/shard_map/ppermute | solution.py:183
  32.2 18.5 %collective-permute-done.7 = bf16[256,704]{0,1:T(8,128)(2,1)S(1)} collective-permute-done((bf16[256,704]{0,1:T(8,128)(2,1)S(1)}, bf16[256,704]{0,1:T(8,128)(2,1)S(1)}, u32[]{:S(2)}, u32[]{:S(2)}) %collective-permute-start.7) | collective-permute-done | bytes 360480 | tf_op jit(solution)/shard_map/ppermute | solution.py:183
  60.0 18.8 %collective-permute-done.6 = bf16[256,704]{0,1:T(8,128)(2,1)S(1)} collective-permute-done((bf16[256,704]{0,1:T(8,128)(2,1)S(1)}, bf16[256,704]{0,1:T(8,128)(2,1)S(1)}, u32[]{:S(2)}, u32[]{:S(2)}) %collective-permute-start.6) | collective-permute-done | bytes 360480 | tf_op jit(solution)/shard_map/ppermute | solution.py:183
  119.6 10.7 %collective-permute-done.4 = bf16[256,1024]{1,0:T(8,128)(2,1)} collective-permute-done((bf16[256,1024]{1,0:T(8,128)(2,1)}, bf16[256,1024]{1,0:T(8,128)(2,1)}, u32[]{:S(2)}, u32[]{:S(2)}) %collective-permute-start.4) | collective-permute-done | bytes 524320 | tf_op jit(solution)/shard_map/ppermute | solution.py:190
  138.4 20.2 %all-gather.15.cloned.1.call-done = bf16[704,1024]{1,0:T(8,128)(2,1)} async-done(((bf16[176,1024]{1,0:T(8,128)(2,1)}), bf16[704,1024]{1,0:T(8,128)(2,1)}) %all-gather.15.cloned.1.call-update) | async-done | bytes 1441808 | tf_op jit(solution)/shard_map/all_gather | solution.py:359
  175.9 11.8 %collective-permute-done.16 = bf16[256,1024]{1,0:T(8,128)(2,1)S(1)} collective-permute-done((bf16[256,1024]{1,0:T(8,128)(2,1)S(1)}, bf16[256,1024]{1,0:T(8,128)(2,1)S(1)}, u32[]{:S(2)}, u32[]{:S(2)}) %collective-permute-start.16) | collective-permute-done | bytes 524320 | tf_op jit(solution)/shard_map/ppermute | solution.py:190
  188.0 10.1 %collective-permute-done.10 = bf16[256,1024]{1,0:T(8,128)(2,1)S(1)} collective-permute-done((bf16[256,1024]{1,0:T(8,128)(2,1)S(1)}, bf16[256,1024]{1,0:T(8,128)(2,1)S(1)}, u32[]{:S(2)}, u32[]{:S(2)}) %collective-permute-start.10) | collective-permute-done | bytes 524320 | tf_op jit(solution)/shard_map/ppermute | solution.py:190
  223.7 11.8 %collective-permute-done.19 = bf16[256,1024]{1,0:T(8,128)(2,1)S(1)} collective-permute-done((bf16[256,1024]{1,0:T(8,128)(2,1)S(1)}, bf16[256,1024]{1,0:T(8,128)(2,1)S(1)}, u32[]{:S(2)}, u32[]{:S(2)}) %collective-permute-start.19) | collective-permute-done | bytes 524320 | tf_op jit(solution)/shard_map/ppermute | solution.py:190
  235.8 10.1 %collective-permute-done.25 = bf16[256,1024]{1,0:T(8,128)(2,1)S(1)} collective-permute-done((bf16[256,1024]{1,0:T(8,128)(2,1)S(1)}, bf16[256,1024]{1,0:T(8,128)(2,1)S(1)}, u32[]{:S(2)}, u32[]{:S(2)}) %collective-permute-start.25) | collective-permute-done | bytes 524320 | tf_op jit(solution)/shard_map/ppermute | solution.py:190
  268.9 10.8 %collective-permute-done.32 = bf16[256,1024]{1,0:T(8,128)(2,1)S(1)} collective-permute-done((bf16[256,1024]{1,0:T(8,128)(2,1)S(1)}, bf16[256,1024]{1,0:T(8,128)(2,1)S(1)}, u32[]{:S(2)}, u32[]{:S(2)}) %collective-permute-start.32) | collective-permute-done | bytes 524320 | tf_op jit(solution)/shard_map/ppermute | solution.py:190
  279.7 11.2 %collective-permute-done.35 = bf16[256,1024]{1,0:T(8,128)(2,1)S(1)} collective-permute-done((bf16[256,1024]{1,0:T(8,128)(2,1)S(1)}, bf16[256,1024]{1,0:T(8,128)(2,1)S(1)}, u32[]{:S(2)}, u32[]{:S(2)}) %collective-permute-start.35) | collective-permute-done | bytes 524320 | tf_op jit(solution)/shard_map/ppermute | solution.py:190
  291.7 9.9 %collective-permute-done.28 = bf16[256,1024]{1,0:T(8,128)(2,1)S(1)} collective-permute-done((bf16[256,1024]{1,0:T(8,128)(2,1)S(1)}, bf16[256,1024]{1,0:T(8,128)(2,1)S(1)}, u32[]{:S(2)}, u32[]{:S(2)}) %collective-permute-start.28) | collective-permute-done | bytes 524320 | tf_op jit(solution)/shard_map/ppermute | solution.py:190
  307.9 9.1 %shard_map.213 = (bf16[1024,256]{1,0:T(8,128)(2,1)S(1)}, bf16[1024,256]{1,0:T(8,128)(2,1)S(1)}, bf16[1024,256]{1,0:T(8,128)(2,1)S(1)}) custom-call(bf16[1024,256]{1,0:T(8,128)(2,1)S(1)} %convolution_convert_fusion.18.q_ref, bf16[1024,256]{1,0:T(8,128)(2,1)S(1)} %convolution_convert_fusion.6.k_ref, bf16[1024,256]{1,0:T(8,128)(2,1)S(1)} %convolution_convert_fusion.5.v_ref, ...), custom_call_target="tpu_custom_call" | custom-call | flops 5368709120 | bytes 4194304 | tf_op jit(solution)/shard_map/pallas_call | solution.py:136
  345.5 11.2 %collective-permute-done.41 = bf16[256,1024]{1,0:T(8,128)(2,1)S(1)} collective-permute-done((bf16[256,1024]{1,0:T(8,128)(2,1)S(1)}, bf16[256,1024]{1,0:T(8,128)(2,1)S(1)}, u32[]{:S(2)}, u32[]{:S(2)}) %collective-permute-start.41) | collective-permute-done | bytes 524320 | tf_op jit(solution)/shard_map/ppermute | solution.py:190
  402.4 12.4 %collective-permute-done.44 = bf16[256,1024]{1,0:T(8,128)(2,1)S(1)} collective-permute-done((bf16[256,1024]{1,0:T(8,128)(2,1)S(1)}, bf16[256,1024]{1,0:T(8,128)(2,1)S(1)}, u32[]{:S(2)}, u32[]{:S(2)}) %collective-permute-start.44) | collective-permute-done | bytes 524320 | tf_op jit(solution)/shard_map/ppermute | solution.py:190
  415.3 10.4 %collective-permute-done.47 = bf16[256,1024]{1,0:T(8,128)(2,1)S(1)} collective-permute-done((bf16[256,1024]{1,0:T(8,128)(2,1)S(1)}, bf16[256,1024]{1,0:T(8,128)(2,1)S(1)}, u32[]{:S(2)}, u32[]{:S(2)}) %collective-permute-start.47) | collective-permute-done | bytes 524320 | tf_op jit(solution)/shard_map/ppermute | solution.py:190
  504.5 11.3 %collective-permute-done.61 = bf16[256,704]{0,1:T(8,128)(2,1)} collective-permute-done((bf16[256,704]{0,1:T(8,128)(2,1)}, bf16[256,704]{0,1:T(8,128)(2,1)}, u32[]{:S(2)}, u32[]{:S(2)}) %collective-permute-start.61) | collective-permute-done | bytes 360480 | tf_op jit(solution)/shard_map/ppermute | solution.py:183
  539.9 14.5 %collective-permute-done.50 = bf16[256,1024]{1,0:T(8,128)(2,1)} collective-permute-done((bf16[256,1024]{1,0:T(8,128)(2,1)S(1)}, bf16[256,1024]{1,0:T(8,128)(2,1)}, u32[]{:S(2)}, u32[]{:S(2)}) %collective-permute-start.50) | collective-permute-done | bytes 524320 | tf_op jit(solution)/shard_map/ppermute | solution.py:190
  554.5 10.4 %collective-permute-done.53 = bf16[256,1024]{1,0:T(8,128)(2,1)} collective-permute-done((bf16[256,1024]{1,0:T(8,128)(2,1)S(1)}, bf16[256,1024]{1,0:T(8,128)(2,1)}, u32[]{:S(2)}, u32[]{:S(2)}) %collective-permute-start.53) | collective-permute-done | bytes 524320 | tf_op jit(solution)/shard_map/ppermute | solution.py:190
  577.4 17.0 %reduce-scatter.27.cloned.1.call-done = bf16[176,1024]{1,0:T(8,128)(2,1)} async-done(((bf16[704,1024]{1,0:T(8,128)(2,1)}), bf16[176,1024]{1,0:T(8,128)(2,1)}) %reduce-scatter.27.cloned.1.call-update) | async-done | bytes 360464 | tf_op jit(solution)/shard_map/reduce_scatter | solution.py:394
  600.0 91.5 %collective-permute-done.65 = bf16[176,1024]{1,0:T(8,128)(2,1)S(1)} collective-permute-done((bf16[176,1024]{1,0:T(8,128)(2,1)}, bf16[176,1024]{1,0:T(8,128)(2,1)S(1)}, u32[]{:S(2)}, u32[]{:S(2)}) %collective-permute-start.65) | collective-permute-done | bytes 360480 | tf_op jit(solution)/shard_map/ppermute | solution.py:183
  705.4 69.1 %psum.15 = f32[4,1024]{1,0:T(4,128)S(1)} all-reduce(f32[4,1024]{1,0:T(4,128)S(1)} %pad_maximum_fusion.30), channel_id=1, replica_groups=mesh['section'=2,'dp'=4,'tensor'=4] {'section','dp','tensor'}, use_global_device_ids=true, to_apply=%region_37.38 | all-reduce | flops 4096 | bytes 32768 | tf_op jit(solution)/shard_map/psum | solution.py:414
  778.3 8.9 %collective-permute-done.58 = bf16[640,256]{1,0:T(8,128)(2,1)} collective-permute-done((bf16[640,256]{1,0:T(8,128)(2,1)}, bf16[640,256]{1,0:T(8,128)(2,1)}, u32[]{:S(2)}, u32[]{:S(2)}) %collective-permute-start.58) | collective-permute-done | bytes 327712 | tf_op jit(solution)/shard_map/ppermute | solution.py:183
  808.5 23.2 %all-gather.17.cloned.1.call-done = bf16[2560,256]{1,0:T(8,128)(2,1)} async-done(((bf16[640,256]{1,0:T(8,128)(2,1)}), bf16[2560,256]{1,0:T(8,128)(2,1)}) %all-gather.17.cloned.1.call-update) | async-done | bytes 1310736 | tf_op jit(solution)/shard_map/all_gather | solution.py:401
  (705 shorter events, 378.7 us)
Async XLA Ops:
  7.2 76.7 %all-gather.9.cloned.1.call-start = ((), (), s32[]{:S(2)}) async-start(), calls=%async_computation.10 | async-start | bytes 1638400 | tf_op jit(solution)/shard_map/all_gather | solution.py:359
  31.0 77.5 %all-gather.13.cloned.1.call-start = ((), (), s32[]{:S(2)}) async-start(), calls=%async_computation.12 | async-start | bytes 1802240 | tf_op jit(solution)/shard_map/all_gather | solution.py:359
  51.4 83.2 %all-gather.11.cloned.1.call-start = ((), (), s32[]{:S(2)}) async-start(), calls=%async_computation.11 | async-start | bytes 1802240 | tf_op jit(solution)/shard_map/all_gather | solution.py:359
  79.6 78.9 %all-gather.15.cloned.1.call-start = ((), (), s32[]{:S(2)}) async-start(), calls=%async_computation.13 | async-start | bytes 1802240 | tf_op jit(solution)/shard_map/all_gather | solution.py:359
  101.8 387.0 %reduce-scatter.21.cloned.1.call-start = ((), (), s32[]{:S(2)}) async-start(), calls=%async_computation.21 | async-start | bytes 1802240 | tf_op jit(solution)/shard_map/reduce_scatter | solution.py:394
  328.5 165.4 %reduce-scatter.25.cloned.1.call-start = ((), (), s32[]{:S(2)}) async-start(), calls=%async_computation.24 | async-start | bytes 1802240 | tf_op jit(solution)/shard_map/reduce_scatter | solution.py:394
  372.7 124.8 %reduce-scatter.19.cloned.1.call-start = ((), (), s32[]{:S(2)}) async-start(), calls=%async_computation.20 | async-start | bytes 1802240 | tf_op jit(solution)/shard_map/reduce_scatter | solution.py:394
  394.7 104.1 %reduce-scatter.17.cloned.1.call-start = ((), (), s32[]{:S(2)}) async-start(), calls=%async_computation.18 | async-start | bytes 1310720 | tf_op jit(solution)/shard_map/reduce_scatter | solution.py:408
  433.4 65.5 %reduce-scatter.15.cloned.1.call-start = ((), (), s32[]{:S(2)}) async-start(), calls=%async_computation.17 | async-start | bytes 1310720 | tf_op jit(solution)/shard_map/reduce_scatter | solution.py:408
  452.9 74.6 %reduce-scatter.23.cloned.1.call-start = ((), (), s32[]{:S(2)}) async-start(), calls=%async_computation.23 | async-start | bytes 1802240 | tf_op jit(solution)/shard_map/reduce_scatter | solution.py:394
  457.9 113.8 %reduce-scatter.29.cloned.1.call-start = ((), (), s32[]{:S(2)}) async-start(), calls=%async_computation.27 | async-start | bytes 1802240 | tf_op jit(solution)/shard_map/reduce_scatter | solution.py:394
  462.8 131.6 %reduce-scatter.27.cloned.1.call-start = ((), (), s32[]{:S(2)}) async-start(), calls=%async_computation.26 | async-start | bytes 1802240 | tf_op jit(solution)/shard_map/reduce_scatter | solution.py:394
  467.7 230.5 %reduce-scatter.13.cloned.1.call-start = ((), (), s32[]{:S(2)}) async-start(), calls=%async_computation.15 | async-start | bytes 1638400 | tf_op jit(solution)/shard_map/reduce_scatter | solution.py:394
  476.5 298.1 %reduce-scatter.11.cloned.1.call-start = ((), (), s32[]{:S(2)}) async-start(), calls=%async_computation.14 | async-start | bytes 1638400 | tf_op jit(solution)/shard_map/reduce_scatter | solution.py:394
  485.5 290.9 %all-reduce.2.cloned.1.call-start = ((), (), s32[]{:S(2)}) async-start(), calls=%async_computation.19 | async-start | bytes 524288 | tf_op jit(solution)/shard_map/psum | solution.py:413
  504.5 294.1 %all-gather.19.cloned.1.call-start = ((), (), s32[]{:S(2)}) async-start(), calls=%async_computation.22 | async-start | bytes 1802240 | tf_op jit(solution)/shard_map/all_gather | solution.py:401
  518.0 283.9 %all-gather.21.cloned.1.call-start = ((), (), s32[]{:S(2)}) async-start(), calls=%async_computation.25 | async-start | bytes 1802240 | tf_op jit(solution)/shard_map/all_gather | solution.py:401
  532.2 168.2 %collective-permute-start.30 = (bf16[1024,1024]{1,0:T(8,128)(2,1)}, bf16[1024,1024]{1,0:T(8,128)(2,1)}, u32[]{:S(2)}, u32[]{:S(2)}) collective-permute-start(bf16[1024,1024]{1,0:T(8,128)(2,1)} %maximum_select_fusion), channel_id=1, source_target_pairs={{0,2},{1,3},{2,0},{3,1},{16,18},{17,19},{18,16},{19,17},{4,6},{5,7... | collective-permute-start | bytes 6291464 | tf_op jit(solution)/shard_map/ppermute | solution.py:178
  539.9 265.3 %all-gather.23.cloned.1.call-start = ((), (), s32[]{:S(2)}) async-start(), calls=%async_computation.28 | async-start | bytes 1802240 | tf_op jit(solution)/shard_map/all_gather | solution.py:401
  575.3 214.0 %collective-permute-start.55 = (bf16[1024,1024]{1,0:T(8,128)(2,1)}, bf16[1024,1024]{1,0:T(8,128)(2,1)}, u32[]{:S(2)}, u32[]{:S(2)}) collective-permute-start(bf16[1024,1024]{1,0:T(8,128)(2,1)} %pad_maximum_fusion.4), channel_id=1, source_target_pairs={{16,18},{17,19},{18,16},{19,17},{20,22},{21,23},{22,20},{23,21},{2... | collective-permute-start | bytes 6291464 | tf_op jit(solution)/shard_map/ppermute | solution.py:178
  595.2 96.3 %collective-permute-start.65 = (bf16[176,1024]{1,0:T(8,128)(2,1)}, bf16[176,1024]{1,0:T(8,128)(2,1)S(1)}, u32[]{:S(2)}, u32[]{:S(2)}) collective-permute-start(bf16[176,1024]{1,0:T(8,128)(2,1)} %reduce-scatter.27.cloned.1.call-done), channel_id=1, source_target_pairs={{16,2},{17,3},{18,0},{19,1},{20,6},{21,7},{22,4},{23,5},{24,10},{2... | collective-permute-start | bytes 1081352 | tf_op jit(solution)/shard_map/ppermute | solution.py:183
  693.5 138.2 %all-gather.17.cloned.1.call-start = ((), (), s32[]{:S(2)}) async-start(), calls=%async_computation.16 | async-start | bytes 1638400 | tf_op jit(solution)/shard_map/all_gather | solution.py:401
  696.3 93.0 %collective-permute-start.56 = (bf16[1024,1024]{1,0:T(8,128)(2,1)}, bf16[1024,1024]{1,0:T(8,128)(2,1)}, u32[]{:S(2)}, u32[]{:S(2)}) collective-permute-start(bf16[1024,1024]{1,0:T(8,128)(2,1)} %pad_maximum_fusion.6), channel_id=1, source_target_pairs={{0,2},{1,3},{2,0},{3,1},{4,6},{5,7},{6,4},{7,5},{8,10},{9,11},{10,... | collective-permute-start | bytes 6291464 | tf_op jit(solution)/shard_map/ppermute | solution.py:178
  698.3 80.0 %collective-permute-start.57 = (bf16[640,256]{1,0:T(8,128)(2,1)}, bf16[640,256]{1,0:T(8,128)(2,1)}, u32[]{:S(2)}, u32[]{:S(2)}) collective-permute-start(bf16[640,256]{1,0:T(8,128)(2,1)} %reduce-scatter.13.cloned.1.call-done), channel_id=1, source_target_pairs={{0,18},{1,19},{2,16},{3,17},{4,22},{5,23},{6,20},{7,21},{8,26},{9,... | collective-permute-start | bytes 983048 | tf_op jit(solution)/shard_map/ppermute | solution.py:183
  (222 other events, 3193.3 us)
Sparse Core Ops, SparseCore 0:
  31.1 31.3 all-gather.8
  65.0 29.7 all-gather.12
  97.1 29.7 all-gather.10
  128.6 29.8 all-gather.14
  328.6 30.0 reduce-scatter.20
  372.9 30.2 reduce-scatter.24
  406.6 30.0 reduce-scatter.18
  439.8 27.1 reduce-scatter.16
  469.2 25.7 reduce-scatter.14
  498.7 28.7 reduce-scatter.22
  531.0 30.0 reduce-scatter.28
  564.2 30.1 reduce-scatter.26
  597.3 29.3 reduce-scatter.12
  630.0 29.3 reduce-scatter.10
  662.7 42.9 all-reduce.1
  707.5 29.9 all-gather.18
  739.3 29.7 all-gather.20
  770.9 29.9 all-gather.22
  802.9 28.7 all-gather.16
where the time goes:
time: 852 us; the launch traced here: 843 us
  waiting for transfers between devices  403 us (47%)
  other arithmetic  118 us (14%)
  matrix products  101 us (12%)
  blocking collectives  69.1 us (8%)
  starting transfers between devices  59.9 us (7%)
  local copies, waits for them, and re-layouts  42.4 us (5%)
  Pallas kernels  32.9 us (4%)
  between operations  17.3 us (2%)
    ppermute x16, waiting for transfers between devices, team_sum(): parts.append(lax.ppermute(block, TEN, route))  168 us
    ppermute x12, waiting for transfers between devices, across(): return lax.ppermute(block, (SEC, TEN), route)  167 us
    dot_general x64, matrix products, mm(): return lax.dot_general(left, right, dims, preferred_element_type=F32)  101 us
    psum x1, blocking collectives, local(): lax.psum(jnp.stack(first_totals[2] + second_totals[2]), (SEC, DP, TEN))  69.1 us
    unnamed x334, local copies, waits for them, and re-layouts  24.6 us
    all_gather x4, waiting for transfers between devices, local(): lax.all_gather(mine.astype(BF16), DP, axis=0, tiled=True).astype(F32)  23.2 us
    ppermute x12, starting transfers between devices, across(): return lax.ppermute(block, (SEC, TEN), route)  23 us
    all_gather x4, waiting for transfers between devices, fetch(): return lax.all_gather(at.across(piece), DP, axis=0, tiled=True)  20.2 us
  transfers between devices with their start and end apart: 85, of which 32 were waited for; matrix products, arithmetic and copies ran while one was open for 26% of the time, Pallas kernels for 3%

commit v1 on v0

--- a/solution.py
+++ b/solution.py
@@ -151,14 +151,6 @@
     return features * lax.rsqrt(jnp.mean(features * features, axis=-1, keepdims=True) + EPS)
 
 
-def norm_backward(source, gain, upstream):
-    inverse = lax.rsqrt(jnp.mean(source * source, axis=-1, keepdims=True) + EPS)
-    normed = source * inverse
-    scaled = upstream * gain
-    grad_source = inverse * (scaled - normed * jnp.mean(scaled * normed, axis=-1, keepdims=True))
-    return grad_source, jnp.sum(upstream * normed, axis=0)
-
-
 class Place:
     def __init__(self):
         self.count = lax.axis_size(TEN)
@@ -182,36 +174,6 @@
         route = [(c * n + z, (1 - c) * n + (z + t) % n) for c in cores for z in range(n)]
         return lax.ppermute(block, (SEC, TEN), route)
 
-    def team_sum(self, block):
-        n, t = self.count, self.team
-        parts = [block]
-        for step in range(1, t):
-            route = [(z, z // t * t + (z - step) % t) for z in range(n)]
-            parts.append(lax.ppermute(block, TEN, route))
-        if t == 2:
-            return parts[0].astype(F32) + parts[1].astype(F32)
-        stacked = jnp.roll(jnp.stack(parts), self.z % t, axis=0)
-        return jnp.sum(stacked.astype(F32), axis=0)
-
-    def own_half(self, block):
-        half = block.shape[0] // 2
-        return lax.dynamic_slice_in_dim(block, self.core * half, half, 0)
-
-    def other_half(self, block):
-        half = block.shape[0] // 2
-        return lax.dynamic_slice_in_dim(block, (1 - self.core) * half, half, 0)
-
-    def reduce(self, partial):
-        got = self.swap(self.other_half(partial.astype(BF16)))
-        mine = self.own_half(partial) + got.astype(F32)
-        return self.team_sum(mine.astype(BF16))
-
-    def join(self, own):
-        other = self.swap(own)
-        return jnp.concatenate(
-            [jnp.where(self.first, own, other), jnp.where(self.first, other, own)], axis=0
-        )
-
 
 def pack_columns(matrix, width):
     return [matrix[:, i : i + width] for i in range(0, matrix.shape[1], width)]
@@ -232,98 +194,369 @@
     return query, key_up, value_up, out
 
 
-CHUNKS = 2
-
-
-def chunk(block, index):
-    rows = block.shape[0] // CHUNKS
-    return block[index * rows : (index + 1) * rows]
-
-
-def layer_forward(at, source, weights):
+MESH = pl.DeviceIdType.MESH
+PIECES = 4
+VMEM_LIMIT = 56 * 2**20
+
+
+def reciprocal_rms(features):
+    return lax.rsqrt(jnp.mean(features * features, axis=-1, keepdims=True) + EPS)
+
+
+class Team:
+    def __init__(self):
+        count = lax.axis_size(TEN)
+        self.size = count // 2
+        self.core = lax.axis_index(SEC)
+        z = lax.axis_index(TEN)
+        self.place = lax.rem(z, self.size)
+        self.base = z - self.place
+        self.other = {SEC: 1 - self.core}
+
+    def peer(self, step):
+        place = lax.rem(self.place + step, self.size)
+        return place, {TEN: self.base + place}
+
+    def greet(self):
+        barrier = pltpu.get_barrier_semaphore()
+        pl.semaphore_signal(barrier, inc=1, device_id=self.other, device_id_type=MESH)
+        for step in range(1, self.size):
+            pl.semaphore_signal(barrier, inc=1, device_id=self.peer(step)[1], device_id_type=MESH)
+        pl.semaphore_wait(barrier, self.size)
+
+
+def exchange_scratch(team, rows, model):
+    half = rows // PIECES // 2
+    return [
+        pltpu.VMEM((2, half, model), F32),
+        pltpu.VMEM((PIECES, half, model), F32),
+        pltpu.VMEM((PIECES, half, model), BF16),
+        pltpu.VMEM((PIECES, half, model), BF16),
+        pltpu.VMEM((team, PIECES, half, model), BF16),
+        pltpu.SemaphoreType.DMA((PIECES,)),
+        pltpu.SemaphoreType.DMA((PIECES,)),
+        pltpu.SemaphoreType.DMA((team, PIECES)),
+        pltpu.SemaphoreType.DMA((team, PIECES)),
+        pltpu.SemaphoreType.DMA((PIECES,)),
+        pltpu.SemaphoreType.DMA((PIECES,)),
+    ]
+
+
+class Exchange:
+    def __init__(self, team, refs):
+        self.team = team
+        (self.part, self.keep, self.out, self.got, self.far) = refs[:5]
+        (self.core_sent, self.core_here, self.far_sent, self.far_here) = refs[5:9]
+        (self.join_sent, self.join_here) = refs[9:]
+
+    def core_copy(self, i):
+        return pltpu.make_async_remote_copy(
+            src_ref=self.out.at[i],
+            dst_ref=self.got.at[i],
+            send_sem=self.core_sent.at[i],
+            recv_sem=self.core_here.at[i],
+            device_id=self.team.other,
+            device_id_type=MESH,
+        )
+
+    def far_copy(self, i, step, place):
+        return pltpu.make_async_remote_copy(
+            src_ref=self.far.at[place, i],
+            dst_ref=self.far.at[place, i],
+            send_sem=self.far_sent.at[step, i],
+            recv_sem=self.far_here.at[place, i],
+            device_id=self.team.peer(step)[1],
+            device_id_type=MESH,
+        )
+
+    def join_copy(self, i, whole):
+        core = self.team.core
+        return pltpu.make_async_remote_copy(
+            src_ref=whole.at[i, core],
+            dst_ref=whole.at[i, core],
+            send_sem=self.join_sent.at[i],
+            recv_sem=self.join_here.at[i],
+            device_id=self.team.other,
+            device_id_type=MESH,
+        )
+
+    def push(self, i, product):
+        core = self.team.core
+        self.part[...] = product.reshape(self.part.shape)
+        self.out[i] = self.part[1 - core].astype(BF16)
+        self.core_copy(i).start()
+        self.keep[i] = self.part[core]
+
+    def combine(self, i):
+        self.core_copy(i).wait_recv()
+        self.far[self.team.place, i] = (self.keep[i] + self.got[i].astype(F32)).astype(BF16)
+        for step in range(1, self.team.size):
+            self.far_copy(i, step, self.team.place).start()
+
+    def total(self, i):
+        for step in range(1, self.team.size):
+            self.far_copy(i, step, self.team.peer(step)[0]).wait_recv()
+        total = self.far[0, i].astype(F32)
+        for place in range(1, self.team.size):
+            total = total + self.far[place, i].astype(F32)
+        return total
+
+    def join(self, i, whole, half):
+        whole[i, self.team.core] = half
+        self.join_copy(i, whole).start()
+
+    def finish(self, whole, joined=False):
+        def drain(i, _):
+            self.core_copy(i).wait_send()
+            for step in range(1, self.team.size):
+                self.far_copy(i, step, self.team.place).wait_send()
+            self.join_copy(i, whole).wait_send()
+            if not joined:
+                self.join_copy(i, whole).wait_recv()
+            return 0
+
+        lax.fori_loop(0, PIECES, drain, 0)
+
+
+def each_piece(body):
+    lax.fori_loop(0, PIECES, lambda i, _: (body(i), 0)[1], 0)
+
+
+def piece_rows(i, rows):
+    size = rows // PIECES
+    return pl.ds(pl.multiple_of(i * size, size), size)
+
+
+def project_out_kernel(heads, w_out, source, gain, residual, mlp_in, *refs):
+    team = Team()
+    ex = Exchange(team, refs)
+    team.greet()
+    rows = heads.shape[0]
+
+    def send(i):
+        ex.push(i, mm(heads[piece_rows(i, rows), :], w_out[...]))
+
+        @pl.when(i > 0)
+        def _():
+            ex.combine(i - 1)
+
+    each_piece(send)
+    ex.combine(PIECES - 1)
+
+    def receive(i):
+        block = source[i, team.core].astype(F32) + ex.total(i)
+        residual[i] = block
+        ex.join(i, mlp_in, (block * reciprocal_rms(block) * gain[...]).astype(BF16))
+
+    each_piece(receive)
+    ex.finish(mlp_in)
+
+
+def feed_forward_kernel(mlp_in, w_gate, w_up, w_down, residual, gate, up, hidden, output, *refs):
+    team = Team()
+    ex = Exchange(team, refs)
+    team.greet()
+    rows = mlp_in.shape[0]
+
+    def send(i):
+        at = piece_rows(i, rows)
+        block = mlp_in[at, :]
+        gate_block = mm(block, w_gate[...])
+        up_block = mm(block, w_up[...])
+        hidden_block = (jax.nn.silu(gate_block) * up_block).astype(BF16)
+        gate[at, :] = gate_block
+        up[at, :] = up_block
+        hidden[at, :] = hidden_block
+        ex.push(i, mm(hidden_block, w_down[...]))
+
+        @pl.when(i > 0)
+        def _():
+            ex.combine(i - 1)
+
+    each_piece(send)
+    ex.combine(PIECES - 1)
+    each_piece(lambda i: ex.join(i, output, (residual[i] + ex.total(i)).astype(BF16)))
+    ex.finish(output)
+
+
+def rms_back(block, gain, upstream):
+    inverse = reciprocal_rms(block)
+    normed = block * inverse
+    scaled = upstream * gain
+    grad = inverse * (scaled - normed * jnp.mean(scaled * normed, axis=-1, keepdims=True))
+    return grad, jnp.sum(upstream * normed, axis=0, keepdims=True)
+
+
+def feed_back_kernel(
+    upstream, w_gate, w_up, w_down, gate, up, hidden, mlp_in, residual, gain,
+    d_residual, res_grad, gain_grad, grads, d_gate, d_up, *refs
+):
+    team = Team()
+    ex = Exchange(team, refs)
+    team.greet()
+    rows = mlp_in.shape[0]
+    model = mlp_in.shape[1]
+    shape = (rows // PIECES, model)
+
+    def send(i):
+        at = piece_rows(i, rows)
+        grad_hidden = mm(upstream[i].reshape(shape), w_down[...], 1, 1)
+        gate_block = gate[at, :]
+        sigmoid = jax.nn.sigmoid(gate_block)
+        silu = gate_block * sigmoid
+        d_gate_block = grad_hidden * up[at, :] * (sigmoid + silu * (1.0 - sigmoid))
+        d_gate[at, :] = d_gate_block.astype(BF16)
+        d_up[at, :] = (grad_hidden * silu).astype(BF16)
+        ex.push(i, mm(d_gate[at, :], w_gate[...], 1, 1) + mm(d_up[at, :], w_up[...], 1, 1))
+
+        @pl.when(i > 0)
+        def _():
+            ex.combine(i - 1)
+
+    each_piece(send)
+    ex.combine(PIECES - 1)
+    grads[0:model, :] = mm(mlp_in[...], d_gate[...], 0, 0).astype(BF16)
+    grads[model : 2 * model, :] = mm(mlp_in[...], d_up[...], 0, 0).astype(BF16)
+    whole = upstream[...].reshape(rows, model)
+    grads[2 * model :, :] = mm(whole, hidden[...], 0, 0).astype(BF16)
+    gain_grad[...] = jnp.zeros_like(gain_grad)
+
+    def receive(i):
+        part, gain_part = rms_back(residual[i], gain[...], ex.total(i))
+        block = upstream[i, team.core].astype(F32) + part
+        d_residual[i] = block
+        gain_grad[...] += gain_part
+        ex.join(i, res_grad, block.astype(BF16))
+
+    each_piece(receive)
+    ex.finish(res_grad)
+
+
+def attend_in_back_kernel(
+    d_queries, d_latents, w_query, w_latent, source, d_residual, gain, attn_in,
+    heads_out, res_grad, latents, d_keys, d_values,
+    input_grad, gain_grad, grads, g_latent, *refs
+):
+    team = Team()
+    ex = Exchange(team, refs)
+    team.greet()
+    rows = d_queries.shape[0]
+
+    def send(i):
+        at = piece_rows(i, rows)
+        ex.push(i, mm(d_queries[at, :], w_query[...], 1, 1) + mm(d_latents[at, :], w_latent[...], 1, 1))
+
+        @pl.when(i > 0)
+        def _():
+            ex.combine(i - 1)
+
+    each_piece(send)
+    ex.combine(PIECES - 1)
+    model, width = w_query.shape
+    grads[0:model, :] = mm(attn_in[...], d_queries[...], 0, 0).astype(BF16)
+    g_latent[...] = mm(attn_in[...], d_latents[...], 0, 0).astype(BF16)
+    grads[model : model + LH, :] = mm(latents[...], d_keys[...], 0, 0).astype(BF16)
+    grads[model + LH : model + 2 * LH, :] = mm(latents[...], d_values[...], 0, 0).astype(BF16)
+    g_out = mm(heads_out[...], res_grad[...], 0, 0).astype(BF16)
+    for j, block in enumerate(pack_columns(g_out, width)):
+        start = model + 2 * LH + j * width
+        grads[start : start + width, :] = block
+    gain_grad[...] = jnp.zeros_like(gain_grad)
+
+    def receive(i):
+        part, gain_part = rms_back(source[i, team.core].astype(F32), gain[...], ex.total(i))
+        gain_grad[...] += gain_part
+        ex.join(i, input_grad, (d_residual[i] + part).astype(BF16))
+
+    each_piece(receive)
+    ex.finish(input_grad)
+
+
+def team_call(kernel, number, model, outs, operands, scratch=(), flops=0):
+    team = lax.axis_size(TEN) // 2
+    vmem = pl.BlockSpec(memory_space=pltpu.VMEM)
+    return pl.pallas_call(
+        kernel,
+        in_specs=[vmem] * len(operands),
+        out_specs=[vmem] * len(outs),
+        out_shape=[jax.ShapeDtypeStruct(*out) for out in outs],
+        scratch_shapes=list(scratch) + exchange_scratch(team, LEN, model),
+        compiler_params=pltpu.CompilerParams(
+            collective_id=number, has_side_effects=True, vmem_limit_bytes=VMEM_LIMIT
+        ),
+        cost_estimate=pl.CostEstimate(flops=flops, bytes_accessed=2**22, transcendentals=0),
+    )(*operands)
+
+
+def pieces_of(block):
+    return block.reshape(PIECES, 2, block.shape[0] // PIECES // 2, block.shape[1])
+
+
+def layer_forward(source, weights):
     w_query, w_key_up, w_value_up, w_out, w_gate, w_up, w_down, w_latent, gain_attn, gain_mlp = weights
+    rows, model = source.shape
+    hidden_width = w_gate.shape[1]
     attn_in = (rms_scale(source.astype(F32)) * gain_attn).astype(BF16)
     queries = mm(attn_in, w_query).astype(BF16)
     latents = mm(attn_in, w_latent).astype(BF16)
     keys = mm(latents, w_key_up).astype(BF16)
     values = mm(latents, w_value_up).astype(BF16)
     heads_out, norms = attend_forward(queries, keys, values)
-    residuals, mlp_ins, gates, ups, hiddens, outputs = [], [], [], [], [], []
-    for i in range(CHUNKS):
-        attended = at.reduce(mm(chunk(heads_out, i), w_out))
-        residual = at.own_half(chunk(source, i)).astype(F32) + attended
-        residuals.append(residual)
-        mlp_ins.append(at.join((rms_scale(residual) * gain_mlp).astype(BF16)))
-    for i in range(CHUNKS):
-        gate = mm(mlp_ins[i], w_gate)
-        up = mm(mlp_ins[i], w_up)
-        hidden = (jax.nn.silu(gate) * up).astype(BF16)
-        output = residuals[i] + at.reduce(mm(hidden, w_down))
-        outputs.append(at.join(output.astype(BF16)))
-        gates.append(gate)
-        ups.append(up)
-        hiddens.append(hidden)
-    whole = functools.partial(jnp.concatenate, axis=0)
-    kept = (
-        source,
-        attn_in,
-        queries,
-        latents,
-        keys,
-        values,
-        heads_out,
-        norms,
-        residuals,
-        whole(mlp_ins),
-        whole(gates),
-        whole(ups),
-        whole(hiddens),
-    )
-    return whole(outputs), kept
-
-
-def layer_backward(at, kept, upstream, weights):
+    split = (PIECES, 2, rows // PIECES // 2, model)
+    own = (PIECES, rows // PIECES // 2, model)
+    residual, mlp_in = team_call(
+        project_out_kernel, 0, model, [(own, F32), (split, BF16)],
+        (heads_out, w_out, pieces_of(source), gain_mlp[None]),
+        flops=LINK_FLOPS,
+    )
+    mlp_in = mlp_in.reshape(rows, model)
+    wide = (rows, hidden_width)
+    gate, up, hidden, output = team_call(
+        feed_forward_kernel, 1, model, [(wide, F32), (wide, F32), (wide, BF16), (split, BF16)],
+        (mlp_in, w_gate, w_up, w_down, residual),
+        flops=LINK_FLOPS,
+    )
+    kept = (source, attn_in, queries, latents, keys, values, heads_out, norms)
+    return output.reshape(rows, model), kept + (residual, mlp_in, gate, up, hidden)
+
+
+LINK_FLOPS = 30 * 10**9
+
+
+def feed_back(kept, upstream, weights):
     w_query, w_key_up, w_value_up, w_out, w_gate, w_up, w_down, w_latent, gain_attn, gain_mlp = weights
-    source, attn_in, queries, latents, keys, values, heads_out, norms, residuals, mlp_in, gate, up, hidden = kept
-    grad_hidden = mm(upstream, w_down, 1, 1)
-    sigmoid = jax.nn.sigmoid(gate)
-    d_gate = (grad_hidden * up * sigmoid * (1.0 + gate * (1.0 - sigmoid))).astype(BF16)
-    d_up = (grad_hidden * gate * sigmoid).astype(BF16)
-    d_residuals, gain_mlp_grad = [], 0.0
-    joined = []
-    for i in range(CHUNKS):
-        term = mm(chunk(d_gate, i), w_gate, 1, 1) + mm(chunk(d_up, i), w_up, 1, 1)
-        part, gain_part = norm_backward(residuals[i], gain_mlp, at.reduce(term))
-        d_residual = at.own_half(chunk(upstream, i)).astype(F32) + part
-        d_residuals.append(d_residual)
-        gain_mlp_grad = gain_mlp_grad + gain_part
-        joined.append(at.join(d_residual.astype(BF16)))
-    g_down = mm(hidden, upstream, 0, 0).astype(BF16)
-    g_gate = mm(mlp_in, d_gate, 0, 0).astype(BF16)
-    g_up = mm(mlp_in, d_up, 0, 0).astype(BF16)
-    res_grad = jnp.concatenate(joined, axis=0)
+    residual, mlp_in, gate, up, hidden = kept[8:]
+    rows, model = upstream.shape
+    split = (PIECES, 2, rows // PIECES // 2, model)
+    own = (PIECES, rows // PIECES // 2, model)
+    width = w_gate.shape[1]
+    return team_call(
+        feed_back_kernel, 2, model,
+        [(own, F32), (split, BF16), ((1, model), F32), ((3 * model, width), BF16)],
+        (pieces_of(upstream), w_gate, w_up, w_down, gate, up, hidden, mlp_in, residual, gain_mlp[None]),
+        scratch=[pltpu.VMEM((rows, width), BF16), pltpu.VMEM((rows, width), BF16)],
+        flops=LINK_FLOPS,
+    )
+
+
+def attend_back(kept, d_residual, res_grad, weights):
+    w_query, w_key_up, w_value_up, w_out, w_gate, w_up, w_down, w_latent, gain_attn, gain_mlp = weights
+    source, attn_in, queries, latents, keys, values, heads_out, norms = kept[:8]
+    rows, model = source.shape
+    split = (PIECES, 2, rows // PIECES // 2, model)
+    width = w_query.shape[1]
+    res_grad = res_grad.reshape(rows, model)
     d_heads = mm(res_grad, w_out, 1, 1).astype(BF16)
     d_queries, d_keys, d_values = attend_backward(queries, keys, values, heads_out, d_heads, norms)
     d_latents = (mm(d_keys, w_key_up, 1, 1) + mm(d_values, w_value_up, 1, 1)).astype(BF16)
-    grads, gain_attn_grad = [], 0.0
-    for i in range(CHUNKS):
-        term = mm(chunk(d_queries, i), w_query, 1, 1) + mm(chunk(d_latents, i), w_latent, 1, 1)
-        part, gain_part = norm_backward(
-            at.own_half(chunk(source, i)).astype(F32), gain_attn, at.reduce(term)
-        )
-        gain_attn_grad = gain_attn_grad + gain_part
-        grads.append(at.join((d_residuals[i] + part).astype(BF16)))
-    g_out = mm(heads_out, res_grad, 0, 0).astype(BF16)
-    g_query = mm(attn_in, d_queries, 0, 0).astype(BF16)
-    g_key_up = mm(latents, d_keys, 0, 0).astype(BF16)
-    g_value_up = mm(latents, d_values, 0, 0).astype(BF16)
-    g_latent = mm(attn_in, d_latents, 0, 0).astype(BF16)
-    attention = pack_attention(g_query, g_key_up, g_value_up, g_out)
-    return jnp.concatenate(grads, axis=0), (
-        (attention, g_gate, g_up, g_down),
-        g_latent,
-        (gain_attn_grad, gain_mlp_grad),
-    )
+    input_grad, gain_grad, grads, g_latent = team_call(
+        attend_in_back_kernel, 3, model,
+        [(split, BF16), ((1, model), F32), ((2 * model + 2 * LH, width), BF16), (w_latent.shape, BF16)],
+        (d_queries, d_latents, w_query, w_latent, pieces_of(source), d_residual, gain_attn[None], attn_in,
+         heads_out, res_grad, latents, d_keys, d_values),
+        flops=LINK_FLOPS,
+    )
+    return input_grad.reshape(rows, model), gain_grad, grads, g_latent
 
 
 def local(
@@ -375,31 +608,47 @@
         return lax.dynamic_slice_in_dim(block, at.sequence * LEN, LEN, 0)
 
     source = sequence_rows(inputs)
-    first_out, first_kept = layer_forward(at, source, weights[0])
-    second_out, second_kept = layer_forward(at, first_out, weights[1])
-    second_grad, second_totals = layer_backward(at, second_kept, sequence_rows(out_grad), weights[1])
-    first_grad, first_totals = layer_backward(at, first_kept, second_grad, weights[0])
+    first_out, first_kept = layer_forward(source, weights[0])
+    second_out, second_kept = layer_forward(first_out, weights[1])
+    layer_mine = jnp.where(at.first, first_out, second_out)
+    layer_far = at.opposite(layer_mine)
+
+    def scatter(matrix):
+        return lax.psum_scatter(matrix, DP, scatter_dimension=0, tiled=True)
+
+    d_residual, res_grad, mlp_gain_two, feed_two = feed_back(
+        second_kept, sequence_rows(out_grad), weights[1]
+    )
+    feed_two = scatter(feed_two)
+    second_grad, attn_gain_two, attend_two, latent_two = attend_back(
+        second_kept, d_residual, res_grad, weights[1]
+    )
+    second_grad, layer_far = lax.optimization_barrier((second_grad, layer_far))
+    attend_two = scatter(attend_two)
+    d_residual, res_grad, mlp_gain_one, feed_one = feed_back(first_kept, second_grad, weights[0])
+    d_residual, feed_two = lax.optimization_barrier((d_residual, feed_two))
+    feed_one = scatter(feed_one)
+    first_grad, attn_gain_one, attend_one, latent_one = attend_back(
+        first_kept, d_residual, res_grad, weights[0]
+    )
+    attend_one = scatter(attend_one)
 
     def both_sequences(mine, other):
         top = at.sequence == 0
         return jnp.concatenate([jnp.where(top, mine, other), jnp.where(top, other, mine)], axis=0)[None]
 
-    layer_mine = jnp.where(at.first, first_out, second_out)
-    layer_out = both_sequences(layer_mine, at.opposite(layer_mine))
+    layer_out = both_sequences(layer_mine, layer_far)
     grad_mine = jnp.where(at.first, first_grad, second_grad)
     grad_far = at.opposite(second_grad, (1,)) + at.opposite(first_grad, (0,))
     input_grad = both_sequences(grad_mine, grad_far)
 
-    def scatter(matrix):
-        return lax.psum_scatter(matrix, DP, scatter_dimension=0, tiled=True)
-
-    totals = []
-    for one, two in zip(first_totals[0], second_totals[0]):
-        one, two = scatter(one), scatter(two)
+    def gather(one, two):
         far_part = at.across(two, (0,)) + at.across(one, (1,))
         mine = jnp.where(at.first, one, two).astype(F32) + far_part.astype(F32)
-        totals.append(lax.all_gather(mine.astype(BF16), DP, axis=0, tiled=True).astype(F32))
-    g_query, g_key_up, g_value_up, g_out = unpack_attention(totals[0], model)
+        return lax.all_gather(mine.astype(BF16), DP, axis=0, tiled=True).astype(F32)
+
+    g_feed = gather(feed_one, feed_two)
+    g_query, g_key_up, g_value_up, g_out = unpack_attention(gather(attend_one, attend_two), model)
 
     def latent_rows(mine, shard):
         wide = lax.dynamic_update_slice_in_dim(
@@ -407,11 +656,11 @@
         )
         return lax.psum_scatter(wide, TEN, scatter_dimension=0, tiled=True)
 
-    one = latent_rows(first_totals[1], jnp.where(at.first, at.z, opposite_z))
-    two = latent_rows(second_totals[1], jnp.where(at.first, opposite_z, at.z))
+    one = latent_rows(latent_one, jnp.where(at.first, at.z, opposite_z))
+    two = latent_rows(latent_two, jnp.where(at.first, opposite_z, at.z))
     mine = jnp.where(at.first, one, two) + at.swap(jnp.where(at.first, two, one))
     g_latent = lax.psum(mine, DP).astype(F32)
-    gains = lax.psum(jnp.stack(first_totals[2] + second_totals[2]), (SEC, DP, TEN)) / at.team
+    gains = lax.psum(jnp.concatenate([attn_gain_one, mlp_gain_one, attn_gain_two, mlp_gain_two], axis=0), (SEC, DP, TEN)) / at.team
     gains = jnp.where(at.first, gains[:2], gains[2:])
     width = model // at.count
     gains = lax.dynamic_slice_in_dim(gains, at.z * width, width, 1)
@@ -423,9 +672,9 @@
         g_key_up[None],
         g_value_up[None],
         g_out[None],
-        totals[1][None],
-        totals[2][None],
-        totals[3][None],
+        g_feed[None, :model],
+        g_feed[None, model : 2 * model],
+        g_feed[2 * model :].T[None],
         gains[0:1],
         gains[1:2],
     )

time: 852 us -> 880 us (1.033)
  Pallas kernels: 32.9 us -> 349 us
  waiting for transfers between devices: 403 us -> 266 us
  matrix products: 101 us -> 16 us
  other arithmetic: 118 us -> 53.3 us
  starting transfers between devices: 59.9 us -> 19.8 us
  blocking collectives: 69.1 us -> 105 us
    pallas_call x0 -> x8, Pallas kernels: none -> 316 us  [team_call(): pl.pallas_call(kernel, in_specs=[vmem] * len(operands), out_specs=[vmem]...]
    ppermute x16 -> x0, waiting for transfers between devices: 168 us -> none  [team_sum(): parts.append(lax.ppermute(block, TEN, route))]
    dot_general x64 -> x14, matrix products: 101 us -> 16 us  [mm(): return lax.dot_general(left, right, dims, preferred_element_type=F32)]
    reduce_scatter x8 -> x4, waiting for transfers between devices: 18.8 us -> 100 us  [scatter(): return lax.psum_scatter(matrix, DP, scatter_dimension=0, tiled=True)]
    ppermute x12 -> x8, waiting for transfers between devices: 167 us -> 97.6 us  [across(): return lax.ppermute(block, (SEC, TEN), route)]
    ppermute x3, waiting for transfers between devices: 0.01 us -> 35.9 us  [opposite(): return lax.ppermute(block, (SEC, TEN), route)]
    psum x1, blocking collectives: 69.1 us -> 105 us  [local(): lax.psum(jnp.concatenate([attn_gain_one, mlp_gain_one, attn_gain_two, mlp...]
    convert_element_type x31 -> x4, other arithmetic: 37.8 us -> 9.41 us  [gather(): return lax.all_gather(mine.astype(BF16), DP, axis=0, tiled=True).astype(F32)]
  transfers between devices with their start and end apart: 85 -> 27, of which waited for: 32 -> 12; matrix products, arithmetic and copies ran while one was open for 26% -> 9% of each run, Pallas kernels for 3% -> 22%
where the time goes in v1:
time: 880 us; the launch traced here: 875 us
  Pallas kernels  349 us (40%)
  waiting for transfers between devices  266 us (30%)
  blocking collectives  105 us (12%)
  other arithmetic  53.3 us (6%)
  local copies, waits for them, and re-layouts  50.8 us (6%)
  starting transfers between devices  19.8 us (2%)
  matrix products  16 us (2%)
  between operations  15.2 us (2%)
    pallas_call x8, Pallas kernels, team_call(): pl.pallas_call(kernel, in_specs=[vmem] * len(operands), out_specs=[vmem]...  316 us
    psum x1, blocking collectives, local(): lax.psum(jnp.concatenate([attn_gain_one, mlp_gain_one, attn_gain_two, mlp...  105 us
    reduce_scatter x4, waiting for transfers between devices, scatter(): return lax.psum_scatter(matrix, DP, scatter_dimension=0, tiled=True)  100 us
    ppermute x8, waiting for transfers between devices, across(): return lax.ppermute(block, (SEC, TEN), route)  97.6 us
    ppermute x3, waiting for transfers between devices, opposite(): return lax.ppermute(block, (SEC, TEN), route)  35.9 us
    unnamed x139, local copies, waits for them, and re-layouts  28.7 us
    reduce_scatter x2, waiting for transfers between devices, latent_rows(): return lax.psum_scatter(wide, TEN, scatter_dimension=0, tiled=True)  25.7 us
    pallas_call x2, Pallas kernels, attend_backward(): pl.pallas_call(attend_back_kernel, grid=(columns // width,), in_specs=[sp...  18.1 us
  transfers between devices with their start and end apart: 27, of which 12 were waited for; matrix products, arithmetic and copies ran while one was open for 9% of the time, Pallas kernels for 22%

profile of v1, /device:TPU:0, one launch (start us, length us, event | category | flops | bytes accessed | tf_op | source)
XLA Modules:
  0.0 874.6 jit_solution(16157840294122661738)
XLA Ops:
  15.9 14.5 %collective-permute-done.1 = bf16[640,256]{1,0:T(8,128)(2,1)S(1)} collective-permute-done((bf16[640,256]{1,0:T(8,128)(2,1)S(1)}, bf16[640,256]{1,0:T(8,128)(2,1)S(1)}, u32[]{:S(2)}, u32[]{:S(2)}) %collective-permute-start.1) | collective-permute-done | bytes 327712 | tf_op jit(solution)/shard_map/ppermute | solution.py:175
  32.2 18.5 %collective-permute-done.5 = bf16[176,1024]{1,0:T(8,128)(2,1)S(1)} collective-permute-done((bf16[176,1024]{1,0:T(8,128)(2,1)S(1)}, bf16[176,1024]{1,0:T(8,128)(2,1)S(1)}, u32[]{:S(2)}, u32[]{:S(2)}) %collective-permute-start.5) | collective-permute-done | bytes 360480 | tf_op jit(solution)/shard_map/ppermute | solution.py:175
  53.5 20.3 %collective-permute-done.3 = bf16[256,704]{1,0:T(8,128)(2,1)} collective-permute-done((bf16[256,704]{1,0:T(8,128)(2,1)}, bf16[256,704]{1,0:T(8,128)(2,1)}, u32[]{:S(2)}, u32[]{:S(2)}) %collective-permute-start.3) | collective-permute-done | bytes 360480 | tf_op jit(solution)/shard_map/ppermute | solution.py:175
  89.0 8.0 collective-permute-done.4
  106.0 7.4 shard_map.211
  115.7 33.2 %shard_map.212 = (f32[4,128,1024]{2,1,0:T(8,128)}, bf16[4,2,128,1024]{3,2,1,0:T(8,128)(2,1)}) custom-call(bf16[1024,256]{1,0:T(8,128)(2,1)} %copy-done.10, bf16[256,1024]{1,0:T(8,128)(2,1)} %get-tuple-element.166.w_out, bf16[4,2,128,1024]{3,2,1,0:T(8,128)(2,1)} %bitcast.118, f32[1,1024]{1,0:T(1,128)} %get-tuple-element.170.gain), custom_call_target="tpu_custom_call" | custom-call | flops 30000001024 | bytes 4194304 | tf_op jit(solution)/shard_map/pallas_call | solution.py:478
  163.2 37.3 %shard_map.213 = (f32[1024,704]{1,0:T(8,128)}, f32[1024,704]{1,0:T(8,128)}, bf16[1024,704]{1,0:T(8,128)(2,1)}, bf16[4,2,128,1024]{3,2,1,0:T(8,128)(2,1)}) custom-call(bf16[1024,1024]{1,0:T(8,128)(2,1)} %bitcast.132, bf16[1024,704]{1,0:T(8,128)(2,1)} %get-tuple-element.144.w_gate, bf16[1024,704]{1,0:T(8,128)(2,1)} %get-tuple-element.142.w_up, ...), custom_call_target="tpu_custom_call" | custom-call | flops 30000001024 | bytes 4194304 | tf_op jit(solution)/shard_map/pallas_call | solution.py:478
  208.3 7.3 shard_map.214
  216.4 33.1 %shard_map.215 = (f32[4,128,1024]{2,1,0:T(8,128)}, bf16[4,2,128,1024]{3,2,1,0:T(8,128)(2,1)}) custom-call(bf16[1024,256]{1,0:T(8,128)(2,1)} %copy-done.12, bf16[256,1024]{1,0:T(8,128)(2,1)} %get-tuple-element.165.w_out, bf16[4,2,128,1024]{3,2,1,0:T(8,128)(2,1)} %get-tuple-element.57.source, f32[1,1024]{1,0:T(1,128)} %get-tuple-element.169.gain), custom_call_target="tpu_custom_call" | custom-call | flops 30000001024 | bytes 4194304 | tf_op jit(solution)/shard_map/pallas_call | solution.py:478
  249.5 37.4 %shard_map.216 = (f32[1024,704]{1,0:T(8,128)}, f32[1024,704]{1,0:T(8,128)}, bf16[1024,704]{1,0:T(8,128)(2,1)}, bf16[4,2,128,1024]{3,2,1,0:T(8,128)(2,1)}) custom-call(bf16[1024,1024]{1,0:T(8,128)(2,1)} %bitcast.138, bf16[1024,704]{1,0:T(8,128)(2,1)} %get-tuple-element.143.w_gate, bf16[1024,704]{1,0:T(8,128)(2,1)} %get-tuple-element.141.w_up, ...), custom_call_target="tpu_custom_call" | custom-call | flops 30000001024 | bytes 4194304 | tf_op jit(solution)/shard_map/pallas_call | solution.py:478
  286.9 41.7 %shard_map.217 = (f32[4,128,1024]{2,1,0:T(8,128)}, bf16[4,2,128,1024]{3,2,1,0:T(8,128)(2,1)}, f32[1,1024]{1,0:T(1,128)}, bf16[3072,704]{1,0:T(8,128)(2,1)}) custom-call(bf16[4,2,128,1024]{3,2,1,0:T(8,128)(2,1)} %bitcast.127, bf16[1024,704]{1,0:T(8,128)(2,1)} %get-tuple-element.143.w_gate, bf16[1024,704]{1,0:T(8,128)(2,1)} %get-tuple-element.141.w_up, ...), custom_call_target="tpu_custom_call" | custom-call | flops 30000001024 | bytes 4194304 | tf_op jit(solution)/shard_map/pallas_call | solution.py:478
  335.7 9.3 %shard_map.218 = (bf16[1024,256]{1,0:T(8,128)(2,1)S(1)}, bf16[1024,256]{1,0:T(8,128)(2,1)S(1)}, bf16[1024,256]{1,0:T(8,128)(2,1)S(1)}) custom-call(bf16[1024,256]{1,0:T(8,128)(2,1)S(1)} %convolution_convert_fusion.7.q_ref, bf16[1024,256]{1,0:T(8,128)(2,1)S(1)} %convolution_convert_fusion.1.k_ref, bf16[1024,256]{1,0:T(8,128)(2,1)S(1)} %convolution_convert_fusion.v_ref, ...), custom_call_target="tpu_custom_call" | custom-call | flops 5368709120 | bytes 4194304 | tf_op jit(solution)/shard_map/pallas_call | solution.py:136
  348.5 56.4 %shard_map.219 = (bf16[4,2,128,1024]{3,2,1,0:T(8,128)(2,1)}, f32[1,1024]{1,0:T(1,128)}, bf16[2560,256]{1,0:T(8,128)(2,1)}, bf16[1024,256]{1,0:T(8,128)(2,1)}) custom-call(bf16[1024,256]{1,0:T(8,128)(2,1)} %copy-done.15, bf16[1024,256]{1,0:T(8,128)(2,1)} %fusion.5.d_latents, bf16[1024,256]{1,0:T(8,128)(2,1)} %get-tuple-element.149.w_query, ...), custom_call_target="tpu_custom_call" | custom-call | flops 30000001024 | bytes 4194304 | tf_op jit(solution)/shard_map/pallas_call | solution.py:478
  407.1 35.9 %collective-permute-done.6 = bf16[1024,1024]{1,0:T(8,128)(2,1)} collective-permute-done((bf16[1024,1024]{1,0:T(8,128)(2,1)}, bf16[1024,1024]{1,0:T(8,128)(2,1)}, u32[]{:S(2)}, u32[]{:S(2)}) %collective-permute-start.6) | collective-permute-done | bytes 2097184 | tf_op jit(solution)/shard_map/ppermute | solution.py:170
  443.0 41.1 %shard_map.220 = (f32[4,128,1024]{2,1,0:T(8,128)}, bf16[4,2,128,1024]{3,2,1,0:T(8,128)(2,1)}, f32[1,1024]{1,0:T(1,128)}, bf16[3072,704]{1,0:T(8,128)(2,1)}) custom-call(bf16[4,2,128,1024]{3,2,1,0:T(8,128)(2,1)} %get-tuple-element.71, bf16[1024,704]{1,0:T(8,128)(2,1)} %get-tuple-element.144.w_gate, bf16[1024,704]{1,0:T(8,128)(2,1)} %get-tuple-element.142.w_up, ...), custom_call_target="tpu_custom_call" | custom-call | flops 30000001024 | bytes 4194304 | tf_op jit(solution)/shard_map/pallas_call | solution.py:478
  486.7 8.9 %shard_map.221 = (bf16[1024,256]{1,0:T(8,128)(2,1)S(1)}, bf16[1024,256]{1,0:T(8,128)(2,1)S(1)}, bf16[1024,256]{1,0:T(8,128)(2,1)S(1)}) custom-call(bf16[1024,256]{1,0:T(8,128)(2,1)S(1)} %copy-done.9, bf16[1024,256]{1,0:T(8,128)(2,1)S(1)} %copy-done.1, bf16[1024,256]{1,0:T(8,128)(2,1)S(1)} %copy-done.3, bf16[1024,256]{1,0:T(8,128)(2,1)S(1)} %copy-done.11, ...), custom_call_target="tpu_custom_call" | custom-call | flops 5368709120 | bytes 4194304 | tf_op jit(solution)/shard_map/pallas_call | solution.py:136
  499.8 35.7 %shard_map.222 = (bf16[4,2,128,1024]{3,2,1,0:T(8,128)(2,1)}, f32[1,1024]{1,0:T(1,128)}, bf16[2560,256]{1,0:T(8,128)(2,1)}, bf16[1024,256]{1,0:T(8,128)(2,1)}) custom-call(bf16[1024,256]{1,0:T(8,128)(2,1)} %copy-done.14, bf16[1024,256]{1,0:T(8,128)(2,1)} %fusion.6.d_latents, bf16[1024,256]{1,0:T(8,128)(2,1)} %copy-done.41, bf16[1024,256]{1,0:T(8,128)(2,1)} %copy-done.43, ...), custom_call_target="tpu_custom_call" | custom-call | flops 30000001024 | bytes 4194304 | tf_op jit(solution)/shard_map/pallas_call | solution.py:478
  539.9 25.6 %reduce-scatter.13.cloned.1.call-done = bf16[256,512]{1,0:T(8,128)(2,1)} async-done(((bf16[1024,512]{1,0:T(8,128)(2,1)}), bf16[256,512]{1,0:T(8,128)(2,1)}) %reduce-scatter.13.cloned.1.call-update) | async-done | bytes 262160 | tf_op jit(solution)/shard_map/reduce_scatter | solution.py:657
  566.6 29.9 %reduce-scatter.11.cloned.1.call-done = bf16[640,256]{1,0:T(8,128)(2,1)} async-done(((bf16[2560,256]{1,0:T(8,128)(2,1)}), bf16[640,256]{1,0:T(8,128)(2,1)}) %reduce-scatter.11.cloned.1.call-update) | async-done | bytes 327696 | tf_op jit(solution)/shard_map/reduce_scatter | solution.py:617
  600.2 28.5 %reduce-scatter.9.cloned.1.call-done = bf16[640,256]{1,0:T(8,128)(2,1)} async-done(((bf16[2560,256]{1,0:T(8,128)(2,1)}), bf16[640,256]{1,0:T(8,128)(2,1)}) %reduce-scatter.9.cloned.1.call-update) | async-done | bytes 327696 | tf_op jit(solution)/shard_map/reduce_scatter | solution.py:617
  631.8 9.9 %collective-permute-done.10 = bf16[640,256]{1,0:T(8,128)(2,1)S(1)} collective-permute-done((bf16[640,256]{1,0:T(8,128)(2,1)}, bf16[640,256]{1,0:T(8,128)(2,1)S(1)}, u32[]{:S(2)}, u32[]{:S(2)}) %collective-permute-start.10) | collective-permute-done | bytes 327712 | tf_op jit(solution)/shard_map/ppermute | solution.py:175
  646.7 42.0 %reduce-scatter.17.cloned.1.call-done = bf16[768,704]{1,0:T(8,128)(2,1)} async-done(((bf16[3072,704]{1,0:T(8,128)(2,1)}), bf16[768,704]{1,0:T(8,128)(2,1)}) %reduce-scatter.17.cloned.1.call-update) | async-done | bytes 1081360 | tf_op jit(solution)/shard_map/reduce_scatter | solution.py:617
  694.0 26.4 %collective-permute-done.13 = bf16[768,704]{0,1:T(8,128)(2,1)} collective-permute-done((bf16[768,704]{0,1:T(8,128)(2,1)}, bf16[768,704]{0,1:T(8,128)(2,1)}, u32[]{:S(2)}, u32[]{:S(2)}) %collective-permute-start.13) | collective-permute-done | bytes 1081376 | tf_op jit(solution)/shard_map/ppermute | solution.py:175
  734.7 104.8 %psum.15 = f32[4,1024]{1,0:T(4,128)S(1)} all-reduce(f32[4,1024]{1,0:T(4,128)S(1)} %pad_maximum_fusion.4), channel_id=1, replica_groups=mesh['section'=2,'dp'=4,'tensor'=4] {'section','dp','tensor'}, use_global_device_ids=true, to_apply=%region_9.10 | all-reduce | flops 4096 | bytes 32768 | tf_op jit(solution)/shard_map/psum | solution.py:663
  (262 shorter events, 146.4 us)
Async XLA Ops:
  7.2 93.7 %all-gather.7.cloned.1.call-start = ((), (), s32[]{:S(2)}) async-start(), calls=%async_computation.6 | async-start | bytes 1638400 | tf_op jit(solution)/shard_map/all_gather | solution.py:592
  31.1 117.8 %all-gather.13.cloned.1.call-start = ((), (), s32[]{:S(2)}) async-start(), calls=%async_computation.9 | async-start | bytes 1802240 | tf_op jit(solution)/shard_map/all_gather | solution.py:592
  32.1 18.6 %collective-permute-start.5 = (bf16[176,1024]{1,0:T(8,128)(2,1)S(1)}, bf16[176,1024]{1,0:T(8,128)(2,1)S(1)}, u32[]{:S(2)}, u32[]{:S(2)}) collective-permute-start(bf16[176,1024]{1,0:T(8,128)(2,1)S(1)} %dynamic-slice_bitcast_fusion.1), channel_id=1, source_target_pairs={{0,18},{1,19},{2,16},{3,17},{16,2},{17,3},{18,0},{19,1},{4,22},{5,... | collective-permute-start | bytes 1081352 | tf_op jit(solution)/shard_map/ppermute | solution.py:175
  51.5 100.8 %all-gather.9.cloned.1.call-start = ((), (), s32[]{:S(2)}) async-start(), calls=%async_computation.7 | async-start | bytes 1966080 | tf_op jit(solution)/shard_map/all_gather | solution.py:592
  53.5 20.3 %collective-permute-start.3 = (bf16[256,704]{1,0:T(8,128)(2,1)}, bf16[256,704]{1,0:T(8,128)(2,1)}, u32[]{:S(2)}, u32[]{:S(2)}) collective-permute-start(bf16[256,704]{1,0:T(8,128)(2,1)} %bitcast.128), channel_id=1, source_target_pairs={{0,18},{1,19},{2,16},{3,17},{16,2},{17,3},{18,0},{19,1},{4,22},{5,... | collective-permute-start | bytes 1081352 | tf_op jit(solution)/shard_map/ppermute | solution.py:175
  73.8 86.1 %all-gather.11.cloned.1.call-start = ((), (), s32[]{:S(2)}) async-start(), calls=%async_computation.8 | async-start | bytes 1966080 | tf_op jit(solution)/shard_map/all_gather | solution.py:592
  75.5 21.7 %collective-permute-start.2 = (bf16[1024,256]{1,0:T(8,128)(2,1)}, bf16[1024,256]{1,0:T(8,128)(2,1)}, u32[]{:S(2)}, u32[]{:S(2)}) collective-permute-start(bf16[1024,256]{1,0:T(8,128)(2,1)} %dynamic-slice_bitcast_fusion), channel_id=1, source_target_pairs={{0,16},{16,0},{1,17},{17,1},{2,18},{18,2},{3,19},{19,3},{4,20},{20... | collective-permute-start | bytes 1572872 | tf_op jit(solution)/shard_map/ppermute | solution.py:165
  76.8 20.3 %collective-permute-start.4 = (bf16[256,704]{1,0:T(8,128)(2,1)}, bf16[256,704]{1,0:T(8,128)(2,1)}, u32[]{:S(2)}, u32[]{:S(2)}) collective-permute-start(bf16[256,704]{1,0:T(8,128)(2,1)} %bitcast.12), channel_id=1, source_target_pairs={{0,18},{1,19},{2,16},{3,17},{16,2},{17,3},{18,0},{19,1},{4,22},{5,... | collective-permute-start | bytes 1081352 | tf_op jit(solution)/shard_map/ppermute | solution.py:175
  97.1 402.8 %reduce-scatter.7.cloned.1.call-start = ((), (), s32[]{:S(2)}) async-start(), calls=%async_computation.10 | async-start | bytes 5898240 | tf_op jit(solution)/shard_map/reduce_scatter | solution.py:617
  328.6 211.3 %reduce-scatter.15.cloned.1.call-start = ((), (), s32[]{:S(2)}) async-start(), calls=%async_computation.15 | async-start | bytes 1310720 | tf_op jit(solution)/shard_map/reduce_scatter | solution.py:657
  332.0 110.9 %collective-permute-start.6 = (bf16[1024,1024]{1,0:T(8,128)(2,1)}, bf16[1024,1024]{1,0:T(8,128)(2,1)}, u32[]{:S(2)}, u32[]{:S(2)}) collective-permute-start(bf16[1024,1024]{1,0:T(8,128)(2,1)} %bitcast.19), channel_id=1, source_target_pairs={{0,2},{1,3},{2,0},{3,1},{16,18},{17,19},{18,16},{19,17},{4,6},{5,7... | collective-permute-start | bytes 6291464 | tf_op jit(solution)/shard_map/ppermute | solution.py:170
  407.0 158.5 %reduce-scatter.13.cloned.1.call-start = ((), (), s32[]{:S(2)}) async-start(), calls=%async_computation.14 | async-start | bytes 1310720 | tf_op jit(solution)/shard_map/reduce_scatter | solution.py:657
  537.7 58.7 %reduce-scatter.11.cloned.1.call-start = ((), (), s32[]{:S(2)}) async-start(), calls=%async_computation.12 | async-start | bytes 1638400 | tf_op jit(solution)/shard_map/reduce_scatter | solution.py:617
  538.5 90.3 %reduce-scatter.9.cloned.1.call-start = ((), (), s32[]{:S(2)}) async-start(), calls=%async_computation.11 | async-start | bytes 1638400 | tf_op jit(solution)/shard_map/reduce_scatter | solution.py:617
  539.2 149.5 %reduce-scatter.17.cloned.1.call-start = ((), (), s32[]{:S(2)}) async-start(), calls=%async_computation.17 | async-start | bytes 5898240 | tf_op jit(solution)/shard_map/reduce_scatter | solution.py:617
  539.8 306.1 %all-reduce.2.cloned.1.call-start = ((), (), s32[]{:S(2)}) async-start(), calls=%async_computation.16 | async-start | bytes 524288 | tf_op jit(solution)/shard_map/psum | solution.py:662
  566.5 63.5 %collective-permute-start.11 = (bf16[256,512]{1,0:T(8,128)(2,1)S(1)}, bf16[256,512]{1,0:T(8,128)(2,1)S(1)}, u32[]{:S(2)}, u32[]{:S(2)}) collective-permute-start(bf16[256,512]{1,0:T(8,128)(2,1)S(1)} %broadcast_select_fusion.8), channel_id=1, source_target_pairs={{0,16},{16,0},{1,17},{17,1},{2,18},{18,2},{3,19},{19,3},{4,20},{20... | collective-permute-start | bytes 786440 | tf_op jit(solution)/shard_map/ppermute | solution.py:165
  596.5 35.4 %collective-permute-start.9 = (bf16[640,256]{1,0:T(8,128)(2,1)}, bf16[640,256]{1,0:T(8,128)(2,1)S(1)}, u32[]{:S(2)}, u32[]{:S(2)}) collective-permute-start(bf16[640,256]{1,0:T(8,128)(2,1)} %reduce-scatter.11.cloned.1.call-done), channel_id=1, source_target_pairs={{0,18},{1,19},{2,16},{3,17},{4,22},{5,23},{6,20},{7,21},{8,26},{9,... | collective-permute-start | bytes 983048 | tf_op jit(solution)/shard_map/ppermute | solution.py:175
  631.8 215.9 %all-gather.15.cloned.1.call-start = ((), (), s32[]{:S(2)}) async-start(), calls=%async_computation.13 | async-start | bytes 1638400 | tf_op jit(solution)/shard_map/all_gather | solution.py:648
  643.6 208.8 %all-gather.17.cloned.1.call-start = ((), (), s32[]{:S(2)}) async-start(), calls=%async_computation.18 | async-start | bytes 5898240 | tf_op jit(solution)/shard_map/all_gather | solution.py:648
  644.4 48.0 %collective-permute-start.12 = (bf16[768,704]{0,1:T(8,128)(2,1)S(1)}, bf16[768,704]{0,1:T(8,128)(2,1)}, u32[]{:S(2)}, u32[]{:S(2)}) collective-permute-start(bf16[768,704]{0,1:T(8,128)(2,1)S(1)} %copy.46), channel_id=1, source_target_pairs={{0,18},{1,19},{2,16},{3,17},{4,22},{5,23},{6,20},{7,21},{8,26},{9,... | collective-permute-start | bytes 3244040 | tf_op jit(solution)/shard_map/ppermute | solution.py:175
  691.0 29.4 %collective-permute-start.13 = (bf16[768,704]{0,1:T(8,128)(2,1)}, bf16[768,704]{0,1:T(8,128)(2,1)}, u32[]{:S(2)}, u32[]{:S(2)}) collective-permute-start(bf16[768,704]{0,1:T(8,128)(2,1)} %copy.47), channel_id=1, source_target_pairs={{16,2},{17,3},{18,0},{19,1},{20,6},{21,7},{22,4},{23,5},{24,10},{2... | collective-permute-start | bytes 3244040 | tf_op jit(solution)/shard_map/ppermute | solution.py:175
  725.6 114.4 %collective-permute-start.7 = (bf16[1024,1024]{1,0:T(8,128)(2,1)}, bf16[1024,1024]{1,0:T(8,128)(2,1)}, u32[]{:S(2)}, u32[]{:S(2)}) collective-permute-start(bf16[1024,1024]{1,0:T(8,128)(2,1)} %bitcast.120), channel_id=1, source_target_pairs={{16,18},{17,19},{18,16},{19,17},{20,22},{21,23},{22,20},{23,21},{2... | collective-permute-start | bytes 6291464 | tf_op jit(solution)/shard_map/ppermute | solution.py:170
  727.6 112.5 %collective-permute-start.8 = (bf16[1024,1024]{1,0:T(8,128)(2,1)}, bf16[1024,1024]{1,0:T(8,128)(2,1)}, u32[]{:S(2)}, u32[]{:S(2)}) collective-permute-start(bf16[1024,1024]{1,0:T(8,128)(2,1)} %bitcast.122), channel_id=1, source_target_pairs={{0,2},{1,3},{2,0},{3,1},{4,6},{5,7},{6,4},{7,5},{8,10},{9,11},{10,... | collective-permute-start | bytes 6291464 | tf_op jit(solution)/shard_map/ppermute | solution.py:170
  (67 other events, 1006.6 us)
Sparse Core Ops, SparseCore 0:
  31.2 31.3 all-gather.6
  64.4 29.8 all-gather.12
  96.2 30.9 all-gather.8
  128.9 30.9 all-gather.10
  328.7 57.1 reduce-scatter.6
  407.1 35.8 reduce-scatter.14
  537.8 27.6 reduce-scatter.12
  568.4 27.9 reduce-scatter.10
  599.4 29.3 reduce-scatter.8
  631.6 57.0 reduce-scatter.16
  692.2 42.9 all-reduce.1
  737.6 28.9 all-gather.14
  769.2 57.0 all-gather.16

commit v2 on v1

--- a/solution.py
+++ b/solution.py
@@ -217,12 +217,218 @@
         place = lax.rem(self.place + step, self.size)
         return place, {TEN: self.base + place}
 
-    def greet(self):
-        barrier = pltpu.get_barrier_semaphore()
-        pl.semaphore_signal(barrier, inc=1, device_id=self.other, device_id_type=MESH)
-        for step in range(1, self.size):
-            pl.semaphore_signal(barrier, inc=1, device_id=self.peer(step)[1], device_id_type=MESH)
-        pl.semaphore_wait(barrier, self.size)
+    def greet(self, others=()):
+        partners = [self.other] + [self.peer(step)[1] for step in range(1, self.size)]
+        greet(partners + list(others))
+
+
+def greet(partners):
+    barrier = pltpu.get_barrier_semaphore()
+    for partner in partners:
+        pl.semaphore_signal(barrier, inc=1, device_id=partner, device_id_type=MESH)
+    pl.semaphore_wait(barrier, len(partners))
+
+
+class Plane:
+    def __init__(self):
+        self.count = lax.axis_size(DP)
+        self.me = lax.axis_index(DP)
+
+    def peer(self, step):
+        place = lax.rem(self.me + step, self.count)
+        return place, {DP: place}
+
+    def peers(self):
+        return [self.peer(step)[1] for step in range(1, self.count)]
+
+    def scatters(self, loads, refs):
+        items = []
+        for load in loads:
+            items.append(Scatter(self, load, *refs[:3]))
+            refs = refs[3:]
+        return items, refs
+
+
+def scatter_scratch(load):
+    count = load.shape[0]
+    return [
+        pltpu.VMEM(load.shape, BF16),
+        pltpu.SemaphoreType.DMA((count,)),
+        pltpu.SemaphoreType.DMA((count,)),
+    ]
+
+
+class Scatter:
+    def __init__(self, plane, load, slots, sent, here):
+        self.plane, self.load, self.slots, self.sent, self.here = plane, load, slots, sent, here
+
+    def copy(self, step, piece, slot):
+        return pltpu.make_async_remote_copy(
+            src_ref=self.load.at[piece],
+            dst_ref=self.slots.at[slot],
+            send_sem=self.sent.at[step],
+            recv_sem=self.here.at[slot],
+            device_id=self.plane.peer(step)[1],
+            device_id_type=MESH,
+        )
+
+    def start(self):
+        for step in range(1, self.plane.count):
+            self.copy(step, self.plane.peer(step)[0], self.plane.me).start()
+
+    def total(self):
+        total = self.load[self.plane.me].astype(F32)
+        for step in range(1, self.plane.count):
+            place = self.plane.peer(step)[0]
+            self.copy(step, place, place).wait_recv()
+            total = total + self.slots[place].astype(F32)
+        return total
+
+    def drain(self):
+        for step in range(1, self.plane.count):
+            self.copy(step, self.plane.peer(step)[0], self.plane.me).wait_send()
+
+
+class Gather:
+    def __init__(self, plane, whole, sent, here):
+        self.plane, self.whole, self.sent, self.here = plane, whole, sent, here
+
+    def copy(self, step, piece):
+        return pltpu.make_async_remote_copy(
+            src_ref=self.whole.at[piece],
+            dst_ref=self.whole.at[piece],
+            send_sem=self.sent.at[step],
+            recv_sem=self.here.at[piece],
+            device_id=self.plane.peer(step)[1],
+            device_id_type=MESH,
+        )
+
+    def start(self):
+        for step in range(1, self.plane.count):
+            self.copy(step, self.plane.me).start()
+
+    def finish(self):
+        for step in range(1, self.plane.count):
+            self.copy(step, self.plane.peer(step)[0]).wait_recv()
+            self.copy(step, self.plane.me).wait_send()
+
+
+FEED = 3
+
+
+def finish_kernel(groups, *refs):
+    zero, one = refs[:5], refs[5:10]
+    grad = refs[10]
+    outs = refs[11:16]
+    grad_far = refs[16]
+    refs = refs[17:]
+    leave, come = refs[:5], refs[5:10]
+    slots, held = refs[10], refs[11]
+    cross_sent, cross_here, gather_sent, gather_here = refs[12:16]
+    block_sent, block_here, grad_sent, grad_here = refs[16:20]
+    plane = Plane()
+    beside, _ = plane.scatters(zero[FEED:], refs[20:])
+    count = lax.axis_size(TEN)
+    z = lax.axis_index(TEN)
+    core = lax.axis_index(SEC)
+    first = core == 0
+    opposite = lax.rem(z + count // 2, count)
+    across = {SEC: 1 - core, TEN: opposite}
+    chips = [lax.rem(z + step, count) for step in range(1, count)]
+    greet(plane.peers() + [across] + [{TEN: chip} for chip in chips])
+    for scatter in beside:
+        scatter.start()
+
+    def cross(k):
+        return pltpu.make_async_remote_copy(
+            src_ref=leave[k],
+            dst_ref=come[k],
+            send_sem=cross_sent.at[k],
+            recv_sem=cross_here.at[k],
+            device_id=across,
+            device_id_type=MESH,
+        )
+
+    def depart(k, part):
+        leave[k][...] = jnp.where(first, one[k][...], part)
+        cross(k).start()
+
+    def arrive(k, part):
+        cross(k).wait_recv()
+        return jnp.where(first, part, one[k][...]).astype(F32) + come[k][...].astype(F32)
+
+    gathers = [Gather(plane, outs[k], gather_sent.at[k], gather_here.at[k]) for k in range(5)]
+
+    def spread(k, total):
+        outs[k][plane.me] = total.astype(BF16)
+        gathers[k].start()
+
+    for k in range(FEED):
+        depart(k, zero[k][...])
+    grad_copy = pltpu.make_async_remote_copy(
+        src_ref=grad,
+        dst_ref=grad_far,
+        send_sem=grad_sent,
+        recv_sem=grad_here,
+        device_id={TEN: opposite},
+        device_id_type=MESH,
+    )
+
+    @pl.when(first)
+    def _():
+        grad_copy.start()
+
+    late = []
+    for k, scatter in enumerate(beside):
+        held_part = scatter.total().astype(BF16)
+        late.append(held_part)
+        depart(FEED + k, held_part)
+    for k in range(FEED):
+        spread(k, arrive(k, zero[k][...]))
+    spread(FEED, arrive(FEED, late[0]))
+    held[...] = arrive(FEED + 1, late[1]).astype(BF16).reshape(held.shape)
+
+    def block(step, chip, slot):
+        return pltpu.make_async_remote_copy(
+            src_ref=held.at[chip],
+            dst_ref=slots.at[slot],
+            send_sem=block_sent.at[step],
+            recv_sem=block_here.at[slot],
+            device_id={TEN: chip},
+            device_id_type=MESH,
+        )
+
+    for step, chip in enumerate(chips):
+        block(step, chip, z).start()
+    slots[z] = held[z]
+    for step, chip in enumerate(chips):
+        block(step, chip, chip).wait_recv()
+    shares = [slots[shard].astype(F32) for shard in range(count)]
+    sums = [sum(s for s, g in zip(shares, groups) if g == group) for group in range(KVH)]
+    gain_rows = sums[0]
+    for extra in sums[1:]:
+        gain_rows = gain_rows + extra
+    depth = gain_rows.shape[0] - GAIN_ROWS
+    gain_rows = gain_rows * (2.0 / count)
+    blocks = [
+        jnp.concatenate([part[:depth], gain_rows[depth:]], axis=0) for part in sums
+    ]
+    spread(FEED + 1, jnp.concatenate(blocks, axis=1))
+    for gather in gathers:
+        gather.finish()
+    for scatter in beside:
+        scatter.drain()
+    for k in range(5):
+        cross(k).wait_send()
+    for step, chip in enumerate(chips):
+        block(step, chip, z).wait_send()
+
+    @pl.when(first)
+    def _():
+        grad_copy.wait()
+
+
+GAIN_ROWS = 16
 
 
 def exchange_scratch(team, rows, model):
@@ -388,12 +594,20 @@
 
 
 def feed_back_kernel(
-    upstream, w_gate, w_up, w_down, gate, up, hidden, mlp_in, residual, gain,
-    d_residual, res_grad, gain_grad, grads, d_gate, d_up, *refs
+    upstream, w_gate, w_up, w_down, gate, up, hidden, mlp_in, residual, gain, *rest
 ):
+    count = (len(rest) - 19) // 5
+    loads, rest = rest[:count], rest[count:]
+    d_residual, res_grad, gain_grad, g_gate, g_up, g_down = rest[:6]
+    sums, rest = rest[6 : 6 + count], rest[6 + count :]
+    (d_gate, d_up), rest = rest[:2], rest[2:]
     team = Team()
+    plane = Plane()
+    beside, refs = plane.scatters(loads, rest)
     ex = Exchange(team, refs)
-    team.greet()
+    team.greet(plane.peers() if loads else [])
+    for scatter in beside:
+        scatter.start()
     rows = mlp_in.shape[0]
     model = mlp_in.shape[1]
     shape = (rows // PIECES, model)
@@ -415,10 +629,10 @@
 
     each_piece(send)
     ex.combine(PIECES - 1)
-    grads[0:model, :] = mm(mlp_in[...], d_gate[...], 0, 0).astype(BF16)
-    grads[model : 2 * model, :] = mm(mlp_in[...], d_up[...], 0, 0).astype(BF16)
+    g_gate[...] = mm(mlp_in[...], d_gate[...], 0, 0).astype(BF16)
+    g_up[...] = mm(mlp_in[...], d_up[...], 0, 0).astype(BF16)
     whole = upstream[...].reshape(rows, model)
-    grads[2 * model :, :] = mm(whole, hidden[...], 0, 0).astype(BF16)
+    g_down[...] = mm(hidden[...], whole, 0, 0).astype(BF16)
     gain_grad[...] = jnp.zeros_like(gain_grad)
 
     def receive(i):
@@ -429,17 +643,28 @@
         ex.join(i, res_grad, block.astype(BF16))
 
     each_piece(receive)
+    for scatter, total in zip(beside, sums):
+        total[...] = scatter.total().astype(BF16)
     ex.finish(res_grad)
+    for scatter in beside:
+        scatter.drain()
 
 
 def attend_in_back_kernel(
     d_queries, d_latents, w_query, w_latent, source, d_residual, gain, attn_in,
-    heads_out, res_grad, latents, d_keys, d_values,
-    input_grad, gain_grad, grads, g_latent, *refs
+    heads_out, res_grad, latents, d_keys, d_values, *rest
 ):
+    count = (len(rest) - 15) // 5
+    loads, rest = rest[:count], rest[count:]
+    input_grad, gain_grad, grads, g_latent = rest[:4]
+    sums, rest = rest[4 : 4 + count], rest[4 + count :]
     team = Team()
+    plane = Plane()
+    beside, refs = plane.scatters(loads, rest)
     ex = Exchange(team, refs)
-    team.greet()
+    team.greet(plane.peers())
+    for scatter in beside:
+        scatter.start()
     rows = d_queries.shape[0]
 
     def send(i):
@@ -469,10 +694,17 @@
         ex.join(i, input_grad, (d_residual[i] + part).astype(BF16))
 
     each_piece(receive)
+    for scatter, total in zip(beside, sums):
+        total[...] = scatter.total().astype(BF16)
     ex.finish(input_grad)
-
-
-def team_call(kernel, number, model, outs, operands, scratch=(), flops=0):
+    for scatter in beside:
+        scatter.drain()
+
+
+def team_call(kernel, number, model, outs, operands, scratch=(), flops=0, loads=()):
+    operands = tuple(operands) + tuple(loads)
+    outs = outs + [(load.shape[1:], BF16) for load in loads]
+    beside = [item for load in loads for item in scatter_scratch(load)]
     team = lax.axis_size(TEN) // 2
     vmem = pl.BlockSpec(memory_space=pltpu.VMEM)
     return pl.pallas_call(
@@ -480,7 +712,7 @@
         in_specs=[vmem] * len(operands),
         out_specs=[vmem] * len(outs),
         out_shape=[jax.ShapeDtypeStruct(*out) for out in outs],
-        scratch_shapes=list(scratch) + exchange_scratch(team, LEN, model),
+        scratch_shapes=list(scratch) + beside + exchange_scratch(team, LEN, model),
         compiler_params=pltpu.CompilerParams(
             collective_id=number, has_side_effects=True, vmem_limit_bytes=VMEM_LIMIT
         ),
@@ -523,23 +755,42 @@
 LINK_FLOPS = 30 * 10**9
 
 
-def feed_back(kept, upstream, weights):
+def feed_back(kept, upstream, weights, number, loads=()):
     w_query, w_key_up, w_value_up, w_out, w_gate, w_up, w_down, w_latent, gain_attn, gain_mlp = weights
     residual, mlp_in, gate, up, hidden = kept[8:]
     rows, model = upstream.shape
     split = (PIECES, 2, rows // PIECES // 2, model)
     own = (PIECES, rows // PIECES // 2, model)
     width = w_gate.shape[1]
-    return team_call(
-        feed_back_kernel, 2, model,
-        [(own, F32), (split, BF16), ((1, model), F32), ((3 * model, width), BF16)],
+    d_residual, res_grad, gain_grad, *grads = team_call(
+        feed_back_kernel, number, model,
+        [(own, F32), (split, BF16), ((1, model), F32), (w_gate.shape, BF16), (w_gate.shape, BF16), (w_down.shape, BF16)],
         (pieces_of(upstream), w_gate, w_up, w_down, gate, up, hidden, mlp_in, residual, gain_mlp[None]),
         scratch=[pltpu.VMEM((rows, width), BF16), pltpu.VMEM((rows, width), BF16)],
         flops=LINK_FLOPS,
-    )
-
-
-def attend_back(kept, d_residual, res_grad, weights):
+        loads=loads,
+    )
+    return d_residual, res_grad, gain_grad, [by_dp(g) for g in grads[:3]], grads[3:]
+
+
+def by_dp(matrix):
+    count = lax.axis_size(DP)
+    return matrix.reshape(count, matrix.shape[0] // count, matrix.shape[1])
+
+
+def latent_parts(g_latent, gain_attn, gain_mlp):
+    count, pieces = lax.axis_size(TEN), lax.axis_size(DP)
+    model = g_latent.shape[0]
+    depth = model // count // pieces
+    rows = g_latent.reshape(count, pieces, depth, LH).transpose(1, 0, 2, 3)
+    gains = jnp.stack([gain_attn[0], gain_mlp[0]]).astype(BF16).reshape(2, count, model // count)
+    gains = gains.transpose(1, 0, 2)
+    gains = jnp.pad(gains, ((0, 0), (0, GAIN_ROWS - 2), (0, LH - model // count)))
+    gains = jnp.pad(gains[None], ((0, pieces - 1), (0, 0), (0, 0), (0, 0)))
+    return jnp.concatenate([rows, gains], axis=2).reshape(pieces, count * (depth + GAIN_ROWS), LH)
+
+
+def attend_back(kept, d_residual, res_grad, gain_mlp_grad, weights, loads):
     w_query, w_key_up, w_value_up, w_out, w_gate, w_up, w_down, w_latent, gain_attn, gain_mlp = weights
     source, attn_in, queries, latents, keys, values, heads_out, norms = kept[:8]
     rows, model = source.shape
@@ -549,14 +800,38 @@
     d_heads = mm(res_grad, w_out, 1, 1).astype(BF16)
     d_queries, d_keys, d_values = attend_backward(queries, keys, values, heads_out, d_heads, norms)
     d_latents = (mm(d_keys, w_key_up, 1, 1) + mm(d_values, w_value_up, 1, 1)).astype(BF16)
-    input_grad, gain_grad, grads, g_latent = team_call(
+    input_grad, gain_grad, grads, g_latent, *sums = team_call(
         attend_in_back_kernel, 3, model,
         [(split, BF16), ((1, model), F32), ((2 * model + 2 * LH, width), BF16), (w_latent.shape, BF16)],
         (d_queries, d_latents, w_query, w_latent, pieces_of(source), d_residual, gain_attn[None], attn_in,
          heads_out, res_grad, latents, d_keys, d_values),
         flops=LINK_FLOPS,
-    )
-    return input_grad.reshape(rows, model), gain_grad, grads, g_latent
+        loads=loads,
+    )
+    parts = [by_dp(grads), latent_parts(g_latent, gain_grad, gain_mlp_grad)]
+    return input_grad.reshape(rows, model), parts, sums
+
+
+def finish(groups, zero, one, grad):
+    pieces, count = lax.axis_size(DP), lax.axis_size(TEN)
+    vmem = pl.BlockSpec(memory_space=pltpu.VMEM)
+    depth = one[4].shape[0] // count
+    outs = [(pieces,) + part.shape for part in one[:4]] + [(pieces, depth, KVH * LH), grad.shape]
+    dma = pltpu.SemaphoreType.DMA
+    shapes = [pltpu.VMEM(part.shape, BF16) for part in one]
+    blocks = pltpu.VMEM((count, depth, LH), BF16)
+    return pl.pallas_call(
+        functools.partial(finish_kernel, groups),
+        in_specs=[vmem] * 11,
+        out_specs=[vmem] * 6,
+        out_shape=[jax.ShapeDtypeStruct(out, BF16) for out in outs],
+        scratch_shapes=shapes + shapes + [blocks, blocks]
+        + [dma((5,)), dma((5,)), dma((5, pieces)), dma((5, pieces)), dma((count,)), dma((count,)), dma, dma]
+        + scatter_scratch(zero[3]) + scatter_scratch(zero[4]),
+        compiler_params=pltpu.CompilerParams(
+            collective_id=5, has_side_effects=True, vmem_limit_bytes=VMEM_LIMIT
+        ),
+    )(*zero, *one, grad)
 
 
 def local(
@@ -610,60 +885,44 @@
     source = sequence_rows(inputs)
     first_out, first_kept = layer_forward(source, weights[0])
     second_out, second_kept = layer_forward(first_out, weights[1])
-    layer_mine = jnp.where(at.first, first_out, second_out)
-    layer_far = at.opposite(layer_mine)
-
-    def scatter(matrix):
-        return lax.psum_scatter(matrix, DP, scatter_dimension=0, tiled=True)
-
-    d_residual, res_grad, mlp_gain_two, feed_two = feed_back(
-        second_kept, sequence_rows(out_grad), weights[1]
-    )
-    feed_two = scatter(feed_two)
-    second_grad, attn_gain_two, attend_two, latent_two = attend_back(
-        second_kept, d_residual, res_grad, weights[1]
-    )
-    second_grad, layer_far = lax.optimization_barrier((second_grad, layer_far))
-    attend_two = scatter(attend_two)
-    d_residual, res_grad, mlp_gain_one, feed_one = feed_back(first_kept, second_grad, weights[0])
-    d_residual, feed_two = lax.optimization_barrier((d_residual, feed_two))
-    feed_one = scatter(feed_one)
-    first_grad, attn_gain_one, attend_one, latent_one = attend_back(
-        first_kept, d_residual, res_grad, weights[0]
-    )
-    attend_one = scatter(attend_one)
+    first_far = at.opposite(first_out, (0,))
+    second_far = at.opposite(second_out, (1,))
+    cotangent, first_far = lax.optimization_barrier((sequence_rows(out_grad), first_far))
+    d_residual, res_grad, mlp_gain, feed_two, _ = feed_back(second_kept, cotangent, weights[1], 2)
+    second_grad, late_two, feed_two = attend_back(
+        second_kept, d_residual, res_grad, mlp_gain, weights[1], feed_two
+    )
+    upstream, second_far = lax.optimization_barrier((second_grad, second_far))
+    grad_far = at.opposite(second_grad, (1,))
+    d_residual, res_grad, mlp_gain, feed_one, late_two = feed_back(
+        first_kept, upstream, weights[0], 4, late_two
+    )
+    first_grad, late_one, feed_one = attend_back(
+        first_kept, d_residual, res_grad, mlp_gain, weights[0], feed_one
+    )
+    late_one[0], grad_far = lax.optimization_barrier((late_one[0], grad_far))
+    groups = tuple(group_of(shard) for shard in range(at.count))
+    *wide, packed, latent, first_grad_far = finish(
+        groups, feed_one + late_one, feed_two + late_two, first_grad
+    )
 
     def both_sequences(mine, other):
         top = at.sequence == 0
         return jnp.concatenate([jnp.where(top, mine, other), jnp.where(top, other, mine)], axis=0)[None]
 
-    layer_out = both_sequences(layer_mine, layer_far)
-    grad_mine = jnp.where(at.first, first_grad, second_grad)
-    grad_far = at.opposite(second_grad, (1,)) + at.opposite(first_grad, (0,))
-    input_grad = both_sequences(grad_mine, grad_far)
-
-    def gather(one, two):
-        far_part = at.across(two, (0,)) + at.across(one, (1,))
-        mine = jnp.where(at.first, one, two).astype(F32) + far_part.astype(F32)
-        return lax.all_gather(mine.astype(BF16), DP, axis=0, tiled=True).astype(F32)
-
-    g_feed = gather(feed_one, feed_two)
-    g_query, g_key_up, g_value_up, g_out = unpack_attention(gather(attend_one, attend_two), model)
-
-    def latent_rows(mine, shard):
-        wide = lax.dynamic_update_slice_in_dim(
-            jnp.zeros((model, KVH * LH), BF16), mine, group_of(shard) * LH, 1
-        )
-        return lax.psum_scatter(wide, TEN, scatter_dimension=0, tiled=True)
-
-    one = latent_rows(latent_one, jnp.where(at.first, at.z, opposite_z))
-    two = latent_rows(latent_two, jnp.where(at.first, opposite_z, at.z))
-    mine = jnp.where(at.first, one, two) + at.swap(jnp.where(at.first, two, one))
-    g_latent = lax.psum(mine, DP).astype(F32)
-    gains = lax.psum(jnp.concatenate([attn_gain_one, mlp_gain_one, attn_gain_two, mlp_gain_two], axis=0), (SEC, DP, TEN)) / at.team
-    gains = jnp.where(at.first, gains[:2], gains[2:])
+    layer_out = both_sequences(
+        jnp.where(at.first, first_out, second_out), jnp.where(at.first, first_far, second_far)
+    )
+    input_grad = both_sequences(
+        jnp.where(at.first, first_grad, second_grad), jnp.where(at.first, first_grad_far, grad_far)
+    )
+    g_gate, g_up, g_down = [part.reshape(-1, part.shape[2]).astype(F32) for part in wide]
+    packed = packed.reshape(-1, packed.shape[2]).astype(F32)
+    g_query, g_key_up, g_value_up, g_out = unpack_attention(packed, model)
     width = model // at.count
-    gains = lax.dynamic_slice_in_dim(gains, at.z * width, width, 1)
+    depth = latent.shape[1] - GAIN_ROWS
+    g_latent = latent[:, :depth].reshape(width, KVH * LH).astype(F32)
+    gains = latent[0, depth : depth + 2, :width].astype(F32)
     return (
         layer_out,
         input_grad,
@@ -672,9 +931,9 @@
         g_key_up[None],
         g_value_up[None],
         g_out[None],
-        g_feed[None, :model],
-        g_feed[None, model : 2 * model],
-        g_feed[2 * model :].T[None],
+        g_gate[None],
+        g_up[None],
+        g_down[None],
         gains[0:1],
         gains[1:2],
     )

time: 880 us -> 787 us (0.89)
  Pallas kernels: 349 us -> 597 us
  waiting for transfers between devices: 266 us -> 65.3 us
  blocking collectives: 105 us -> 0 us
  local copies, waits for them, and re-layouts: 50.8 us -> 36.7 us
    pallas_call x0 -> x1, Pallas kernels: none -> 148 us  [finish(): pl.pallas_call(functools.partial(finish_kernel, groups), in_specs=[vmem]...]
    reduce_scatter x6 -> x0, waiting for transfers between devices: 126 us -> none  [the longest x4 100 us: scatter(): return lax.psum_scatter(matrix, DP, scatter_dimension=0, tiled=True)]
    psum x1 -> x0, blocking collectives: 105 us -> none  [local(): lax.psum(jnp.concatenate([attn_gain_one, mlp_gain_one, attn_gain_two, mlp...]
    pallas_call x8, Pallas kernels: 316 us -> 417 us  [team_call(): pl.pallas_call(kernel, in_specs=[vmem] * len(operands), out_specs=[vmem]...]
    ppermute x8 -> x4, waiting for transfers between devices: 97.6 us -> 60.3 us  [across(): return lax.ppermute(block, (SEC, TEN), route)]
    ppermute x3, waiting for transfers between devices: 35.9 us -> 0.01 us  [opposite(): return lax.ppermute(block, (SEC, TEN), route)]
    unnamed x139 -> x132, local copies, waits for them, and re-layouts: 28.7 us -> 23.6 us
  transfers between devices with their start and end apart: 27 -> 13, of which waited for: 12 -> 5; matrix products, arithmetic and copies ran while one was open for 9% -> 6% of each run, Pallas kernels for 22% -> 53%
where the time goes in v2:
time: 787 us; the launch traced here: 784 us
  Pallas kernels  597 us (76%)
  waiting for transfers between devices  65.3 us (8%)
  other arithmetic  45.8 us (6%)
  local copies, waits for them, and re-layouts  36.7 us (5%)
  between operations  14.9 us (2%)
  starting transfers between devices  11.8 us (1%)
  matrix products  11.8 us (1%)
    pallas_call x8, Pallas kernels, team_call(): pl.pallas_call(kernel, in_specs=[vmem] * len(operands), out_specs=[vmem]...  417 us
    pallas_call x1, Pallas kernels, finish(): pl.pallas_call(functools.partial(finish_kernel, groups), in_specs=[vmem]...  148 us
    ppermute x4, waiting for transfers between devices, across(): return lax.ppermute(block, (SEC, TEN), route)  60.3 us
    unnamed x132, local copies, waits for them, and re-layouts  23.6 us
    pallas_call x2, Pallas kernels, attend_backward(): pl.pallas_call(attend_back_kernel, grid=(columns // width,), in_specs=[sp...  17.8 us
    select_n x7, other arithmetic, local(): jnp.where(at.first, b, a)  16.8 us
  transfers between devices with their start and end apart: 13, of which 5 were waited for; matrix products, arithmetic and copies ran while one was open for 6% of the time, Pallas kernels for 53%

profile of v2, /device:TPU:0, one launch (start us, length us, event | category | flops | bytes accessed | tf_op | source)
XLA Modules:
  0.0 783.5 jit_solution(14472964188444163289)
XLA Ops:
  12.3 3.5 collective-permute-start.1
  15.8 14.5 %collective-permute-done.1 = bf16[640,256]{1,0:T(8,128)(2,1)S(1)} collective-permute-done((bf16[640,256]{1,0:T(8,128)(2,1)S(1)}, bf16[640,256]{1,0:T(8,128)(2,1)S(1)}, u32[]{:S(2)}, u32[]{:S(2)}) %collective-permute-start.1) | collective-permute-done | bytes 327712 | tf_op jit(solution)/shard_map/ppermute | solution.py:175
  32.3 18.5 %collective-permute-done.5 = bf16[176,1024]{1,0:T(8,128)(2,1)S(1)} collective-permute-done((bf16[176,1024]{1,0:T(8,128)(2,1)S(1)}, bf16[176,1024]{1,0:T(8,128)(2,1)S(1)}, u32[]{:S(2)}, u32[]{:S(2)}) %collective-permute-start.5) | collective-permute-done | bytes 360480 | tf_op jit(solution)/shard_map/ppermute | solution.py:175
  52.6 20.2 %collective-permute-done.3 = bf16[256,704]{1,0:T(8,128)(2,1)S(1)} collective-permute-done((bf16[256,704]{1,0:T(8,128)(2,1)}, bf16[256,704]{1,0:T(8,128)(2,1)S(1)}, u32[]{:S(2)}, u32[]{:S(2)}) %collective-permute-start.3) | collective-permute-done | bytes 360480 | tf_op jit(solution)/shard_map/ppermute | solution.py:175
  89.6 7.2 collective-permute-done.4
  105.4 7.3 shard_map.211
  114.9 33.1 %shard_map.212 = (f32[4,128,1024]{2,1,0:T(8,128)}, bf16[4,2,128,1024]{3,2,1,0:T(8,128)(2,1)}) custom-call(bf16[1024,256]{1,0:T(8,128)(2,1)} %copy-done.10, bf16[256,1024]{1,0:T(8,128)(2,1)} %get-tuple-element.179.w_out, bf16[4,2,128,1024]{3,2,1,0:T(8,128)(2,1)} %bitcast.162, f32[1,1024]{1,0:T(1,128)} %get-tuple-element.181.gain), custom_call_target="tpu_custom_call" | custom-call | flops 30000001024 | bytes 4194304 | tf_op jit(solution)/shard_map/pallas_call | solution.py:710
  148.1 3.5 bitcast_select_fusion.4
  151.6 3.4 bitcast_select_fusion.2
  155.0 4.9 all-gather.9.cloned.1.call-done
  163.2 37.2 %shard_map.213 = (f32[1024,704]{1,0:T(8,128)}, f32[1024,704]{1,0:T(8,128)}, bf16[1024,704]{1,0:T(8,128)(2,1)}, bf16[4,2,128,1024]{3,2,1,0:T(8,128)(2,1)}) custom-call(bf16[1024,1024]{1,0:T(8,128)(2,1)} %bitcast.190, bf16[1024,704]{1,0:T(8,128)(2,1)} %get-tuple-element.157.w_gate, bf16[1024,704]{1,0:T(8,128)(2,1)} %get-tuple-element.155.w_up, ...), custom_call_target="tpu_custom_call" | custom-call | flops 30000001024 | bytes 4194304 | tf_op jit(solution)/shard_map/pallas_call | solution.py:710
  205.8 4.7 collective-permute-start.6
  211.2 7.3 shard_map.214
  219.2 54.3 %shard_map.215 = (f32[4,128,1024]{2,1,0:T(8,128)}, bf16[4,2,128,1024]{3,2,1,0:T(8,128)(2,1)}) custom-call(bf16[1024,256]{1,0:T(8,128)(2,1)} %copy-done.12, bf16[256,1024]{1,0:T(8,128)(2,1)} %get-tuple-element.178.w_out, bf16[4,2,128,1024]{3,2,1,0:T(8,128)(2,1)} %get-tuple-element.77.source, f32[1,1024]{1,0:T(1,128)} %get-tuple-element.180.gain), custom_call_target="tpu_custom_call" | custom-call | flops 30000001024 | bytes 4194304 | tf_op jit(solution)/shard_map/pallas_call | solution.py:710
  273.5 37.4 %shard_map.216 = (f32[1024,704]{1,0:T(8,128)}, f32[1024,704]{1,0:T(8,128)}, bf16[1024,704]{1,0:T(8,128)(2,1)}, bf16[4,2,128,1024]{3,2,1,0:T(8,128)(2,1)}) custom-call(bf16[1024,1024]{1,0:T(8,128)(2,1)} %bitcast.196, bf16[1024,704]{1,0:T(8,128)(2,1)} %get-tuple-element.156.w_gate, bf16[1024,704]{1,0:T(8,128)(2,1)} %get-tuple-element.154.w_up, ...), custom_call_target="tpu_custom_call" | custom-call | flops 30000001024 | bytes 4194304 | tf_op jit(solution)/shard_map/pallas_call | solution.py:710
  312.9 64.7 %shard_map.217 = (f32[4,128,1024]{2,1,0:T(8,128)}, bf16[4,2,128,1024]{3,2,1,0:T(8,128)(2,1)}, f32[1,1024]{1,0:T(1,128)}, bf16[1024,704]{1,0:T(8,128)(2,1)}, bf16...) custom-call(bf16[4,2,128,1024]{3,2,1,0:T(8,128)(2,1)} %bitcast.173, bf16[1024,704]{1,0:T(8,128)(2,1)} %get-tuple-element.156.w_gate, ...), custom_call_target="tpu_custom_call" | custom-call | flops 30000001024 | bytes 4194304 | tf_op jit(solution)/shard_map/pallas_call | solution.py:710
  380.8 8.9 %shard_map.218 = (bf16[1024,256]{1,0:T(8,128)(2,1)S(1)}, bf16[1024,256]{1,0:T(8,128)(2,1)S(1)}, bf16[1024,256]{1,0:T(8,128)(2,1)S(1)}) custom-call(bf16[1024,256]{1,0:T(8,128)(2,1)S(1)} %convolution_convert_fusion.7.q_ref, bf16[1024,256]{1,0:T(8,128)(2,1)S(1)} %convolution_convert_fusion.1.k_ref, bf16[1024,256]{1,0:T(8,128)(2,1)S(1)} %convolution_convert_fusion.v_ref, ...), custom_call_target="tpu_custom_call" | custom-call | flops 5368709120 | bytes 4194304 | tf_op jit(solution)/shard_map/pallas_call | solution.py:136
  391.2 62.2 %shard_map.219 = (bf16[4,2,128,1024]{3,2,1,0:T(8,128)(2,1)}, f32[1,1024]{1,0:T(1,128)}, bf16[2560,256]{1,0:T(8,128)(2,1)}, bf16[1024,256]{1,0:T(8,128)(2,1)}, bf...) custom-call(bf16[1024,256]{1,0:T(8,128)(2,1)} %copy-done.15, ...), custom_call_target="tpu_custom_call" | custom-call | flops 30000001024 | bytes 4194304 | tf_op jit(solution)/shard_map/pallas_call | solution.py:710
  456.9 66.7 %shard_map.220 = (f32[4,128,1024]{2,1,0:T(8,128)}, bf16[4,2,128,1024]{3,2,1,0:T(8,128)(2,1)}, f32[1,1024]{1,0:T(1,128)}, bf16[1024,704]{1,0:T(8,128)(2,1)}, bf16...) custom-call(bf16[4,2,128,1024]{3,2,1,0:T(8,128)(2,1)} %get-tuple-element, ...), custom_call_target="tpu_custom_call" | custom-call | flops 30000001024 | bytes 4194304 | tf_op jit(solution)/shard_map/pallas_call | solution.py:710
  526.2 8.9 %shard_map.221 = (bf16[1024,256]{1,0:T(8,128)(2,1)S(1)}, bf16[1024,256]{1,0:T(8,128)(2,1)S(1)}, bf16[1024,256]{1,0:T(8,128)(2,1)S(1)}) custom-call(bf16[1024,256]{1,0:T(8,128)(2,1)S(1)} %copy-done.9, bf16[1024,256]{1,0:T(8,128)(2,1)S(1)} %copy-done.3, bf16[1024,256]{1,0:T(8,128)(2,1)S(1)} %copy-done.1, bf16[1024,256]{1,0:T(8,128)(2,1)S(1)} %copy-done.11, ...), custom_call_target="tpu_custom_call" | custom-call | flops 5368709120 | bytes 4194304 | tf_op jit(solution)/shard_map/pallas_call | solution.py:136
  536.6 61.7 %shard_map.222 = (bf16[4,2,128,1024]{3,2,1,0:T(8,128)(2,1)}, f32[1,1024]{1,0:T(1,128)}, bf16[2560,256]{1,0:T(8,128)(2,1)}, bf16[1024,256]{1,0:T(8,128)(2,1)}, bf...) custom-call(bf16[1024,256]{1,0:T(8,128)(2,1)} %copy-done.14, ...), custom_call_target="tpu_custom_call" | custom-call | flops 30000001024 | bytes 4194304 | tf_op jit(solution)/shard_map/pallas_call | solution.py:710
  601.0 147.6 %shard_map.223 = (bf16[4,256,704]{2,1,0:T(8,128)(2,1)}, bf16[4,256,704]{2,1,0:T(8,128)(2,1)}, bf16[4,176,1024]{2,1,0:T(8,128)(2,1)}, bf16[4,640,256]{2,1,0:T(8,1...) custom-call(bf16[256,704]{1,0:T(8,128)(2,1)} %get-tuple-element.116.refs_0_, ...), custom_call_target="tpu_custom_call" | custom-call | tf_op jit(solution)/shard_map/pallas_call | solution.py:823
  762.6 3.6 copy.34
  766.2 4.5 broadcast_select_fusion.5
  (214 shorter events, 83.0 us)
Async XLA Ops:
  7.2 93.2 %all-gather.5.cloned.1.call-start = ((), (), s32[]{:S(2)}) async-start(), calls=%async_computation | async-start | bytes 1638400 | tf_op jit(solution)/shard_map/all_gather | solution.py:867
  7.2 44.3 %copy-start.25 = (bf16[1,1024,704]{1,2,0:T(8,128)(2,1)S(1)}, bf16[1,1024,704]{1,2,0:T(8,128)(2,1)}, u32[]{:S(2)}) copy-start(bf16[1,1024,704]{1,2,0:T(8,128)(2,1)} %param.19) | copy-start | bytes 4325380
  12.2 61.4 %copy-start.56 = (f32[1,1024]{1,0:T(1,128)S(1)}, f32[1,1024]{1,0:T(1,128)}, u32[]{:S(2)}) copy-start(f32[1,1024]{1,0:T(1,128)} %param.23) | copy-start | bytes 12292
  12.2 61.4 %copy-start.57 = (f32[1,1024]{1,0:T(1,128)S(1)}, f32[1,1024]{1,0:T(1,128)}, u32[]{:S(2)}) copy-start(f32[1,1024]{1,0:T(1,128)} %param.22) | copy-start | bytes 12292
  12.3 18.0 %collective-permute-start.1 = (bf16[640,256]{1,0:T(8,128)(2,1)S(1)}, bf16[640,256]{1,0:T(8,128)(2,1)S(1)}, u32[]{:S(2)}, u32[]{:S(2)}) collective-permute-start(bf16[640,256]{1,0:T(8,128)(2,1)S(1)} %constant_dynamic-slice_fusion.3), channel_id=1, source_target_pairs={{0,18},{1,19},{2,16},{3,17},{16,2},{17,3},{18,0},{19,1},{4,22},{5,... | collective-permute-start | bytes 983048 | tf_op jit(solution)/shard_map/ppermute | solution.py:175
  31.0 117.1 %all-gather.11.cloned.1.call-start = ((), (), s32[]{:S(2)}) async-start(), calls=%async_computation.3 | async-start | bytes 1802240 | tf_op jit(solution)/shard_map/all_gather | solution.py:867
  31.1 45.2 %copy-start.40 = (bf16[1,1024,512]{2,1,0:T(8,128)(2,1)S(1)}, bf16[1,1024,512]{2,1,0:T(8,128)(2,1)}, u32[]{:S(2)}) copy-start(bf16[1,1024,512]{2,1,0:T(8,128)(2,1)} %param.15) | copy-start | bytes 3145732
  32.2 18.6 %collective-permute-start.5 = (bf16[176,1024]{1,0:T(8,128)(2,1)S(1)}, bf16[176,1024]{1,0:T(8,128)(2,1)S(1)}, u32[]{:S(2)}, u32[]{:S(2)}) collective-permute-start(bf16[176,1024]{1,0:T(8,128)(2,1)S(1)} %dynamic-slice_bitcast_fusion.1), channel_id=1, source_target_pairs={{0,18},{1,19},{2,16},{3,17},{16,2},{17,3},{18,0},{19,1},{4,22},{5,... | collective-permute-start | bytes 1081352 | tf_op jit(solution)/shard_map/ppermute | solution.py:175
  51.5 100.1 %all-gather.7.cloned.1.call-start = ((), (), s32[]{:S(2)}) async-start(), calls=%async_computation.1 | async-start | bytes 1966080 | tf_op jit(solution)/shard_map/all_gather | solution.py:867
  52.6 20.2 %collective-permute-start.3 = (bf16[256,704]{1,0:T(8,128)(2,1)}, bf16[256,704]{1,0:T(8,128)(2,1)S(1)}, u32[]{:S(2)}, u32[]{:S(2)}) collective-permute-start(bf16[256,704]{1,0:T(8,128)(2,1)} %bitcast.182), channel_id=1, source_target_pairs={{0,18},{1,19},{2,16},{3,17},{16,2},{17,3},{18,0},{19,1},{4,22},{5,... | collective-permute-start | bytes 1081352 | tf_op jit(solution)/shard_map/ppermute | solution.py:175
  73.5 86.4 %all-gather.9.cloned.1.call-start = ((), (), s32[]{:S(2)}) async-start(), calls=%async_computation.2 | async-start | bytes 1966080 | tf_op jit(solution)/shard_map/all_gather | solution.py:867
  74.2 12.1 %collective-permute-start = (f32[2,1024]{1,0:T(2,128)}, f32[2,1024]{1,0:T(2,128)}, u32[]{:S(2)}, u32[]{:S(2)}) collective-permute-start(f32[2,1024]{1,0:T(2,128)} %pad_maximum_fusion.4), channel_id=1, source_target_pairs={{0,16},{16,0},{1,17},{17,1},{2,18},{18,2},{3,19},{19,3},{4,20},{20... | collective-permute-start | bytes 24584 | tf_op jit(solution)/shard_map/ppermute | solution.py:165
  76.2 20.5 %collective-permute-start.4 = (bf16[256,704]{1,0:T(8,128)(2,1)}, bf16[256,704]{1,0:T(8,128)(2,1)}, u32[]{:S(2)}, u32[]{:S(2)}) collective-permute-start(bf16[256,704]{1,0:T(8,128)(2,1)} %bitcast.12), channel_id=1, source_target_pairs={{0,18},{1,19},{2,16},{3,17},{16,2},{17,3},{18,0},{19,1},{4,22},{5,... | collective-permute-start | bytes 1081352 | tf_op jit(solution)/shard_map/ppermute | solution.py:175
  77.1 19.7 %collective-permute-start.2 = (bf16[1024,256]{1,0:T(8,128)(2,1)}, bf16[1024,256]{1,0:T(8,128)(2,1)}, u32[]{:S(2)}, u32[]{:S(2)}) collective-permute-start(bf16[1024,256]{1,0:T(8,128)(2,1)} %dynamic-slice_bitcast_fusion), channel_id=1, source_target_pairs={{0,16},{16,0},{1,17},{17,1},{2,18},{18,2},{3,19},{19,3},{4,20},{20... | collective-permute-start | bytes 1572872 | tf_op jit(solution)/shard_map/ppermute | solution.py:165
  87.7 115.0 %copy-start.59 = (f32[1,1024]{1,0:T(1,128)}, f32[1,1024]{1,0:T(1,128)S(1)}, u32[]{:S(2)}) copy-start(f32[1,1024]{1,0:T(1,128)S(1)} %get-tuple-element.185.gain) | copy-start | bytes 12292
  205.8 107.1 %collective-permute-start.6 = (bf16[1024,1024]{1,0:T(8,128)(2,1)S(1)}, bf16[1024,1024]{1,0:T(8,128)(2,1)}, u32[]{:S(2)}, u32[]{:S(2)}) collective-permute-start(bf16[1024,1024]{1,0:T(8,128)(2,1)S(1)} %bitcast.160), channel_id=1, source_target_pairs={{0,2},{1,3},{2,0},{3,1},{4,6},{5,7},{6,4},{7,5},{8,10},{9,11},{10,... | collective-permute-start | bytes 6291464 | tf_op jit(solution)/shard_map/ppermute | solution.py:170
  310.9 145.1 %collective-permute-start.7 = (bf16[1024,1024]{1,0:T(8,128)(2,1)}, bf16[1024,1024]{1,0:T(8,128)(2,1)}, u32[]{:S(2)}, u32[]{:S(2)}) collective-permute-start(bf16[1024,1024]{1,0:T(8,128)(2,1)} %bitcast.165), channel_id=1, source_target_pairs={{16,18},{17,19},{18,16},{19,17},{20,22},{21,23},{22,20},{23,21},{2... | collective-permute-start | bytes 6291464 | tf_op jit(solution)/shard_map/ppermute | solution.py:170
  312.9 65.4 %copy-start.30 = (bf16[1,256,1024]{2,1,0:T(8,128)(2,1)S(1)}, bf16[1,256,1024]{2,1,0:T(8,128)(2,1)}, u32[]{:S(2)}) copy-start(bf16[1,256,1024]{2,1,0:T(8,128)(2,1)} %param.18) | copy-start | bytes 1572868
  312.9 65.4 %copy-start.52 = (bf16[1,256,256]{2,1,0:T(8,128)(2,1)S(1)}, bf16[1,256,256]{2,1,0:T(8,128)(2,1)}, u32[]{:S(2)}) copy-start(bf16[1,256,256]{2,1,0:T(8,128)(2,1)} %get-tuple-element.170) | copy-start | bytes 393220
  312.9 65.4 %copy-start.53 = (bf16[1,256,256]{2,1,0:T(8,128)(2,1)S(1)}, bf16[1,256,256]{2,1,0:T(8,128)(2,1)}, u32[]{:S(2)}) copy-start(bf16[1,256,256]{2,1,0:T(8,128)(2,1)} %get-tuple-element.171) | copy-start | bytes 393220
  312.9 65.4 %copy-start.54 = (bf16[1,256,256]{2,1,0:T(8,128)(2,1)S(1)}, bf16[1,256,256]{2,1,0:T(8,128)(2,1)}, u32[]{:S(2)}) copy-start(bf16[1,256,256]{2,1,0:T(8,128)(2,1)} %get-tuple-element.172) | copy-start | bytes 393220
  312.9 65.4 %copy-start.55 = (bf16[1,256,256]{2,1,0:T(8,128)(2,1)S(1)}, bf16[1,256,256]{2,1,0:T(8,128)(2,1)}, u32[]{:S(2)}) copy-start(bf16[1,256,256]{2,1,0:T(8,128)(2,1)} %get-tuple-element.173) | copy-start | bytes 393220
  455.2 145.8 %collective-permute-start.8 = (bf16[1024,1024]{1,0:T(8,128)(2,1)}, bf16[1024,1024]{1,0:T(8,128)(2,1)S(1)}, u32[]{:S(2)}, u32[]{:S(2)}) collective-permute-start(bf16[1024,1024]{1,0:T(8,128)(2,1)} %bitcast.166), channel_id=1, source_target_pairs={{16,18},{17,19},{18,16},{19,17},{20,22},{21,23},{22,20},{23,21},{2... | collective-permute-start | bytes 6291464 | tf_op jit(solution)/shard_map/ppermute | solution.py:170
  601.0 147.6 %copy-start.27 = (bf16[1024,1024]{1,0:T(8,128)(2,1)}, bf16[1024,1024]{1,0:T(8,128)(2,1)S(1)}, u32[]{:S(2)}) copy-start(bf16[1024,1024]{1,0:T(8,128)(2,1)S(1)} %collective-permute-done.8) | copy-start | bytes 6291460
  (50 other events, 188.9 us)
Sparse Core Ops, SparseCore 0:
  31.1 31.3 all-gather.4
  64.4 29.8 all-gather.10
  96.2 30.9 all-gather.6
  128.9 30.9 all-gather.8

commit v3 on v1

v3 whole, which is shorter than its diff:
```python
import functools
import math

import jax
import jax.numpy as jnp
from jax import lax
from jax.experimental import pallas as pl
from jax.experimental.pallas import tpu as pltpu
from jax.sharding import PartitionSpec as P

QH = 16
HD = 64
KVH = 2
LH = 256
LEN = 1024
EPS = 1e-05
F32 = jnp.float32
BF16 = jnp.bfloat16
SEC, DP, TEN = "section", "dp", "tensor"
LOG2_SCALE = HD**-0.5 * math.log2(math.e)
KEY_ROWS = 256


def mm(left, right, left_dim=1, right_dim=0):
    dims = (((left_dim,), (right_dim,)), ((), ()))
    return lax.dot_general(left, right, dims, preferred_element_type=F32)


def head_masks(width):
    if width == HD:
        return [None]
    lane = lax.broadcasted_iota(jnp.int32, (1, width), 1)
    return [lane // HD == j for j in range(width // HD)]


def keep_head(block, mask):
    return block if mask is None else jnp.where(mask, block, jnp.zeros_like(block))


def attend_kernel(q_ref, k_ref, v_ref, o_ref, norm_ref):
    width = q_ref.shape[1]
    masks = head_masks(width)
    rows = KEY_ROWS
    place_k = lax.broadcasted_iota(jnp.int32, (rows, rows), 0)
    place_q = lax.broadcasted_iota(jnp.int32, (rows, rows), 1)
    for start in range(0, LEN, rows):
        query = q_ref[start : start + rows, :]
        total = None
        for j, mask in enumerate(masks):
            query_j = keep_head(query, mask)
            scores = mm(k_ref[start : start + rows, :], query_j, 1, 1) * LOG2_SCALE
            scores = jnp.where(place_k <= place_q, scores, -jnp.inf)
            largest = jnp.max(scores, axis=0, keepdims=True)
            if start:
                before = mm(k_ref[0:start, :], query_j, 1, 1) * LOG2_SCALE
                largest = jnp.maximum(largest, jnp.max(before, axis=0, keepdims=True))
            weight = jnp.exp2(scores - largest)
            norm = jnp.sum(weight, axis=0, keepdims=True)
            value = keep_head(v_ref[start : start + rows, :], mask)
            out = mm(value, weight.astype(BF16), 0, 0)
            if start:
                weight = jnp.exp2(before - largest)
                norm = norm + jnp.sum(weight, axis=0, keepdims=True)
                value = keep_head(v_ref[0:start, :], mask)
                out = out + mm(value, weight.astype(BF16), 0, 0)
            out = out / norm
            total = out if total is None else total + out
            norm_ref[0, j : j + 1, start : start + rows] = largest + jnp.log2(norm)
        o_ref[start : start + rows, :] = total.T.astype(BF16)


def attend_forward(queries, keys, values):
    rows, columns = queries.shape
    width = min(2 * HD, columns)
    heads = width // HD
    spec = pl.BlockSpec((rows, width), lambda i: (0, i))
    return pl.pallas_call(
        attend_kernel,
        grid=(columns // width,),
        in_specs=[spec] * 3,
        out_specs=[spec, pl.BlockSpec((1, heads, rows), lambda i: (i, 0, 0))],
        out_shape=[
            jax.ShapeDtypeStruct((rows, columns), BF16),
            jax.ShapeDtypeStruct((columns // width, heads, rows), F32),
        ],
        compiler_params=pltpu.CompilerParams(vmem_limit_bytes=40 * 2**20),
        cost_estimate=pl.CostEstimate(
            flops=rows * rows * columns * 8, bytes_accessed=rows * columns * 8, transcendentals=0
        ),
    )(queries, keys, values)


def attend_back_kernel(q_ref, k_ref, v_ref, o_ref, g_ref, norm_ref, dq_ref, dk_ref, dv_ref, acc):
    width = q_ref.shape[1]
    masks = head_masks(width)
    rows = KEY_ROWS
    place_k = lax.broadcasted_iota(jnp.int32, (rows, rows), 0)
    place_q = lax.broadcasted_iota(jnp.int32, (rows, rows), 1)
    product = g_ref[...].astype(F32) * o_ref[...].astype(F32)
    product = product.T
    acc[...] = jnp.zeros_like(acc)
    deltas = [
        jnp.sum(product[j * HD : (j + 1) * HD, :], axis=0, keepdims=True)
        for j in range(len(masks))
    ]
    for start in range(0, LEN, rows):
        end = start + rows
        key = k_ref[start:end, :]
        value = v_ref[start:end, :]
        grad_key = grad_value = None
        for j, mask in enumerate(masks):
            query_j = keep_head(q_ref[start:, :], mask)
            grad_j = keep_head(g_ref[start:, :], mask)
            scores = mm(key, query_j, 1, 1) * LOG2_SCALE
            probs = jnp.exp2(scores - norm_ref[0, j : j + 1, start:])
            first = jnp.where(place_k <= place_q, probs[:, :rows], 0.0)
            probs = first if end == LEN else jnp.concatenate([first, probs[:, rows:]], axis=1)
            grad_probs = mm(value, grad_j, 1, 1)
            grad_scores = (probs * (grad_probs - deltas[j][:, start:])).astype(BF16)
            value_term = mm(probs.astype(BF16), grad_j)
            key_term = mm(grad_scores, query_j)
            grad_key = key_term if grad_key is None else grad_key + key_term
            grad_value = value_term if grad_value is None else grad_value + value_term
            acc[:, start:] += mm(keep_head(key, mask), grad_scores, 0, 0)
        dk_ref[start:end, :] = (grad_key * HD**-0.5).astype(BF16)
        dv_ref[start:end, :] = grad_value.astype(BF16)
    dq_ref[...] = (acc[...].T * HD**-0.5).astype(BF16)


def attend_backward(queries, keys, values, heads_out, grad_heads, norms):
    rows, columns = queries.shape
    width = min(2 * HD, columns)
    heads = width // HD
    spec = pl.BlockSpec((rows, width), lambda i: (0, i))
    shape = jax.ShapeDtypeStruct((rows, columns), BF16)
    return pl.pallas_call(
        attend_back_kernel,
        grid=(columns // width,),
        in_specs=[spec] * 5 + [pl.BlockSpec((1, heads, rows), lambda i: (i, 0, 0))],
        out_specs=[spec] * 3,
        out_shape=[shape] * 3,
        scratch_shapes=[pltpu.VMEM((width, rows), F32)],
        compiler_params=pltpu.CompilerParams(vmem_limit_bytes=40 * 2**20),
        cost_estimate=pl.CostEstimate(
            flops=rows * rows * columns * 20, bytes_accessed=rows * columns * 16, transcendentals=0
        ),
    )(queries, keys, values, heads_out, grad_heads, norms)


def rms_scale(features):
    return features * lax.rsqrt(jnp.mean(features * features, axis=-1, keepdims=True) + EPS)


class Place:
    def __init__(self):
        self.count = lax.axis_size(TEN)
        self.team = self.count // 2
        self.z = lax.axis_index(TEN)
        self.core = lax.axis_index(SEC)
        self.dp = lax.axis_index(DP)
        self.sequence = self.z // self.team
        self.first = self.core == 0

    def opposite(self, block, cores=(0, 1)):
        n, t = self.count, self.team
        route = [(core * n + z, core * n + (z + t) % n) for core in cores for z in range(n)]
        return lax.ppermute(block, (SEC, TEN), route)

    def across(self, block, core):
        n, t = self.count, self.team
        route = [(core * n + z, (1 - core) * n + (z + t) % n) for z in range(n)]
        return lax.ppermute(block, (SEC, TEN), route)


def pack_columns(matrix, width):
    return [matrix[:, i : i + width] for i in range(0, matrix.shape[1], width)]


def pack_attention(query, key_up, value_up, out):
    width = query.shape[1]
    return jnp.concatenate([query, key_up, value_up] + pack_columns(out, width), axis=0)


def unpack_attention(packed, model):
    width = packed.shape[1]
    query = packed[:model]
    key_up = packed[model : model + LH]
    value_up = packed[model + LH : model + 2 * LH]
    rest = packed[model + 2 * LH :]
    out = jnp.concatenate([rest[i : i + width] for i in range(0, rest.shape[0], width)], axis=1)
    return query, key_up, value_up, out


def by_dp(matrix):
    count = lax.axis_size(DP)
    return matrix.reshape(count, matrix.shape[0] // count, matrix.shape[1])


def whole_of(pieces):
    return pieces.reshape(-1, pieces.shape[2])


MESH = pl.DeviceIdType.MESH
PIECES = 4
VMEM_LIMIT = 58 * 2**20
LINK_FLOPS = 30 * 10**9
GAIN_ROWS = 16
DMA = pltpu.SemaphoreType.DMA


def reciprocal_rms(features):
    return lax.rsqrt(jnp.mean(features * features, axis=-1, keepdims=True) + EPS)


def send_to(source, target, sent, here, device):
    return pltpu.make_async_remote_copy(
        src_ref=source,
        dst_ref=target,
        send_sem=sent,
        recv_sem=here,
        device_id=device,
        device_id_type=MESH,
    )


def greet(partners):
    barrier = pltpu.get_barrier_semaphore()
    for partner in partners:
        pl.semaphore_signal(barrier, inc=1, device_id=partner, device_id_type=MESH)
    pl.semaphore_wait(barrier, len(partners))


class Team:
    def __init__(self):
        count = lax.axis_size(TEN)
        self.size = count // 2
        self.core = lax.axis_index(SEC)
        z = lax.axis_index(TEN)
        self.place = lax.rem(z, self.size)
        self.base = z - self.place
        self.other = {SEC: 1 - self.core}

    def peer(self, step):
        place = lax.rem(self.place + step, self.size)
        return place, {TEN: self.base + place}

    def partners(self):
        return [self.other] + [self.peer(step)[1] for step in range(1, self.size)]


class Plane:
    def __init__(self):
        me = lax.axis_index(DP)
        self.me = me
        self.one = me + 1 - 2 * lax.rem(me, 2)
        self.two = lax.rem(me + 2, 4)
        self.both = lax.rem(self.one + 2, 4)

    def partners(self):
        return [{DP: self.one}, {DP: self.two}]

    def order(self, turn):
        return (self.one, self.two) if turn % 2 == 0 else (self.two, self.one)


def scatter_scratch(load):
    return [
        pltpu.VMEM((3,) + load.shape[1:], BF16),
        pltpu.VMEM(load.shape[1:], BF16),
        DMA((3,)),
        DMA((3,)),
    ]


class Scatter:
    def __init__(self, plane, turn, load, slots, part, sent, here):
        self.load, self.slots, self.part = load, slots, part
        self.me, self.both = plane.me, plane.both
        self.near, self.far = plane.order(turn)
        self.copies = [
            send_to(load.at[self.near], slots.at[0], sent.at[0], here.at[0], {DP: self.near}),
            send_to(load.at[self.both], slots.at[1], sent.at[1], here.at[1], {DP: self.near}),
            send_to(part, slots.at[2], sent.at[2], here.at[2], {DP: self.far}),
        ]

    def start(self):
        self.copies[1].start()
        self.copies[0].start()

    def middle(self):
        self.copies[1].wait_recv()
        self.part[...] = (self.load[self.far].astype(F32) + self.slots[1].astype(F32)).astype(BF16)
        self.copies[2].start()

    def total(self):
        self.copies[0].wait_recv()
        total = self.load[self.me].astype(F32) + self.slots[0].astype(F32)
        self.copies[2].wait_recv()
        return total + self.slots[2].astype(F32)

    def drain(self):
        for copy in self.copies:
            copy.wait_send()


class Gather:
    def __init__(self, plane, turn, whole, sent, here, active=None):
        self.whole, self.me, self.both, self.active = whole, plane.me, plane.both, active
        self.near, self.far = plane.order(turn)

        def copy(k, piece, device):
            at = whole.at[piece]
            return send_to(at, at, sent.at[k], here.at[piece], {DP: device})

        self.first = copy(0, self.me, self.near)
        self.second = [copy(1, self.me, self.far), copy(2, self.near, self.far)]
        self.coming = [copy(0, piece, self.near) for piece in (self.near, self.far, self.both)]

    def when(self, body):
        if self.active is None:
            body()
        else:
            pl.when(self.active)(body)

    def start(self, piece):
        def body():
            self.whole[self.me] = piece[...]
            self.first.start()
            self.second[0].start()

        self.when(body)

    def middle(self):
        def body():
            self.coming[0].wait_recv()
            self.second[1].start()

        self.when(body)

    def finish(self):
        def body():
            self.coming[1].wait_recv()
            self.coming[2].wait_recv()
            for copy in [self.first] + self.second:
                copy.wait_send()

        self.when(body)


def exchange_scratch(rows, model):
    team = lax.axis_size(TEN) // 2
    half = rows // PIECES // 2
    return [
        pltpu.VMEM((2, half, model), F32),
        pltpu.VMEM((PIECES, half, model), F32),
        pltpu.VMEM((PIECES, half, model), BF16),
        pltpu.VMEM((PIECES, half, model), BF16),
        pltpu.VMEM((team, PIECES, half, model), BF16),
        DMA((PIECES,)),
        DMA((PIECES,)),
        DMA((team, PIECES)),
        DMA((team, PIECES)),
        DMA((PIECES,)),
        DMA((PIECES,)),
    ]


EXCHANGE = 11


class Exchange:
    def __init__(self, team, refs):
        self.team = team
        (self.part, self.keep, self.out, self.got, self.far) = refs[:5]
        (self.core_sent, self.core_here, self.far_sent, self.far_here) = refs[5:9]
        (self.join_sent, self.join_here) = refs[9:]

    def core_copy(self, i):
        return send_to(
            self.out.at[i], self.got.at[i], self.core_sent.at[i], self.core_here.at[i], self.team.other
        )

    def far_copy(self, i, step, place):
        at = self.far.at[place, i]
        return send_to(
            at, at, self.far_sent.at[step, i], self.far_here.at[place, i], self.team.peer(step)[1]
        )

    def join_copy(self, i, whole):
        at = whole.at[i, self.team.core]
        return send_to(at, at, self.join_sent.at[i], self.join_here.at[i], self.team.other)

    def push(self, i, product):
        core = self.team.core
        self.part[...] = product.reshape(self.part.shape)
        self.out[i] = self.part[1 - core].astype(BF16)
        self.core_copy(i).start()
        self.keep[i] = self.part[core]

    def combine(self, i):
        self.core_copy(i).wait_recv()
        self.far[self.team.place, i] = (self.keep[i] + self.got[i].astype(F32)).astype(BF16)
        for step in range(1, self.team.size):
            self.far_copy(i, step, self.team.place).start()

    def send_all(self, product):
        def send(i):
            self.push(i, product(i))

            @pl.when(i > 0)
            def _():
                self.combine(i - 1)

        each_piece(send)
        self.combine(PIECES - 1)

    def total(self, i):
        for step in range(1, self.team.size):
            self.far_copy(i, step, self.team.peer(step)[0]).wait_recv()
        total = self.far[0, i].astype(F32)
        for place in range(1, self.team.size):
            total = total + self.far[place, i].astype(F32)
        return total

    def join(self, i, whole, half):
        whole[i, self.team.core] = half
        self.join_copy(i, whole).start()

    def finish(self, whole):
        def drain(i):
            self.core_copy(i).wait_send()
            for step in range(1, self.team.size):
                self.far_copy(i, step, self.team.place).wait_send()
            self.join_copy(i, whole).wait()

        each_piece(drain)


def each_piece(body):
    lax.fori_loop(0, PIECES, lambda i, _: (body(i), 0)[1], 0)


def piece_rows(i, rows):
    size = rows // PIECES
    return pl.ds(pl.multiple_of(i * size, size), size)


class Weights:
    def __init__(self, layer, refs, held, sems):
        self.held = held
        self.copies = []
        mine = lax.axis_index(SEC) == layer
        for k in range(3):
            own, far = (pltpu.make_async_copy(refs[3 * s + k], held[k], sems.at[k]) for s in range(2))
            pl.when(mine)(own.start)
            pl.when(jnp.logical_not(mine))(far.start)
            self.copies.append(own)

    def wait(self):
        for copy in self.copies:
            copy.wait()


def weights_scratch(own):
    return [pltpu.VMEM(matrix.shape, BF16) for matrix in own] + [DMA((3,))]


def team_kernel(body, counts, core, *refs):
    inner, loads, pieces, outs, scratch = counts

    def take(count):
        nonlocal refs
        taken, refs = refs[:count], refs[count:]
        return taken

    inner, loads, pieces = take(inner), take(loads), take(pieces)
    outs, sums, wholes = take(outs), take(len(loads)), take(len(pieces))
    scratch = take(scratch)
    team = Team()
    plane = Plane()
    scatters = [Scatter(plane, k, load, *take(4)) for k, load in enumerate(loads)]
    active = lax.axis_index(SEC) == core
    gathers = [Gather(plane, k, whole, *take(2), active) for k, whole in enumerate(wholes)]
    ex = Exchange(team, refs)
    greet(team.partners() + (plane.partners() if loads or pieces else []))
    for scatter in scatters:
        scatter.start()
    for gather, piece in zip(gathers, pieces):
        gather.start(piece)

    def middle():
        for item in gathers + scatters:
            item.middle()

    body(ex, middle, *inner, *outs, *scratch)
    for scatter, total in zip(scatters, sums):
        total[...] = scatter.total().astype(BF16)
        scatter.drain()
    for gather in gathers:
        gather.finish()


def team_call(body, number, model, outs, operands, scratch=(), loads=(), pieces=(), core=0, far=0):
    vmem = pl.BlockSpec(memory_space=pltpu.VMEM)
    dp = lax.axis_size(DP)
    counts = (len(operands), len(loads), len(pieces), len(outs), len(scratch))
    outs = outs + [(load.shape[1:], BF16) for load in loads]
    outs = outs + [((dp,) + piece.shape, BF16) for piece in pieces]
    beside = [item for load in loads for item in scatter_scratch(load)]
    beside = beside + [DMA((3,)), DMA((dp,))] * len(pieces)
    specs = [vmem] * (len(operands) - far) + [pl.BlockSpec(memory_space=pl.ANY)] * far
    return pl.pallas_call(
        functools.partial(team_kernel, body, counts, core),
        in_specs=specs + [vmem] * (len(loads) + len(pieces)),
        out_specs=[vmem] * len(outs),
        out_shape=[jax.ShapeDtypeStruct(*out) for out in outs],
        scratch_shapes=list(scratch) + beside + exchange_scratch(LEN, model),
        compiler_params=pltpu.CompilerParams(
            collective_id=number, has_side_effects=True, vmem_limit_bytes=VMEM_LIMIT
        ),
        cost_estimate=pl.CostEstimate(flops=LINK_FLOPS, bytes_accessed=2**22, transcendentals=0),
    )(*operands, *loads, *pieces)


def project_out(ex, middle, heads, w_out, source, gain, residual, mlp_in):
    rows = heads.shape[0]
    ex.send_all(lambda i: mm(heads[piece_rows(i, rows), :], w_out[...]))
    middle()

    def receive(i):
        block = source[i, ex.team.core].astype(F32) + ex.total(i)
        residual[i] = block
        ex.join(i, mlp_in, (block * reciprocal_rms(block) * gain[...]).astype(BF16))

    each_piece(receive)
    ex.finish(mlp_in)


def feed_forward(layer, ex, middle, mlp_in, residual, *refs):
    weights = Weights(layer, refs[:6], refs[10:13], refs[13])
    gate, up, hidden, output, w_gate, w_up, w_down = refs[6:13]
    rows = mlp_in.shape[0]
    weights.wait()

    def product(i):
        at = piece_rows(i, rows)
        block = mlp_in[at, :]
        gate_block = mm(block, w_gate[...], 1, 1)
        up_block = mm(block, w_up[...], 1, 1)
        hidden_block = (jax.nn.silu(gate_block) * up_block).astype(BF16)
        gate[at, :] = gate_block
        up[at, :] = up_block
        hidden[at, :] = hidden_block
        return mm(hidden_block, w_down[...])

    ex.send_all(product)
    middle()
    each_piece(lambda i: ex.join(i, output, (residual[i] + ex.total(i)).astype(BF16)))
    ex.finish(output)


def rms_back(block, gain, upstream):
    inverse = reciprocal_rms(block)
    normed = block * inverse
    scaled = upstream * gain
    grad = inverse * (scaled - normed * jnp.mean(scaled * normed, axis=-1, keepdims=True))
    return grad, jnp.sum(upstream * normed, axis=0, keepdims=True)


def feed_back(layer, ex, middle, upstream, gate, up, hidden, mlp_in, residual, gain, *refs):
    weights = Weights(layer, refs[:6], refs[14:17], refs[17])
    d_residual, res_grad, gain_grad, g_gate, g_up, g_down = refs[6:12]
    d_gate, d_up, w_gate, w_up, w_down = refs[12:17]
    rows, model = mlp_in.shape
    shape = (rows // PIECES, model)
    weights.wait()

    def product(i):
        at = piece_rows(i, rows)
        grad_hidden = mm(upstream[i].reshape(shape), w_down[...], 1, 1)
        gate_block = gate[at, :]
        sigmoid = jax.nn.sigmoid(gate_block)
        silu = gate_block * sigmoid
        d_gate_block = grad_hidden * up[at, :] * (sigmoid + silu * (1.0 - sigmoid))
        d_gate[at, :] = d_gate_block.astype(BF16)
        d_up[at, :] = (grad_hidden * silu).astype(BF16)
        return mm(d_gate[at, :], w_gate[...]) + mm(d_up[at, :], w_up[...])

    ex.send_all(product)
    g_gate[...] = mm(d_gate[...], mlp_in[...], 0, 0).astype(BF16)
    g_up[...] = mm(d_up[...], mlp_in[...], 0, 0).astype(BF16)
    g_down[...] = mm(hidden[...], upstream[...].reshape(rows, model), 0, 0).astype(BF16)
    middle()
    gain_grad[...] = jnp.zeros_like(gain_grad)

    def receive(i):
        part, gain_part = rms_back(residual[i], gain[...], ex.total(i))
        block = upstream[i, ex.team.core].astype(F32) + part
        d_residual[i] = block
        gain_grad[...] += gain_part
        ex.join(i, res_grad, block.astype(BF16))

    each_piece(receive)
    ex.finish(res_grad)


def attend_in_back(
    ex, middle, d_queries, d_latents, w_query, w_latent, source, d_residual, gain, attn_in,
    heads_out, res_grad, latents, d_keys, d_values, input_grad, gain_grad, grads, g_latent
):
    rows = d_queries.shape[0]

    def product(i):
        at = piece_rows(i, rows)
        return mm(d_queries[at, :], w_query[...], 1, 1) + mm(d_latents[at, :], w_latent[...], 1, 1)

    ex.send_all(product)
    model, width = w_query.shape
    grads[0:model, :] = mm(attn_in[...], d_queries[...], 0, 0).astype(BF16)
    g_latent[...] = mm(attn_in[...], d_latents[...], 0, 0).astype(BF16)
    grads[model : model + LH, :] = mm(latents[...], d_keys[...], 0, 0).astype(BF16)
    grads[model + LH : model + 2 * LH, :] = mm(latents[...], d_values[...], 0, 0).astype(BF16)
    g_out = mm(heads_out[...], res_grad[...], 0, 0).astype(BF16)
    for j, block in enumerate(pack_columns(g_out, width)):
        start = model + 2 * LH + j * width
        grads[start : start + width, :] = block
    middle()
    gain_grad[...] = jnp.zeros_like(gain_grad)

    def receive(i):
        part, gain_part = rms_back(source[i, ex.team.core].astype(F32), gain[...], ex.total(i))
        gain_grad[...] += gain_part
        ex.join(i, input_grad, (d_residual[i] + part).astype(BF16))

    each_piece(receive)
    ex.finish(input_grad)


def fetch_kernel(packed, latent, gains, whole, far_latent, far_gains, sent, here, gather_sent, gather_here):
    plane = Plane()
    count = lax.axis_size(TEN)
    core = lax.axis_index(SEC)
    opposite = lax.rem(lax.axis_index(TEN) + count // 2, count)
    other, across = {SEC: 1 - core}, {SEC: 1 - core, TEN: opposite}
    greet(plane.partners() + [other, across])
    piece = send_to(packed.at[plane.me], whole.at[plane.me], sent.at[0], here.at[0], across)
    small = [
        send_to(latent, far_latent, sent.at[1], here.at[1], other),
        send_to(gains, far_gains, sent.at[2], here.at[2], other),
    ]
    pl.when(core == 0)(piece.start)
    for copy in small:
        copy.start()
    gather = Gather(plane, 0, whole, gather_sent, gather_here)

    @pl.when(core == 1)
    def _():
        piece.wait_recv()
        gather.first.start()
        gather.second[0].start()
        gather.middle()
        gather.finish()

    for copy in small:
        copy.wait()
    pl.when(core == 0)(piece.wait_send)


def fetch(packed, latent, gains):
    vmem = pl.BlockSpec(memory_space=pltpu.VMEM)
    shapes = [jax.ShapeDtypeStruct(x.shape, x.dtype) for x in (packed, latent, gains)]
    return pl.pallas_call(
        fetch_kernel,
        in_specs=[vmem] * 3,
        out_specs=[vmem] * 3,
        out_shape=shapes,
        scratch_shapes=[DMA((3,)), DMA((3,)), DMA((3,)), DMA((4,))],
        compiler_params=pltpu.CompilerParams(
            collective_id=8, has_side_effects=True, vmem_limit_bytes=16 * 2**20
        ),
        cost_estimate=pl.CostEstimate(flops=LINK_FLOPS // 2, bytes_accessed=2**21, transcendentals=0),
    )(packed, latent, gains)


def finish_kernel(groups, *refs):
    feed, late, done, grad = refs[:3], refs[3:5], refs[5:7], refs[7]
    outs, grad_far = refs[8:13], refs[13]
    refs = refs[14:]
    come, leave, slots, held = refs[:5], refs[5:7], refs[7], refs[8]
    cross_sent, cross_here, gather_sent, gather_here = refs[9:13]
    block_sent, block_here, grad_sent, grad_here = refs[13:17]
    plane = Plane()
    team = Team()
    scatters = [Scatter(plane, k, late[k], *refs[17 + 4 * k : 21 + 4 * k]) for k in range(2)]
    count = lax.axis_size(TEN)
    z = lax.axis_index(TEN)
    core = lax.axis_index(SEC)
    first, second = core == 0, core == 1
    opposite = lax.rem(z + count // 2, count)
    across = {SEC: 1 - core, TEN: opposite}
    chips = [lax.rem(z + step, count) for step in range(1, count)]
    greet(plane.partners() + [across] + [{TEN: chip} for chip in chips])
    for scatter in scatters:
        scatter.start()
    sources = list(feed) + list(leave)
    crosses = [
        send_to(sources[k], come[k], cross_sent.at[k], cross_here.at[k], across) for k in range(5)
    ]

    @pl.when(second)
    def _():
        for k in range(3):
            crosses[k].start()

    share = grad.at[team.place], grad_far.at[team.place]
    grad_copies = [send_to(*share, grad_sent.at[0], grad_here.at[team.place], {TEN: opposite})]
    grad_coming = []
    for step in range(1, team.size):
        place, peer = team.peer(step)
        grad_copies.append(send_to(share[1], share[1], grad_sent.at[step], grad_here.at[team.place], peer))
        theirs = grad_far.at[place]
        grad_coming.append(send_to(theirs, theirs, grad_sent.at[step], grad_here.at[place], peer))
    pl.when(first)(grad_copies[0].start)
    actives = [first] * 3 + [None] * 2
    gathers = [
        Gather(plane, k, outs[k], gather_sent.at[k], gather_here.at[k], actives[k]) for k in range(5)
    ]

    def spread(k, total):
        outs[k][plane.me] = total
        gathers[k].first.start()
        gathers[k].second[0].start()

    for scatter in scatters:
        scatter.middle()
    for k, scatter in enumerate(scatters):
        leave[k][...] = scatter.total().astype(BF16)
        pl.when(second)(crosses[3 + k].start)

    def arrive(k):
        crosses[k].wait_recv()
        return (sources[k][...].astype(F32) + come[k][...].astype(F32)).astype(BF16)

    @pl.when(first)
    def _():
        for k in range(3):
            spread(k, arrive(k))
        grad_copies[0].wait_recv()
        for copy in grad_copies[1:]:
            copy.start()
        spread(3, arrive(3))
        held[...] = arrive(4).reshape(held.shape)

    @pl.when(second)
    def _():
        spread(3, done[0][...])
        held[...] = done[1][...].reshape(held.shape)

    def block(step, chip, slot):
        return send_to(held.at[chip], slots.at[slot], block_sent.at[step], block_here.at[slot], {TEN: chip})

    for step, chip in enumerate(chips):
        block(step, chip, z).start()
    slots[z] = held[z]
    for gather in gathers[:4]:
        gather.middle()
    for step, chip in enumerate(chips):
        block(step, chip, chip).wait_recv()
    shares = [slots[shard].astype(F32) for shard in range(count)]
    sums = [sum(s for s, g in zip(shares, groups) if g == group) for group in range(KVH)]
    gain_rows = sums[0]
    for extra in sums[1:]:
        gain_rows = gain_rows + extra
    depth = gain_rows.shape[0] - GAIN_ROWS
    gain_rows = gain_rows * (2.0 / count)
    blocks = [jnp.concatenate([part[:depth], gain_rows[depth:]], axis=0) for part in sums]
    spread(4, jnp.concatenate(blocks, axis=1).astype(BF16))
    gathers[4].middle()
    for gather in gathers:
        gather.finish()
    for scatter in scatters:
        scatter.drain()
    for step, chip in enumerate(chips):
        block(step, chip, z).wait_send()

    @pl.when(second)
    def _():
        for copy in crosses:
            copy.wait_send()

    @pl.when(first)
    def _():
        for copy in grad_copies:
            copy.wait_send()
        for copy in grad_coming:
            copy.wait_recv()


def finish(groups, feed, late, done, grad):
    pieces, count = lax.axis_size(DP), lax.axis_size(TEN)
    vmem = pl.BlockSpec(memory_space=pltpu.VMEM)
    depth = done[1].shape[0] // count
    ours = list(feed) + list(done)
    outs = [(pieces,) + part.shape for part in ours[:4]] + [(pieces, depth, KVH * LH), grad.shape]
    blocks = pltpu.VMEM((count, depth, LH), BF16)
    return pl.pallas_call(
        functools.partial(finish_kernel, groups),
        in_specs=[vmem] * 8,
        out_specs=[vmem] * 6,
        out_shape=[jax.ShapeDtypeStruct(out, BF16) for out in outs],
        scratch_shapes=[pltpu.VMEM(part.shape, BF16) for part in ours + list(done)] + [blocks, blocks]
        + [DMA((5,)), DMA((5,)), DMA((5, 3)), DMA((5, pieces)), DMA((count,)), DMA((count,))]
        + [DMA((count // 2,)), DMA((count // 2,))]
        + scatter_scratch(late[0]) + scatter_scratch(late[1]),
        compiler_params=pltpu.CompilerParams(
            collective_id=9, has_side_effects=True, vmem_limit_bytes=VMEM_LIMIT
        ),
    )(*feed, *late, *done, grad)


def pieces_of(block):
    return block.reshape(PIECES, 2, block.shape[0] // PIECES // 2, block.shape[1])


def attend_layer(source, weights):
    w_query, w_key_up, w_value_up, w_out, w_latent, gain_attn, gain_mlp = weights
    attn_in = (rms_scale(source.astype(F32)) * gain_attn).astype(BF16)
    queries = mm(attn_in, w_query).astype(BF16)
    latents = mm(attn_in, w_latent).astype(BF16)
    keys = mm(latents, w_key_up).astype(BF16)
    values = mm(latents, w_value_up).astype(BF16)
    heads_out, norms = attend_forward(queries, keys, values)
    return source, attn_in, queries, latents, keys, values, heads_out, norms


def shapes_of(rows, model):
    return (PIECES, 2, rows // PIECES // 2, model), (PIECES, rows // PIECES // 2, model)


def project_layer(number, kept, weights, pieces=(), core=1):
    source, heads_out = kept[0], kept[6]
    rows, model = source.shape
    split, own = shapes_of(rows, model)
    residual, mlp_in, *wholes = team_call(
        project_out, number, model, [(own, F32), (split, BF16)],
        (heads_out, weights[3], pieces_of(source), weights[6][None]),
        pieces=pieces, core=core,
    )
    return residual, mlp_in.reshape(rows, model), [whole_of(w) for w in wholes]


def feed_layer(number, layer, residual, mlp_in, own, far, pieces=()):
    rows, model = mlp_in.shape
    wide = (rows, own[0].shape[0])
    gate, up, hidden, output, *wholes = team_call(
        functools.partial(feed_forward, layer), number, model,
        [(wide, F32), (wide, F32), (wide, BF16), (shapes_of(rows, model)[0], BF16)],
        (mlp_in, residual, *own, *far),
        scratch=weights_scratch(own), pieces=pieces, core=0, far=6,
    )
    return output.reshape(rows, model), (gate, up, hidden), [whole_of(w) for w in wholes]


def feed_layer_back(number, layer, upstream, feed_kept, residual, mlp_in, gain, own, far, loads=()):
    rows, model = upstream.shape
    split, half = shapes_of(rows, model)
    wide = pltpu.VMEM((rows, own[0].shape[0]), BF16)
    outs = [(half, F32), (split, BF16), ((1, model), F32)] + [(w.shape, BF16) for w in own]
    d_residual, res_grad, gain_grad, *grads = team_call(
        functools.partial(feed_back, layer), number, model, outs,
        (pieces_of(upstream), *feed_kept, mlp_in, residual, gain[None], *own, *far),
        scratch=[wide, wide] + weights_scratch(own), loads=loads, far=6,
    )
    res_grad = res_grad.reshape(rows, model)
    return d_residual, res_grad, gain_grad, [by_dp(g) for g in grads[:3]], grads[3:]


def latent_parts(g_latent, gain_attn, gain_mlp):
    count, pieces = lax.axis_size(TEN), lax.axis_size(DP)
    model = g_latent.shape[0]
    depth = model // count // pieces
    rows = g_latent.reshape(count, pieces, depth, LH).transpose(1, 0, 2, 3)
    gains = jnp.stack([gain_attn[0], gain_mlp[0]]).astype(BF16).reshape(2, count, model // count)
    gains = gains.transpose(1, 0, 2)
    gains = jnp.pad(gains, ((0, 0), (0, GAIN_ROWS - 2), (0, LH - model // count)))
    gains = jnp.pad(gains[None], ((0, pieces - 1), (0, 0), (0, 0), (0, 0)))
    return jnp.concatenate([rows, gains], axis=2).reshape(pieces, count * (depth + GAIN_ROWS), LH)


def attend_layer_back(number, kept, d_residual, res_grad, gain_mlp_grad, weights, loads=(), pieces=()):
    w_query, w_key_up, w_value_up, w_out, w_latent, gain_attn, gain_mlp = weights
    source, attn_in, queries, latents, keys, values, heads_out, norms = kept
    rows, model = source.shape
    d_heads = mm(res_grad, w_out, 1, 1).astype(BF16)
    d_queries, d_keys, d_values = attend_backward(queries, keys, values, heads_out, d_heads, norms)
    d_latents = (mm(d_keys, w_key_up, 1, 1) + mm(d_values, w_value_up, 1, 1)).astype(BF16)
    packed = (2 * model + 2 * LH, w_query.shape[1])
    input_grad, gain_grad, grads, g_latent, *rest = team_call(
        attend_in_back, number, model,
        [(shapes_of(rows, model)[0], BF16), ((1, model), F32), (packed, BF16), (w_latent.shape, BF16)],
        (d_queries, d_latents, w_query, w_latent, pieces_of(source), d_residual, gain_attn[None], attn_in,
         heads_out, res_grad, latents, d_keys, d_values),
        loads=loads, pieces=pieces, core=1,
    )
    parts = [by_dp(grads), latent_parts(g_latent, gain_grad, gain_mlp_grad)]
    sums, wholes = rest[: len(loads)], rest[len(loads) :]
    return input_grad.reshape(rows, model), parts, sums, [whole_of(w) for w in wholes]


def tie(*arrays):
    return lax.optimization_barrier(arrays)


def local(
    inputs,
    out_grad,
    w_query,
    w_latent,
    w_key_up,
    w_value_up,
    w_out,
    w_gate,
    w_up,
    w_down,
    norm_attn,
    norm_mlp,
):
    at = Place()
    model = inputs.shape[1]
    heads = w_query.shape[2] // HD

    def group_of(shard):
        return shard * heads // (QH // KVH)

    opposite_z = (at.z + at.team) % at.count

    def latent_of(shard):
        return lax.dynamic_slice_in_dim(w_latent[0], group_of(shard) * LH, LH, 1)

    def dp_piece(matrix):
        rows = matrix.shape[0] // lax.axis_size(DP)
        return lax.dynamic_slice_in_dim(matrix, at.dp * rows, rows, 0)

    def sequence_rows(block):
        return lax.dynamic_slice_in_dim(block, at.sequence * LEN, LEN, 0)

    own_feed = (w_gate[0].T, w_up[0].T, w_down[0])
    own_packed = pack_attention(w_query[0], w_key_up[0], w_value_up[0], w_out[0])
    own_gains = jnp.concatenate([norm_attn, norm_mlp], axis=0)
    own_latent = latent_of(at.z)
    feed_zero = [at.across(dp_piece(w), 0) for w in own_feed]
    packed_zero, far_latent, far_gains = fetch(by_dp(own_packed), latent_of(opposite_z), own_gains)

    def attention_weights(mine, far_packed):
        packed = jnp.where(mine, own_packed, far_packed)
        gains = jnp.where(mine, own_gains, far_gains)
        latent = jnp.where(mine, own_latent, far_latent)
        return unpack_attention(packed, model) + (latent, gains[0], gains[1])

    weights_zero = attention_weights(at.first, whole_of(packed_zero))
    kept_zero = attend_layer(sequence_rows(inputs), weights_zero)
    heads_out, own_packed, *feed_zero = tie(kept_zero[6], own_packed, *feed_zero)
    kept_zero = kept_zero[:6] + (heads_out,) + kept_zero[7:]
    packed_one = at.across(dp_piece(own_packed), 1)
    residual_zero, mlp_zero, far_zero = project_layer(0, kept_zero, weights_zero, feed_zero)
    residual_zero, packed_one, *late_feed = tie(residual_zero, packed_one, *own_feed)
    feed_one = [at.across(dp_piece(w), 1) for w in late_feed]
    first_out, feed_kept_zero, (packed_one,) = feed_layer(
        1, 0, residual_zero, mlp_zero, own_feed, far_zero, [packed_one]
    )

    weights_one = attention_weights(jnp.logical_not(at.first), packed_one)
    kept_one = attend_layer(first_out, weights_one)
    heads_out, *feed_one = tie(kept_one[6], *feed_one)
    kept_one = kept_one[:6] + (heads_out,) + kept_one[7:]
    residual_one, mlp_one, far_one = project_layer(2, kept_one, weights_one, feed_one, 0)
    second_out, feed_kept_one, _ = feed_layer(3, 1, residual_one, mlp_one, own_feed, far_one)

    d_residual, res_grad, mlp_gain, feed_one, _ = feed_layer_back(
        4, 1, sequence_rows(out_grad), feed_kept_one, residual_one, mlp_one, weights_one[6], own_feed, far_one
    )
    layer_mine, d_residual = tie(jnp.where(at.first, first_out, second_out), d_residual)
    layer_far = at.opposite(layer_mine)
    second_grad, late_one, feed_one, _ = attend_layer_back(
        5, kept_one, d_residual, res_grad, mlp_gain, weights_one, feed_one
    )
    feed_cross = [at.across(part, 0) for part in feed_one]
    upstream, layer_far = tie(second_grad, layer_far)
    d_residual, res_grad, mlp_gain, feed_zero, late_one = feed_layer_back(
        6, 0, upstream, feed_kept_zero, residual_zero, mlp_zero, weights_zero[6], own_feed, far_zero, late_one
    )
    d_residual, second_grad, *feed_cross = tie(d_residual, second_grad, *feed_cross)
    grad_far = at.opposite(second_grad, (1,))

    def total(mine, other):
        return (mine.astype(F32) + other.astype(F32)).astype(BF16)

    feed_one = [total(mine, other) for mine, other in zip(feed_one, feed_cross)]
    late_cross = [at.across(part, 0) for part in late_one]
    first_grad, late_zero, feed_zero, wide_one = attend_layer_back(
        7, kept_zero, d_residual, res_grad, mlp_gain, weights_zero, feed_zero, feed_one
    )
    first_grad, grad_far, *late_cross = tie(first_grad, grad_far, *late_cross)
    late_one = [total(mine, other) for mine, other in zip(late_one, late_cross)]
    groups = tuple(group_of(shard) for shard in range(at.count))
    shared = first_grad.reshape(at.team, first_grad.shape[0] // at.team, model)
    *wide_zero, packed, latent, first_grad_far = finish(groups, feed_zero, late_zero, late_one, shared)

    def both_sequences(mine, other):
        both = jnp.broadcast_to(other[None], (2,) + other.shape)
        both = lax.dynamic_update_slice_in_dim(both, mine[None], at.sequence, 0)
        return both.reshape(1, 2 * other.shape[0], model)

    layer_out = both_sequences(layer_mine, layer_far)
    input_grad = both_sequences(
        jnp.where(at.first, first_grad, second_grad),
        jnp.where(at.first, first_grad_far.reshape(first_grad.shape), grad_far),
    )
    g_gate, g_up, g_down = [
        jnp.where(at.first, whole_of(zero), one).astype(F32) for zero, one in zip(wide_zero, wide_one)
    ]
    g_query, g_key_up, g_value_up, g_out = unpack_attention(whole_of(packed).astype(F32), model)
    width = model // at.count
    depth = latent.shape[1] - GAIN_ROWS
    g_latent = latent[:, :depth].reshape(width, KVH * LH).astype(F32)
    gains = latent[0, depth : depth + 2, :width].astype(F32)
    return (
        layer_out,
        input_grad,
        g_query[None],
        g_latent[None],
        g_key_up[None],
        g_value_up[None],
        g_out[None],
        g_gate.T[None],
        g_up.T[None],
        g_down[None],
        gains[0:1],
        gains[1:2],
    )


def solution(mesh):
    columns = P(SEC, None, TEN)
    rows = P(SEC, TEN, None)
    return jax.shard_map(
        local,
        mesh=mesh,
        in_specs=(
            P(DP, None),
            P(DP, None),
            columns,
            P(SEC, None, None),
            columns,
            columns,
            rows,
            columns,
            columns,
            rows,
            P(SEC, None),
            P(SEC, None),
        ),
        out_specs=(
            P(SEC, DP, None),
            P(SEC, DP, None),
            columns,
            rows,
            columns,
            columns,
            rows,
            columns,
            columns,
            rows,
            P(SEC, TEN),
            P(SEC, TEN),
        ),
        check_vma=False,
    )
```

time: 880 us -> 682 us (0.78)
  waiting for transfers between devices: 266 us -> 34 us
  Pallas kernels: 349 us -> 527 us
  blocking collectives: 105 us -> 0 us
  other arithmetic: 53.3 us -> 31.7 us
  local copies, waits for them, and re-layouts: 50.8 us -> 31.4 us
  starting transfers between devices: 19.8 us -> 34.6 us
  between operations: 15.2 us -> 2.03 us
    pallas_call x8 -> x10, Pallas kernels: 316 us -> 494 us  [the longest x8 396 us: team_call(): pl.pallas_call(functools.partial(team_kernel, body, counts, core), in_spe...]
    reduce_scatter x6 -> x0, waiting for transfers between devices: 126 us -> none  [the longest x4 100 us: scatter(): return lax.psum_scatter(matrix, DP, scatter_dimension=0, tiled=True)]
    psum x1 -> x0, blocking collectives: 105 us -> none  [local(): lax.psum(jnp.concatenate([attn_gain_one, mlp_gain_one, attn_gain_two, mlp...]
    ppermute x8 -> x12, waiting for transfers between devices: 97.6 us -> 13.3 us  [across(): return lax.ppermute(block, (SEC, TEN), route)]
    select_n x12 -> x8, other arithmetic: 26.9 us -> 7.02 us  [the longest x1 2.19 us: attention_weights(): latent = jnp.where(mine, own_latent, far_latent)]
    unnamed x139 -> x146, local copies, waits for them, and re-layouts: 28.7 us -> 10.7 us
    ppermute x8 -> x12, starting transfers between devices: 12.4 us -> 30 us  [across(): return lax.ppermute(block, (SEC, TEN), route)]
    ppermute x3 -> x2, waiting for transfers between devices: 35.9 us -> 20.8 us  [opposite(): return lax.ppermute(block, (SEC, TEN), route)]
  transfers between devices with their start and end apart: 27 -> 14, of which waited for: 12 -> 4; matrix products, arithmetic and copies ran while one was open for 9% -> 5% of each run, Pallas kernels for 22% -> 39%
where the time goes in v3:
time: 682 us; the launch traced here: 674 us
  Pallas kernels  527 us (77%)
  starting transfers between devices  34.6 us (5%)
  waiting for transfers between devices  34 us (5%)
  other arithmetic  31.7 us (5%)
  local copies, waits for them, and re-layouts  31.4 us (5%)
  matrix products  14 us (2%)
    pallas_call x8, Pallas kernels, team_call(): pl.pallas_call(functools.partial(team_kernel, body, counts, core), in_spe...  396 us
    pallas_call x1, Pallas kernels, finish(): pl.pallas_call(functools.partial(finish_kernel, groups), in_specs=[vmem]...  91.4 us
    ppermute x12, starting transfers between devices, across(): return lax.ppermute(block, (SEC, TEN), route)  30 us
    ppermute x2, waiting for transfers between devices, opposite(): return lax.ppermute(block, (SEC, TEN), route)  20.8 us
    pallas_call x2, Pallas kernels, attend_backward(): pl.pallas_call(attend_back_kernel, grid=(columns // width,), in_specs=[sp...  18.1 us
    pallas_call x2, Pallas kernels, attend_forward(): pl.pallas_call(attend_kernel, grid=(columns // width,), in_specs=[spec] *...  14.5 us
    dot_general x14, matrix products, mm(): return lax.dot_general(left, right, dims, preferred_element_type=F32)  14 us
  transfers between devices with their start and end apart: 14, of which 4 were waited for; matrix products, arithmetic and copies ran while one was open for 5% of the time, Pallas kernels for 39%

profile of v3, /device:TPU:0, one launch (start us, length us, event | category | flops | bytes accessed | tf_op | source)
XLA Modules:
  0.0 674.3 jit_solution(5096316696815120627)
XLA Ops:
  2.5 6.3 collective-permute-start
  17.7 6.8 %shard_map.211 = (bf16[4,640,256]{2,1,0:T(8,128)(2,1)S(1)}, bf16[1024,256]{1,0:T(8,128)(2,1)S(1)}, f32[2,1024]{1,0:T(2,128)S(1)}) custom-call(bf16[4,640,256]{2,1,0:T(8,128)(2,1)S(1)} %bitcast.151, bf16[1024,256]{1,0:T(8,128)(2,1)S(1)} %dynamic-slice_bitcast_fusion.latent, f32[2,1024]{1,0:T(2,128)S(1)} %pad_maximum_fusion.2.gains), custom_call_target="tpu_custom_call" | custom-call | flops 15000000512 | bytes 2097152 | tf_op jit(solution)/shard_map/pallas_call | solution.py:672
  26.8 3.3 fusion
  35.4 7.2 %shard_map.212 = (bf16[1024,256]{1,0:T(8,128)(2,1)S(1)}, f32[2,2,1024]{2,1,0:T(2,128)S(1)}) custom-call(bf16[1024,256]{1,0:T(8,128)(2,1)S(1)} %convolution_convert_fusion.9.q_ref, bf16[1024,256]{1,0:T(8,128)(2,1)S(1)} %convolution_convert_fusion.3.k_ref, bf16[1024,256]{1,0:T(8,128)(2,1)S(1)} %convolution_convert_fusion.2.v_ref), custom_call_target="tpu_custom_call" | custom-call | flops 2147483648 | bytes 2097152 | tf_op jit(solution)/shard_map/pallas_call | solution.py:77
  47.9 60.5 %shard_map.213 = (f32[4,128,1024]{2,1,0:T(8,128)}, bf16[4,2,128,1024]{3,2,1,0:T(8,128)(2,1)}, bf16[4,176,1024]{2,1,0:T(8,128)(2,1)}, bf16[4,176,1024]{2,1,0:T(8,128)(2,1)}, bf16[4,176,1024]{2,1,0:T(8,128)(2,1)}) custom-call(bf16[1024,256]{1,0:T(8,128)(2,1)} %copy-done.10, bf16[256,1024]{1,0:T(8,128)(2,1)} %pad_maximum_fusion.refs_1_, ...), custom_call_target="tpu_custom_call" | custom-call | flops 30000001024 | bytes 4194304 | tf_op jit(solution)/shard_map/pallas_call | solution.py:512
  109.1 38.9 %shard_map.214 = (f32[1024,704]{1,0:T(8,128)}, f32[1024,704]{1,0:T(8,128)}, bf16[1024,704]{1,0:T(8,128)(2,1)}, bf16[4,2,128,1024]{3,2,1,0:T(8,128)(2,1)}, bf16[4,640,256]{2,1,0:T(8,128)(2,1)}) custom-call(bf16[1024,1024]{1,0:T(8,128)(2,1)} %bitcast.196, f32[4,128,1024]{2,1,0:T(8,128)} %get-tuple-element.119.refs_1_.refs_5_, bf16[704,1024]{1,0:T(8,128)(2,1)} %bitcast.174, ...), custom_call_target="tpu_custom_call" | custom-call | flops 30000001024 | bytes 4194304 | tf_op jit(solution)/shard_map/pallas_call | solution.py:512
  162.4 7.2 %shard_map.215 = (bf16[1024,256]{1,0:T(8,128)(2,1)S(1)}, f32[2,2,1024]{2,1,0:T(2,128)S(1)}) custom-call(bf16[1024,256]{1,0:T(8,128)(2,1)S(1)} %convolution_convert_fusion.7.q_ref, bf16[1024,256]{1,0:T(8,128)(2,1)S(1)} %convolution_convert_fusion.1.k_ref, bf16[1024,256]{1,0:T(8,128)(2,1)S(1)} %convolution_convert_fusion.v_ref), custom_call_target="tpu_custom_call" | custom-call | flops 2147483648 | bytes 2097152 | tf_op jit(solution)/shard_map/pallas_call | solution.py:77
  170.4 5.5 collective-permute-done.4.refs_4_
  175.9 3.9 collective-permute-done.5.refs_5_
  179.8 3.9 collective-permute-done.6.refs_6_
  184.4 34.5 %shard_map.216 = (f32[4,128,1024]{2,1,0:T(8,128)}, bf16[4,2,128,1024]{3,2,1,0:T(8,128)(2,1)}, bf16[4,176,1024]{2,1,0:T(8,128)(2,1)}, bf16[4,176,1024]{2,1,0:T(8,128)(2,1)}, bf16[4,176,1024]{2,1,0:T(8,128)(2,1)}) custom-call(bf16[1024,256]{1,0:T(8,128)(2,1)} %copy-done.12, bf16[256,1024]{1,0:T(8,128)(2,1)} %pad_maximum_fusion.1.refs_1_, ...), custom_call_target="tpu_custom_call" | custom-call | flops 30000001024 | bytes 4194304 | tf_op jit(solution)/shard_map/pallas_call | solution.py:512
  219.0 38.5 %shard_map.217 = (f32[1024,704]{1,0:T(8,128)}, f32[1024,704]{1,0:T(8,128)}, bf16[1024,704]{1,0:T(8,128)(2,1)}, bf16[4,2,128,1024]{3,2,1,0:T(8,128)(2,1)}) custom-call(bf16[1024,1024]{1,0:T(8,128)(2,1)} %bitcast.202, f32[4,128,1024]{2,1,0:T(8,128)} %get-tuple-element.135.refs_1_.refs_5_, bf16[704,1024]{1,0:T(8,128)(2,1)} %bitcast.176, ...), custom_call_target="tpu_custom_call" | custom-call | flops 30000001024 | bytes 4194304 | tf_op jit(solution)/shard_map/pallas_call | solution.py:512
  259.0 44.0 %shard_map.218 = (f32[4,128,1024]{2,1,0:T(8,128)}, bf16[4,2,128,1024]{3,2,1,0:T(8,128)(2,1)}, f32[1,1024]{1,0:T(1,128)}, bf16[704,1024]{1,0:T(8,128)(2,1)}, bf16...) custom-call(bf16[4,2,128,1024]{3,2,1,0:T(8,128)(2,1)} %bitcast.164, f32[1024,704]{1,0:T(8,128)} %get-tuple-element.139.refs_1_, ...), custom_call_target="tpu_custom_call" | custom-call | flops 30000001024 | bytes 4194304 | tf_op jit(solution)/shard_map/pallas_call | solution.py:512
  303.0 2.4 convolution_convert_fusion.5.g_ref
  305.4 9.3 %shard_map.219 = (bf16[1024,256]{1,0:T(8,128)(2,1)S(1)}, bf16[1024,256]{1,0:T(8,128)(2,1)S(1)}, bf16[1024,256]{1,0:T(8,128)(2,1)S(1)}) custom-call(bf16[1024,256]{1,0:T(8,128)(2,1)S(1)} %convolution_convert_fusion.7.q_ref, bf16[1024,256]{1,0:T(8,128)(2,1)S(1)} %convolution_convert_fusion.1.k_ref, bf16[1024,256]{1,0:T(8,128)(2,1)S(1)} %convolution_convert_fusion.v_ref, ...), custom_call_target="tpu_custom_call" | custom-call | flops 5368709120 | bytes 4194304 | tf_op jit(solution)/shard_map/pallas_call | solution.py:136
  316.1 2.6 collective-permute-start.7
  320.8 69.3 %shard_map.220 = (bf16[4,2,128,1024]{3,2,1,0:T(8,128)(2,1)}, f32[1,1024]{1,0:T(1,128)}, bf16[2560,256]{1,0:T(8,128)(2,1)}, bf16[1024,256]{1,0:T(8,128)(2,1)}, bf...) custom-call(bf16[1024,256]{1,0:T(8,128)(2,1)} %copy-done.15, ...), custom_call_target="tpu_custom_call" | custom-call | flops 30000001024 | bytes 4194304 | tf_op jit(solution)/shard_map/pallas_call | solution.py:512
  391.9 5.4 collective-permute-start.10
  400.9 20.8 %collective-permute-done.7 = bf16[1024,1024]{1,0:T(8,128)(2,1)} collective-permute-done((bf16[1024,1024]{1,0:T(8,128)(2,1)S(1)}, bf16[1024,1024]{1,0:T(8,128)(2,1)}, u32[]{:S(2)}, u32[]{:S(2)}) %collective-permute-start.7) | collective-permute-done | bytes 2097184 | tf_op jit(solution)/shard_map/ppermute | solution.py:167
  421.6 43.0 %shard_map.221 = (f32[4,128,1024]{2,1,0:T(8,128)}, bf16[4,2,128,1024]{3,2,1,0:T(8,128)(2,1)}, f32[1,1024]{1,0:T(1,128)}, bf16[704,1024]{1,0:T(8,128)(2,1)}, bf16...) custom-call(bf16[4,2,128,1024]{3,2,1,0:T(8,128)(2,1)} %bitcast.43.refs_0, ...), custom_call_target="tpu_custom_call" | custom-call | flops 30000001024 | bytes 4194304 | tf_op jit(solution)/shard_map/pallas_call | solution.py:512
  468.9 8.9 %shard_map.222 = (bf16[1024,256]{1,0:T(8,128)(2,1)S(1)}, bf16[1024,256]{1,0:T(8,128)(2,1)S(1)}, bf16[1024,256]{1,0:T(8,128)(2,1)S(1)}) custom-call(bf16[1024,256]{1,0:T(8,128)(2,1)S(1)} %copy-done.9, bf16[1024,256]{1,0:T(8,128)(2,1)S(1)} %copy-done.5, bf16[1024,256]{1,0:T(8,128)(2,1)S(1)} %copy-done.3, bf16[1024,256]{1,0:T(8,128)(2,1)S(1)} %copy-done.11, ...), custom_call_target="tpu_custom_call" | custom-call | flops 5368709120 | bytes 4194304 | tf_op jit(solution)/shard_map/pallas_call | solution.py:136
  481.2 5.1 collective-permute-start.12
  489.7 67.0 %shard_map.223 = (bf16[4,2,128,1024]{3,2,1,0:T(8,128)(2,1)}, f32[1,1024]{1,0:T(1,128)}, bf16[2560,256]{1,0:T(8,128)(2,1)}, bf16[1024,256]{1,0:T(8,128)(2,1)}, bf...) custom-call(bf16[1024,256]{1,0:T(8,128)(2,1)} %copy-done.14, ...), custom_call_target="tpu_custom_call" | custom-call | flops 30000001024 | bytes 4194304 | tf_op jit(solution)/shard_map/pallas_call | solution.py:512
  564.3 91.4 %shard_map.224 = (bf16[4,176,1024]{2,1,0:T(8,128)(2,1)}, bf16[4,176,1024]{2,1,0:T(8,128)(2,1)}, bf16[4,176,1024]{2,1,0:T(8,128)(2,1)}, bf16[4,640,256]{2,1,0:T(8...) custom-call(bf16[176,1024]{1,0:T(8,128)(2,1)} %get-tuple-element.180.refs_0_, ...), custom_call_target="tpu_custom_call" | custom-call | tf_op jit(solution)/shard_map/pallas_call | solution.py:806
  (243 shorter events, 86.7 us)
Async XLA Ops:
  2.5 44.1 %collective-permute-start = (bf16[176,1024]{1,0:T(8,128)(2,1)}, bf16[176,1024]{1,0:T(8,128)(2,1)}, u32[]{:S(2)}, u32[]{:S(2)}) collective-permute-start(bf16[176,1024]{1,0:T(8,128)(2,1)} %dynamic-slice_bitcast_fusion.3), channel_id=1, source_target_pairs={{0,18},{1,19},{2,16},{3,17},{4,22},{5,23},{6,20},{7,21},{8,26},{9,... | collective-permute-start | bytes 1081352 | tf_op jit(solution)/shard_map/ppermute | solution.py:172
  10.5 36.1 %collective-permute-start.1 = (bf16[176,1024]{1,0:T(8,128)(2,1)}, bf16[176,1024]{1,0:T(8,128)(2,1)}, u32[]{:S(2)}, u32[]{:S(2)}) collective-permute-start(bf16[176,1024]{1,0:T(8,128)(2,1)} %dynamic-slice_bitcast_fusion.2), channel_id=1, source_target_pairs={{0,18},{1,19},{2,16},{3,17},{4,22},{5,23},{6,20},{7,21},{8,26},{9,... | collective-permute-start | bytes 1081352 | tf_op jit(solution)/shard_map/ppermute | solution.py:172
  14.3 32.3 %collective-permute-start.2 = (bf16[176,1024]{1,0:T(8,128)(2,1)}, bf16[176,1024]{1,0:T(8,128)(2,1)}, u32[]{:S(2)}, u32[]{:S(2)}) collective-permute-start(bf16[176,1024]{1,0:T(8,128)(2,1)} %dynamic-slice_bitcast_fusion.1), channel_id=1, source_target_pairs={{0,18},{1,19},{2,16},{3,17},{4,22},{5,23},{6,20},{7,21},{8,26},{9,... | collective-permute-start | bytes 1081352 | tf_op jit(solution)/shard_map/ppermute | solution.py:172
  24.7 19.5 %copy-start.21 = (bf16[2560,256]{1,0:T(8,128)(2,1)}, bf16[2560,256]{1,0:T(8,128)(2,1)S(1)}, u32[]{:S(2)}) copy-start(bf16[2560,256]{1,0:T(8,128)(2,1)S(1)} %bitcast_select_fusion.2) | copy-start | bytes 3932164
  25.5 19.6 %copy-start.43 = (bf16[256,256]{1,0:T(8,128)(2,1)}, bf16[256,256]{1,0:T(8,128)(2,1)S(1)}, u32[]{:S(2)}) copy-start(bf16[256,256]{1,0:T(8,128)(2,1)S(1)} %get-tuple-element.218) | copy-start | bytes 393220
  25.5 19.6 %copy-start.45 = (bf16[256,256]{1,0:T(8,128)(2,1)}, bf16[256,256]{1,0:T(8,128)(2,1)S(1)}, u32[]{:S(2)}) copy-start(bf16[256,256]{1,0:T(8,128)(2,1)S(1)} %get-tuple-element.219) | copy-start | bytes 393220
  25.5 19.6 %copy-start.47 = (bf16[256,256]{1,0:T(8,128)(2,1)}, bf16[256,256]{1,0:T(8,128)(2,1)S(1)}, u32[]{:S(2)}) copy-start(bf16[256,256]{1,0:T(8,128)(2,1)S(1)} %get-tuple-element.220) | copy-start | bytes 393220
  46.5 104.0 %copy-start.62 = (f32[1,1024]{1,0:T(1,128)}, f32[1,1024]{1,0:T(1,128)S(1)}, u32[]{:S(2)}) copy-start(f32[1,1024]{1,0:T(1,128)S(1)} %get-tuple-element.225.refs_6_) | copy-start | bytes 12292
  46.6 61.8 %collective-permute-start.3 = (bf16[640,256]{1,0:T(8,128)(2,1)S(1)}, bf16[640,256]{1,0:T(8,128)(2,1)S(1)}, u32[]{:S(2)}, u32[]{:S(2)}) collective-permute-start(bf16[640,256]{1,0:T(8,128)(2,1)S(1)} %constant_dynamic-slice_fusion.4), channel_id=1, source_target_pairs={{16,2},{17,3},{18,0},{19,1},{20,6},{21,7},{22,4},{23,5},{24,10},{2... | collective-permute-start | bytes 983048 | tf_op jit(solution)/shard_map/ppermute | solution.py:172
  154.7 21.3 %collective-permute-start.4 = (bf16[176,1024]{1,0:T(8,128)(2,1)S(1)}, bf16[176,1024]{1,0:T(8,128)(2,1)S(1)}, u32[]{:S(2)}, u32[]{:S(2)}) collective-permute-start(bf16[176,1024]{1,0:T(8,128)(2,1)S(1)} %constant_dynamic-slice_fusion.3), channel_id=1, source_target_pairs={{16,2},{17,3},{18,0},{19,1},{20,6},{21,7},{22,4},{23,5},{24,10},{2... | collective-permute-start | bytes 1081352 | tf_op jit(solution)/shard_map/ppermute | solution.py:172
  157.0 22.8 %collective-permute-start.5 = (bf16[176,1024]{1,0:T(8,128)(2,1)S(1)}, bf16[176,1024]{1,0:T(8,128)(2,1)S(1)}, u32[]{:S(2)}, u32[]{:S(2)}) collective-permute-start(bf16[176,1024]{1,0:T(8,128)(2,1)S(1)} %constant_dynamic-slice_fusion.2), channel_id=1, source_target_pairs={{16,2},{17,3},{18,0},{19,1},{20,6},{21,7},{22,4},{23,5},{24,10},{2... | collective-permute-start | bytes 1081352 | tf_op jit(solution)/shard_map/ppermute | solution.py:172
  159.3 24.4 %collective-permute-start.6 = (bf16[176,1024]{1,0:T(8,128)(2,1)S(1)}, bf16[176,1024]{1,0:T(8,128)(2,1)S(1)}, u32[]{:S(2)}, u32[]{:S(2)}) collective-permute-start(bf16[176,1024]{1,0:T(8,128)(2,1)S(1)} %constant_dynamic-slice_fusion.1), channel_id=1, source_target_pairs={{16,2},{17,3},{18,0},{19,1},{20,6},{21,7},{22,4},{23,5},{24,10},{2... | collective-permute-start | bytes 1081352 | tf_op jit(solution)/shard_map/ppermute | solution.py:172
  218.9 38.5 %copy-start.17 = (bf16[4,2,128,1024]{3,2,1,0:T(8,128)(2,1)S(1)}, bf16[4,2,128,1024]{3,2,1,0:T(8,128)(2,1)}, u32[]{:S(2)}) copy-start(bf16[4,2,128,1024]{3,2,1,0:T(8,128)(2,1)} %get-tuple-element.124.refs_2_.refs_4_) | copy-start | bytes 6291460
  316.1 105.5 %collective-permute-start.7 = (bf16[1024,1024]{1,0:T(8,128)(2,1)S(1)}, bf16[1024,1024]{1,0:T(8,128)(2,1)}, u32[]{:S(2)}, u32[]{:S(2)}) collective-permute-start(bf16[1024,1024]{1,0:T(8,128)(2,1)S(1)} %bitcast.152), channel_id=1, source_target_pairs={{0,2},{1,3},{2,0},{3,1},{16,18},{17,19},{18,16},{19,17},{4,6},{5,7... | collective-permute-start | bytes 6291464 | tf_op jit(solution)/shard_map/ppermute | solution.py:167
  320.8 70.0 %copy-start.64 = (f32[1,1024]{1,0:T(1,128)S(1)}, f32[1,1024]{1,0:T(1,128)}, u32[]{:S(2)}) copy-start(f32[1,1024]{1,0:T(1,128)} %get-tuple-element.163) | copy-start | bytes 12292
  391.9 72.7 %collective-permute-start.10 = (bf16[176,1024]{1,0:T(8,128)(2,1)}, bf16[176,1024]{1,0:T(8,128)(2,1)S(1)}, u32[]{:S(2)}, u32[]{:S(2)}) collective-permute-start(bf16[176,1024]{1,0:T(8,128)(2,1)} %get-tuple-element.172), channel_id=1, source_target_pairs={{0,18},{1,19},{2,16},{3,17},{4,22},{5,23},{6,20},{7,21},{8,26},{9,... | collective-permute-start | bytes 1081352 | tf_op jit(solution)/shard_map/ppermute | solution.py:172
  397.3 67.3 %collective-permute-start.8 = (bf16[176,1024]{1,0:T(8,128)(2,1)}, bf16[176,1024]{1,0:T(8,128)(2,1)S(1)}, u32[]{:S(2)}, u32[]{:S(2)}) collective-permute-start(bf16[176,1024]{1,0:T(8,128)(2,1)} %get-tuple-element.170), channel_id=1, source_target_pairs={{0,18},{1,19},{2,16},{3,17},{4,22},{5,23},{6,20},{7,21},{8,26},{9,... | collective-permute-start | bytes 1081352 | tf_op jit(solution)/shard_map/ppermute | solution.py:172
  398.6 66.0 %collective-permute-start.9 = (bf16[176,1024]{1,0:T(8,128)(2,1)}, bf16[176,1024]{1,0:T(8,128)(2,1)S(1)}, u32[]{:S(2)}, u32[]{:S(2)}) collective-permute-start(bf16[176,1024]{1,0:T(8,128)(2,1)} %get-tuple-element.171), channel_id=1, source_target_pairs={{0,18},{1,19},{2,16},{3,17},{4,22},{5,23},{6,20},{7,21},{8,26},{9,... | collective-permute-start | bytes 1081352 | tf_op jit(solution)/shard_map/ppermute | solution.py:172
  421.6 43.0 %copy-start.53 = (bf16[176,1024]{1,0:T(8,128)(2,1)S(1)}, bf16[176,1024]{1,0:T(8,128)(2,1)}, u32[]{:S(2)}) copy-start(bf16[176,1024]{1,0:T(8,128)(2,1)} %get-tuple-element.172) | copy-start | bytes 1081348
  421.6 43.9 %copy-start.52 = (bf16[176,1024]{1,0:T(8,128)(2,1)S(1)}, bf16[176,1024]{1,0:T(8,128)(2,1)}, u32[]{:S(2)}) copy-start(bf16[176,1024]{1,0:T(8,128)(2,1)} %get-tuple-element.171) | copy-start | bytes 1081348
  479.2 83.6 %collective-permute-start.11 = (bf16[1024,1024]{1,0:T(8,128)(2,1)}, bf16[1024,1024]{1,0:T(8,128)(2,1)}, u32[]{:S(2)}, u32[]{:S(2)}) collective-permute-start(bf16[1024,1024]{1,0:T(8,128)(2,1)} %bitcast.40), channel_id=1, source_target_pairs={{16,18},{17,19},{18,16},{19,17},{20,22},{21,23},{22,20},{23,21},{2... | collective-permute-start | bytes 6291464 | tf_op jit(solution)/shard_map/ppermute | solution.py:167
  481.2 81.6 %collective-permute-start.12 = (bf16[640,256]{1,0:T(8,128)(2,1)S(1)}, bf16[640,256]{1,0:T(8,128)(2,1)S(1)}, u32[]{:S(2)}, u32[]{:S(2)}) collective-permute-start(bf16[640,256]{1,0:T(8,128)(2,1)S(1)} %copy-done.54), channel_id=1, source_target_pairs={{0,18},{1,19},{2,16},{3,17},{4,22},{5,23},{6,20},{7,21},{8,26},{9,... | collective-permute-start | bytes 983048 | tf_op jit(solution)/shard_map/ppermute | solution.py:172
  486.3 76.5 %collective-permute-start.13 = (bf16[320,256]{1,0:T(8,128)(2,1)S(1)}, bf16[320,256]{1,0:T(8,128)(2,1)S(1)}, u32[]{:S(2)}, u32[]{:S(2)}) collective-permute-start(bf16[320,256]{1,0:T(8,128)(2,1)S(1)} %copy-done.56), channel_id=1, source_target_pairs={{0,18},{1,19},{2,16},{3,17},{4,22},{5,23},{6,20},{7,21},{8,26},{9,... | collective-permute-start | bytes 491528 | tf_op jit(solution)/shard_map/ppermute | solution.py:172
  489.7 67.7 %copy-start.63 = (f32[1,1024]{1,0:T(1,128)S(1)}, f32[1,1024]{1,0:T(1,128)}, u32[]{:S(2)}) copy-start(f32[1,1024]{1,0:T(1,128)} %get-tuple-element.186) | copy-start | bytes 12292
  (60 other events, 242.5 us)

commit v4 on v3

--- a/solution.py
+++ b/solution.py
@@ -1,5 +1,6 @@
 import functools
 import math
+import types
 
 import jax
 import jax.numpy as jnp
@@ -37,57 +38,38 @@
     return block if mask is None else jnp.where(mask, block, jnp.zeros_like(block))
 
 
-def attend_kernel(q_ref, k_ref, v_ref, o_ref, norm_ref):
-    width = q_ref.shape[1]
+def attend_rows(start, q_ref, k_ref, v_ref, o_ref, norm_ref):
+    columns = q_ref.shape[1]
+    width = min(2 * HD, columns)
     masks = head_masks(width)
     rows = KEY_ROWS
     place_k = lax.broadcasted_iota(jnp.int32, (rows, rows), 0)
     place_q = lax.broadcasted_iota(jnp.int32, (rows, rows), 1)
-    for start in range(0, LEN, rows):
-        query = q_ref[start : start + rows, :]
+    for pair in range(columns // width):
+        lanes = slice(pair * width, (pair + 1) * width)
+        query = q_ref[start : start + rows, lanes]
         total = None
         for j, mask in enumerate(masks):
             query_j = keep_head(query, mask)
-            scores = mm(k_ref[start : start + rows, :], query_j, 1, 1) * LOG2_SCALE
+            scores = mm(k_ref[start : start + rows, lanes], query_j, 1, 1) * LOG2_SCALE
             scores = jnp.where(place_k <= place_q, scores, -jnp.inf)
             largest = jnp.max(scores, axis=0, keepdims=True)
             if start:
-                before = mm(k_ref[0:start, :], query_j, 1, 1) * LOG2_SCALE
+                before = mm(k_ref[0:start, lanes], query_j, 1, 1) * LOG2_SCALE
                 largest = jnp.maximum(largest, jnp.max(before, axis=0, keepdims=True))
             weight = jnp.exp2(scores - largest)
             norm = jnp.sum(weight, axis=0, keepdims=True)
-            value = keep_head(v_ref[start : start + rows, :], mask)
+            value = keep_head(v_ref[start : start + rows, lanes], mask)
             out = mm(value, weight.astype(BF16), 0, 0)
             if start:
                 weight = jnp.exp2(before - largest)
                 norm = norm + jnp.sum(weight, axis=0, keepdims=True)
-                value = keep_head(v_ref[0:start, :], mask)
+                value = keep_head(v_ref[0:start, lanes], mask)
                 out = out + mm(value, weight.astype(BF16), 0, 0)
             out = out / norm
             total = out if total is None else total + out
-            norm_ref[0, j : j + 1, start : start + rows] = largest + jnp.log2(norm)
-        o_ref[start : start + rows, :] = total.T.astype(BF16)
-
-
-def attend_forward(queries, keys, values):
-    rows, columns = queries.shape
-    width = min(2 * HD, columns)
-    heads = width // HD
-    spec = pl.BlockSpec((rows, width), lambda i: (0, i))
-    return pl.pallas_call(
-        attend_kernel,
-        grid=(columns // width,),
-        in_specs=[spec] * 3,
-        out_specs=[spec, pl.BlockSpec((1, heads, rows), lambda i: (i, 0, 0))],
-        out_shape=[
-            jax.ShapeDtypeStruct((rows, columns), BF16),
-            jax.ShapeDtypeStruct((columns // width, heads, rows), F32),
-        ],
-        compiler_params=pltpu.CompilerParams(vmem_limit_bytes=40 * 2**20),
-        cost_estimate=pl.CostEstimate(
-            flops=rows * rows * columns * 8, bytes_accessed=rows * columns * 8, transcendentals=0
-        ),
-    )(queries, keys, values)
+            norm_ref[pair, j : j + 1, start : start + rows] = largest + jnp.log2(norm)
+        o_ref[start : start + rows, lanes] = total.T.astype(BF16)
 
 
 def attend_back_kernel(q_ref, k_ref, v_ref, o_ref, g_ref, norm_ref, dq_ref, dk_ref, dv_ref, acc):
@@ -203,7 +185,7 @@
 MESH = pl.DeviceIdType.MESH
 PIECES = 4
 VMEM_LIMIT = 58 * 2**20
-LINK_FLOPS = 30 * 10**9
+LINK_FLOPS = 4 * 10**9
 GAIN_ROWS = 16
 DMA = pltpu.SemaphoreType.DMA
 
@@ -426,12 +408,14 @@
         whole[i, self.team.core] = half
         self.join_copy(i, whole).start()
 
-    def finish(self, whole):
+    def finish(self, whole, coming=True):
         def drain(i):
             self.core_copy(i).wait_send()
             for step in range(1, self.team.size):
                 self.far_copy(i, step, self.team.place).wait_send()
-            self.join_copy(i, whole).wait()
+            self.join_copy(i, whole).wait_send()
+            if coming:
+                self.join_copy(i, whole).wait_recv()
 
         each_piece(drain)
 
@@ -465,28 +449,78 @@
     return [pltpu.VMEM(matrix.shape, BF16) for matrix in own] + [DMA((3,))]
 
 
-def team_kernel(body, counts, core, *refs):
-    inner, loads, pieces, outs, scratch = counts
+class Beside:
+    def __init__(self, loads=(), pieces=(), core=0, crosses=(), sender=0, add=False):
+        self.loads, self.pieces, self.crosses = list(loads), list(pieces), list(crosses)
+        self.core, self.sender, self.add = core, sender, add
+
+    def operands(self):
+        return self.loads + self.pieces + self.crosses
+
+    def cross_shape(self, cross):
+        return cross.shape if self.add else cross.shape[1:]
+
+    def outs(self):
+        dp = lax.axis_size(DP)
+        shapes = [load.shape[1:] for load in self.loads]
+        shapes = shapes + [(dp,) + piece.shape for piece in self.pieces]
+        return [(shape, BF16) for shape in shapes + [self.cross_shape(c) for c in self.crosses]]
+
+    def specs(self):
+        vmem = pl.BlockSpec(memory_space=pltpu.VMEM)
+        held = len(self.loads) + len(self.pieces)
+        cross = vmem if self.add else pl.BlockSpec(memory_space=pl.ANY)
+        return [vmem] * held + [cross] * len(self.crosses)
+
+    def scratch(self):
+        items = [item for load in self.loads for item in scatter_scratch(load)]
+        items = items + [DMA((3,)), DMA((lax.axis_size(DP),))] * len(self.pieces)
+        return items + [DMA, DMA] * len(self.crosses)
+
+    def counts(self):
+        return len(self.loads), len(self.pieces), len(self.crosses)
+
+
+def across_device():
+    count = lax.axis_size(TEN)
+    opposite = lax.rem(lax.axis_index(TEN) + count // 2, count)
+    return {SEC: 1 - lax.axis_index(SEC), TEN: opposite}
+
+
+def team_kernel(body, counts, beside, add, cores, *refs):
+    inner, outs, scratch = counts
+    loads, pieces, crosses = beside
+    gather_core, sender = cores
 
     def take(count):
         nonlocal refs
         taken, refs = refs[:count], refs[count:]
         return taken
 
-    inner, loads, pieces = take(inner), take(loads), take(pieces)
+    inner, loads, pieces, crosses = take(inner), take(loads), take(pieces), take(crosses)
     outs, sums, wholes = take(outs), take(len(loads)), take(len(pieces))
-    scratch = take(scratch)
+    comes, scratch = take(len(crosses)), take(scratch)
     team = Team()
     plane = Plane()
+    core = lax.axis_index(SEC)
     scatters = [Scatter(plane, k, load, *take(4)) for k, load in enumerate(loads)]
-    active = lax.axis_index(SEC) == core
-    gathers = [Gather(plane, k, whole, *take(2), active) for k, whole in enumerate(wholes)]
+    gathers = [Gather(plane, k, whole, *take(2), core == gather_core) for k, whole in enumerate(wholes)]
+    across = across_device()
+    sources = [cross if add else cross.at[plane.me] for cross in crosses]
+    copies = [send_to(source, come, *take(2), across) for source, come in zip(sources, comes)]
     ex = Exchange(team, refs)
-    greet(team.partners() + (plane.partners() if loads or pieces else []))
+    partners = team.partners()
+    if loads or pieces:
+        partners = partners + plane.partners()
+    if crosses:
+        partners = partners + [across]
+    greet(partners)
     for scatter in scatters:
         scatter.start()
     for gather, piece in zip(gathers, pieces):
         gather.start(piece)
+    for copy in copies:
+        pl.when(core == sender)(copy.start)
 
     def middle():
         for item in gathers + scatters:
@@ -498,65 +532,35 @@
         scatter.drain()
     for gather in gathers:
         gather.finish()
-
-
-def team_call(body, number, model, outs, operands, scratch=(), loads=(), pieces=(), core=0, far=0):
+    for copy in copies:
+        pl.when(core == sender)(copy.wait_send)
+
+    @pl.when(core != sender)
+    def _():
+        for copy, source, come in zip(copies, sources, comes):
+            copy.wait_recv()
+            if add:
+                come[...] = (source[...].astype(F32) + come[...].astype(F32)).astype(BF16)
+
+
+def team_call(body, number, model, outs, operands, scratch=(), beside=None, far=0):
     vmem = pl.BlockSpec(memory_space=pltpu.VMEM)
-    dp = lax.axis_size(DP)
-    counts = (len(operands), len(loads), len(pieces), len(outs), len(scratch))
-    outs = outs + [(load.shape[1:], BF16) for load in loads]
-    outs = outs + [((dp,) + piece.shape, BF16) for piece in pieces]
-    beside = [item for load in loads for item in scatter_scratch(load)]
-    beside = beside + [DMA((3,)), DMA((dp,))] * len(pieces)
+    beside = beside or Beside()
+    counts = (len(operands), len(outs), len(scratch))
+    outs = outs + beside.outs()
     specs = [vmem] * (len(operands) - far) + [pl.BlockSpec(memory_space=pl.ANY)] * far
+    cores = (beside.core, beside.sender)
     return pl.pallas_call(
-        functools.partial(team_kernel, body, counts, core),
-        in_specs=specs + [vmem] * (len(loads) + len(pieces)),
+        functools.partial(team_kernel, body, counts, beside.counts(), beside.add, cores),
+        in_specs=specs + beside.specs(),
         out_specs=[vmem] * len(outs),
         out_shape=[jax.ShapeDtypeStruct(*out) for out in outs],
-        scratch_shapes=list(scratch) + beside + exchange_scratch(LEN, model),
+        scratch_shapes=list(scratch) + beside.scratch() + exchange_scratch(LEN, model),
         compiler_params=pltpu.CompilerParams(
             collective_id=number, has_side_effects=True, vmem_limit_bytes=VMEM_LIMIT
         ),
-        cost_estimate=pl.CostEstimate(flops=LINK_FLOPS, bytes_accessed=2**22, transcendentals=0),
-    )(*operands, *loads, *pieces)
-
-
-def project_out(ex, middle, heads, w_out, source, gain, residual, mlp_in):
-    rows = heads.shape[0]
-    ex.send_all(lambda i: mm(heads[piece_rows(i, rows), :], w_out[...]))
-    middle()
-
-    def receive(i):
-        block = source[i, ex.team.core].astype(F32) + ex.total(i)
-        residual[i] = block
-        ex.join(i, mlp_in, (block * reciprocal_rms(block) * gain[...]).astype(BF16))
-
-    each_piece(receive)
-    ex.finish(mlp_in)
-
-
-def feed_forward(layer, ex, middle, mlp_in, residual, *refs):
-    weights = Weights(layer, refs[:6], refs[10:13], refs[13])
-    gate, up, hidden, output, w_gate, w_up, w_down = refs[6:13]
-    rows = mlp_in.shape[0]
-    weights.wait()
-
-    def product(i):
-        at = piece_rows(i, rows)
-        block = mlp_in[at, :]
-        gate_block = mm(block, w_gate[...], 1, 1)
-        up_block = mm(block, w_up[...], 1, 1)
-        hidden_block = (jax.nn.silu(gate_block) * up_block).astype(BF16)
-        gate[at, :] = gate_block
-        up[at, :] = up_block
-        hidden[at, :] = hidden_block
-        return mm(hidden_block, w_down[...])
-
-    ex.send_all(product)
-    middle()
-    each_piece(lambda i: ex.join(i, output, (residual[i] + ex.total(i)).astype(BF16)))
-    ex.finish(output)
+        cost_estimate=pl.CostEstimate(flops=LINK_FLOPS, bytes_accessed=2**20, transcendentals=0),
+    )(*operands, *beside.operands())
 
 
 def rms_back(block, gain, upstream):
@@ -636,50 +640,228 @@
     ex.finish(input_grad)
 
 
-def fetch_kernel(packed, latent, gains, whole, far_latent, far_gains, sent, here, gather_sent, gather_here):
+def named_call(kernel, number, ins, far, outs, scratch, flops=LINK_FLOPS):
+    ins, far, outs, scratch = (dict(group) for group in (ins, far, outs, scratch))
+    spec = {id(ins): pl.BlockSpec(memory_space=pltpu.VMEM), id(far): pl.BlockSpec(memory_space=pl.ANY)}
+    operands, specs, shapes, items = [], [], [], []
+    layout = []
+    for group, store in ((ins, operands), (far, operands), (outs, shapes), (scratch, items)):
+        for name, value in group.items():
+            values = value if isinstance(value, list) else [value]
+            layout.append((name, len(values) if isinstance(value, list) else None))
+            store.extend(values)
+            if store is operands:
+                specs.extend([spec[id(group)]] * len(values))
+
+    def body(*refs):
+        named, refs = {}, list(refs)
+        for name, count in layout:
+            taken, refs = refs[: count if count is not None else 1], refs[count if count is not None else 1 :]
+            named[name] = taken if count is not None else taken[0]
+        kernel(types.SimpleNamespace(**named))
+
+    results = pl.pallas_call(
+        body,
+        in_specs=specs,
+        out_specs=[pl.BlockSpec(memory_space=pl.ANY if len(out) > 2 else pltpu.VMEM) for out in shapes],
+        out_shape=[jax.ShapeDtypeStruct(*out[:2]) for out in shapes],
+        scratch_shapes=items,
+        compiler_params=pltpu.CompilerParams(
+            collective_id=number, has_side_effects=True, vmem_limit_bytes=VMEM_LIMIT
+        ),
+        cost_estimate=pl.CostEstimate(flops=flops, bytes_accessed=2**20, transcendentals=0),
+    )(*operands)
+    named, results = {}, list(results)
+    for name, value in outs.items():
+        if isinstance(value, list):
+            named[name], results = results[: len(value)], results[len(value) :]
+        else:
+            named[name], results = results[0], results[1:]
+    return types.SimpleNamespace(**named)
+
+
+def forward_kernel(layer, r):
+    team = Team()
     plane = Plane()
-    count = lax.axis_size(TEN)
     core = lax.axis_index(SEC)
-    opposite = lax.rem(lax.axis_index(TEN) + count // 2, count)
-    other, across = {SEC: 1 - core}, {SEC: 1 - core, TEN: opposite}
-    greet(plane.partners() + [other, across])
-    piece = send_to(packed.at[plane.me], whole.at[plane.me], sent.at[0], here.at[0], across)
-    small = [
-        send_to(latent, far_latent, sent.at[1], here.at[1], other),
-        send_to(gains, far_gains, sent.at[2], here.at[2], other),
+    holder = core == layer
+    taker = jnp.logical_not(holder)
+    across = across_device()
+    ex_a, ex_b = Exchange(team, r.ex_a), Exchange(team, r.ex_b)
+    abroad = across if layer == 0 else {TEN: across[TEN]}
+    greet(team.partners() + plane.partners() + [abroad])
+    rows, width = r.queries.shape
+    model = r.w_latent.shape[0]
+    size = rows // PIECES
+    feeds = range(3)
+
+    own_copies = [pltpu.make_async_copy(r.own_feed[k], r.feed[k], r.own_sem.at[k]) for k in feeds]
+    for copy in own_copies:
+        pl.when(holder)(copy.start)
+    gathers = [
+        Gather(plane, k, r.feed[k], r.gather_sent.at[k], r.gather_here.at[k], taker) for k in feeds
     ]
-    pl.when(core == 0)(piece.start)
-    for copy in small:
-        copy.start()
-    gather = Gather(plane, 0, whole, gather_sent, gather_here)
-
-    @pl.when(core == 1)
+
+    def cross(k, source, target):
+        return send_to(source, target, r.cross_sent.at[k], r.cross_here.at[k], across)
+
+    if layer == 0:
+        mine = cross(0, r.own_packed.at[plane.me], r.packed.at[plane.me])
+        small = [
+            send_to(r.pass_latent, r.far_latent, r.small_sent.at[0], r.small_here.at[0], team.other),
+            send_to(r.own_gains, r.far_gains, r.small_sent.at[1], r.small_here.at[1], team.other),
+        ]
+        come = [cross(1 + k, r.own_feed[k].at[plane.me], r.come[k]) for k in feeds]
+        next_packed = cross(4, r.own_packed.at[plane.me], r.packed_next.at[plane.me])
+        next_feed = [cross(5 + k, r.own_feed[k].at[plane.me], r.feed_next[k]) for k in feeds]
+        packed_gather = Gather(plane, 0, r.packed, r.packed_sent, r.packed_here)
+        next_gather = Gather(plane, 1, r.packed_next, r.next_sent, r.next_here)
+        pl.when(holder)(mine.start)
+        for copy in small:
+            copy.start()
+        for copy in small:
+            copy.wait()
+    else:
+        before = send_to(r.before, r.before_far, r.before_sent, r.before_here, abroad)
+        pl.when(core == 0)(before.start)
+        for k in feeds:
+            gathers[k].start(r.pieces[k])
+    gains = jnp.where(holder, r.own_gains[...], r.far_gains[...])
+    r.gains[...] = gains
+    r.w_latent[...] = jnp.where(holder, r.own_latent[...], r.far_latent[...])
+
+    def norm(i):
+        block = r.source[i].reshape(size, model).astype(F32)
+        r.attn_in[piece_rows(i, rows), :] = (block * reciprocal_rms(block) * gains[0:1]).astype(BF16)
+
+    each_piece(norm)
+    if layer == 0:
+
+        @pl.when(taker)
+        def _():
+            mine.wait_recv()
+            packed_gather.first.start()
+            packed_gather.second[0].start()
+            packed_gather.middle()
+            packed_gather.finish()
+            r.packed_next[...] = r.own_packed[...]
+
+        @pl.when(holder)
+        def _():
+            r.packed[...] = r.own_packed[...]
+            mine.wait_send()
+            for copy in come:
+                copy.start()
+
+    weights = r.packed[...].reshape(2 * model + 2 * LH, width)
+
+    def project(i):
+        at = piece_rows(i, rows)
+        block = r.attn_in[at, :]
+        r.queries[at, :] = mm(block, weights[:model]).astype(BF16)
+        latents = mm(block, r.w_latent[...]).astype(BF16)
+        r.latents[at, :] = latents
+        r.keys[at, :] = mm(latents, weights[model : model + LH]).astype(BF16)
+        r.values[at, :] = mm(latents, weights[model + LH : model + 2 * LH]).astype(BF16)
+
+    each_piece(project)
+    w_out = [
+        weights[model + 2 * LH + start : model + 2 * LH + start + width] for start in range(0, model, width)
+    ]
+    for i in range(PIECES):
+        attend_rows(i * size, r.queries, r.keys, r.values, r.heads_out, r.norms)
+        heads = r.heads_out[i * size : (i + 1) * size, :]
+        ex_a.push(i, jnp.concatenate([mm(heads, block) for block in w_out], axis=1))
+        if i:
+            ex_a.combine(i - 1)
+    ex_a.combine(PIECES - 1)
+    if layer == 0:
+        pl.when(taker)(next_packed.start)
+
+        @pl.when(taker)
+        def _():
+            for k in feeds:
+                come[k].wait_recv()
+                gathers[k].whole[plane.me] = r.come[k][...]
+                gathers[k].first.start()
+                gathers[k].second[0].start()
+
+    def receive(i):
+        block = r.source[i, core].astype(F32) + ex_a.total(i)
+        r.residual[i] = block
+        ex_a.join(i, r.mlp_in, (block * reciprocal_rms(block) * gains[1:2]).astype(BF16))
+
+    def feed(i):
+        ex_a.join_copy(i, r.mlp_in).wait_recv()
+        at = piece_rows(i, rows)
+        block = r.mlp_in[i].reshape(size, model)
+        shape = (r.hidden.shape[1], model)
+        gate = mm(block, r.feed[0][...].reshape(shape), 1, 1)
+        up = mm(block, r.feed[1][...].reshape(shape), 1, 1)
+        hidden = (jax.nn.silu(gate) * up).astype(BF16)
+        r.gate[at, :] = gate
+        r.up[at, :] = up
+        r.hidden[at, :] = hidden
+        ex_b.push(i, mm(hidden, r.feed[2][...].reshape(shape)))
+
+    receive(0)
+    for gather in gathers:
+        gather.middle()
+
+    @pl.when(holder)
     def _():
-        piece.wait_recv()
-        gather.first.start()
-        gather.second[0].start()
-        gather.middle()
+        for copy in own_copies:
+            copy.wait()
+
+    for gather in gathers:
         gather.finish()
-
-    for copy in small:
-        copy.wait()
-    pl.when(core == 0)(piece.wait_send)
-
-
-def fetch(packed, latent, gains):
-    vmem = pl.BlockSpec(memory_space=pltpu.VMEM)
-    shapes = [jax.ShapeDtypeStruct(x.shape, x.dtype) for x in (packed, latent, gains)]
-    return pl.pallas_call(
-        fetch_kernel,
-        in_specs=[vmem] * 3,
-        out_specs=[vmem] * 3,
-        out_shape=shapes,
-        scratch_shapes=[DMA((3,)), DMA((3,)), DMA((3,)), DMA((4,))],
-        compiler_params=pltpu.CompilerParams(
-            collective_id=8, has_side_effects=True, vmem_limit_bytes=16 * 2**20
-        ),
-        cost_estimate=pl.CostEstimate(flops=LINK_FLOPS // 2, bytes_accessed=2**21, transcendentals=0),
-    )(packed, latent, gains)
+    receive(1)
+    feed(0)
+    if layer == 0:
+
+        @pl.when(taker)
+        def _():
+            for copy in next_feed:
+                copy.start()
+
+        @pl.when(holder)
+        def _():
+            next_packed.wait_recv()
+            next_gather.first.start()
+            next_gather.second[0].start()
+
+    def steady(i, _):
+        receive(i)
+        feed(i - 1)
+        ex_b.combine(i - 2)
+        return 0
+
+    lax.fori_loop(2, PIECES, steady, 0)
+    feed(PIECES - 1)
+    ex_b.combine(PIECES - 2)
+    ex_b.combine(PIECES - 1)
+    if layer == 0:
+        pl.when(holder)(next_gather.middle)
+    each_piece(lambda i: ex_b.join(i, r.output, (r.residual[i] + ex_b.total(i)).astype(BF16)))
+    ex_a.finish(r.mlp_in, False)
+    ex_b.finish(r.output)
+    if layer == 0:
+
+        @pl.when(holder)
+        def _():
+            next_gather.finish()
+            for copy in come:
+                copy.wait_send()
+            for copy in next_feed:
+                copy.wait_recv()
+
+        @pl.when(taker)
+        def _():
+            next_packed.wait_send()
+            for copy in next_feed:
+                copy.wait_send()
+    else:
+        pl.when(core == 0)(before.wait)
 
 
 def finish_kernel(groups, *refs):
@@ -720,7 +902,6 @@
         grad_copies.append(send_to(share[1], share[1], grad_sent.at[step], grad_here.at[team.place], peer))
         theirs = grad_far.at[place]
         grad_coming.append(send_to(theirs, theirs, grad_sent.at[step], grad_here.at[place], peer))
-    pl.when(first)(grad_copies[0].start)
     actives = [first] * 3 + [None] * 2
     gathers = [
         Gather(plane, k, outs[k], gather_sent.at[k], gather_here.at[k], actives[k]) for k in range(5)
@@ -730,6 +911,10 @@
         outs[k][plane.me] = total
         gathers[k].first.start()
         gathers[k].second[0].start()
+
+    def arrive(k):
+        crosses[k].wait_recv()
+        return (sources[k][...].astype(F32) + come[k][...].astype(F32)).astype(BF16)
 
     for scatter in scatters:
         scatter.middle()
@@ -737,17 +922,12 @@
         leave[k][...] = scatter.total().astype(BF16)
         pl.when(second)(crosses[3 + k].start)
 
-    def arrive(k):
-        crosses[k].wait_recv()
-        return (sources[k][...].astype(F32) + come[k][...].astype(F32)).astype(BF16)
-
     @pl.when(first)
     def _():
-        for k in range(3):
-            spread(k, arrive(k))
-        grad_copies[0].wait_recv()
-        for copy in grad_copies[1:]:
-            copy.start()
+        spread(0, arrive(0))
+        grad_copies[0].start()
+        spread(1, arrive(1))
+        spread(2, arrive(2))
         spread(3, arrive(3))
         held[...] = arrive(4).reshape(held.shape)
 
@@ -766,6 +946,13 @@
         gather.middle()
     for step, chip in enumerate(chips):
         block(step, chip, chip).wait_recv()
+
+    @pl.when(first)
+    def _():
+        grad_copies[0].wait_recv()
+        for copy in grad_copies[1:]:
+            copy.start()
+
     shares = [slots[shard].astype(F32) for shard in range(count)]
     sums = [sum(s for s, g in zip(shares, groups) if g == group) for group in range(KVH)]
     gain_rows = sums[0]
@@ -822,46 +1009,75 @@
     return block.reshape(PIECES, 2, block.shape[0] // PIECES // 2, block.shape[1])
 
 
-def attend_layer(source, weights):
-    w_query, w_key_up, w_value_up, w_out, w_latent, gain_attn, gain_mlp = weights
-    attn_in = (rms_scale(source.astype(F32)) * gain_attn).astype(BF16)
-    queries = mm(attn_in, w_query).astype(BF16)
-    latents = mm(attn_in, w_latent).astype(BF16)
-    keys = mm(latents, w_key_up).astype(BF16)
-    values = mm(latents, w_value_up).astype(BF16)
-    heads_out, norms = attend_forward(queries, keys, values)
-    return source, attn_in, queries, latents, keys, values, heads_out, norms
-
-
 def shapes_of(rows, model):
     return (PIECES, 2, rows // PIECES // 2, model), (PIECES, rows // PIECES // 2, model)
 
 
-def project_layer(number, kept, weights, pieces=(), core=1):
-    source, heads_out = kept[0], kept[6]
+def forward_layer(layer, number, source, ins, far):
     rows, model = source.shape
     split, own = shapes_of(rows, model)
-    residual, mlp_in, *wholes = team_call(
-        project_out, number, model, [(own, F32), (split, BF16)],
-        (heads_out, weights[3], pieces_of(source), weights[6][None]),
-        pieces=pieces, core=core,
-    )
-    return residual, mlp_in.reshape(rows, model), [whole_of(w) for w in wholes]
-
-
-def feed_layer(number, layer, residual, mlp_in, own, far, pieces=()):
-    rows, model = mlp_in.shape
-    wide = (rows, own[0].shape[0])
-    gate, up, hidden, output, *wholes = team_call(
-        functools.partial(feed_forward, layer), number, model,
-        [(wide, F32), (wide, F32), (wide, BF16), (shapes_of(rows, model)[0], BF16)],
-        (mlp_in, residual, *own, *far),
-        scratch=weights_scratch(own), pieces=pieces, core=0, far=6,
-    )
-    return output.reshape(rows, model), (gate, up, hidden), [whole_of(w) for w in wholes]
-
-
-def feed_layer_back(number, layer, upstream, feed_kept, residual, mlp_in, gain, own, far, loads=()):
+    packed = ins[dict_key(ins, 0)]
+    pieces, depth, width = packed.shape
+    feed = far[dict_key(far, 0)]
+    wide = (rows, pieces * feed[0].shape[1])
+    pair = min(2 * HD, width)
+    narrow = ((rows, width), BF16)
+    outs = dict(
+        attn_in=((rows, model), BF16),
+        queries=narrow,
+        latents=((rows, LH), BF16),
+        keys=narrow,
+        values=narrow,
+        heads_out=narrow,
+        norms=((width // pair, pair // HD, rows), F32),
+        residual=(own, F32),
+        mlp_in=(split, BF16),
+        gate=(wide, F32),
+        up=(wide, F32),
+        hidden=(wide, BF16),
+        output=(split, BF16),
+        w_latent=((model, LH), BF16),
+        gains=((2, model), F32),
+        feed=[(w.shape, BF16) for w in feed],
+    )
+    scratch = dict(
+        ex_a=exchange_scratch(rows, model),
+        ex_b=exchange_scratch(rows, model),
+        own_sem=DMA((3,)),
+        gather_sent=DMA((3, 3)),
+        gather_here=DMA((3, pieces)),
+        cross_sent=DMA((8,)),
+        cross_here=DMA((8,)),
+    )
+    if layer == 0:
+        outs.update(
+            packed=(packed.shape, BF16),
+            far_latent=((model, LH), BF16),
+            far_gains=((2, model), F32),
+            packed_next=(packed.shape, BF16),
+            feed_next=[(w.shape[1:], BF16) for w in feed],
+        )
+        scratch.update(
+            come=[pltpu.VMEM(w.shape[1:], BF16) for w in feed],
+            small_sent=DMA((2,)),
+            small_here=DMA((2,)),
+            packed_sent=DMA((3,)),
+            packed_here=DMA((pieces,)),
+            next_sent=DMA((3,)),
+            next_here=DMA((pieces,)),
+        )
+    else:
+        outs.update(before_far=((rows, model), BF16, True))
+        scratch.update(before_sent=DMA, before_here=DMA)
+    ins = dict(source=pieces_of(source), **ins)
+    return named_call(functools.partial(forward_kernel, layer), number, ins, far, outs, scratch)
+
+
+def dict_key(group, index):
+    return list(group)[index]
+
+
+def feed_layer_back(number, layer, upstream, feed_kept, residual, mlp_in, gain, own, far, beside=None):
     rows, model = upstream.shape
     split, half = shapes_of(rows, model)
     wide = pltpu.VMEM((rows, own[0].shape[0]), BF16)
@@ -869,7 +1085,7 @@
     d_residual, res_grad, gain_grad, *grads = team_call(
         functools.partial(feed_back, layer), number, model, outs,
         (pieces_of(upstream), *feed_kept, mlp_in, residual, gain[None], *own, *far),
-        scratch=[wide, wide] + weights_scratch(own), loads=loads, far=6,
+        scratch=[wide, wide] + weights_scratch(own), beside=beside, far=6,
     )
     res_grad = res_grad.reshape(rows, model)
     return d_residual, res_grad, gain_grad, [by_dp(g) for g in grads[:3]], grads[3:]
@@ -887,7 +1103,7 @@
     return jnp.concatenate([rows, gains], axis=2).reshape(pieces, count * (depth + GAIN_ROWS), LH)
 
 
-def attend_layer_back(number, kept, d_residual, res_grad, gain_mlp_grad, weights, loads=(), pieces=()):
+def attend_layer_back(number, kept, d_residual, res_grad, gain_mlp_grad, weights, beside):
     w_query, w_key_up, w_value_up, w_out, w_latent, gain_attn, gain_mlp = weights
     source, attn_in, queries, latents, keys, values, heads_out, norms = kept
     rows, model = source.shape
@@ -900,11 +1116,10 @@
         [(shapes_of(rows, model)[0], BF16), ((1, model), F32), (packed, BF16), (w_latent.shape, BF16)],
         (d_queries, d_latents, w_query, w_latent, pieces_of(source), d_residual, gain_attn[None], attn_in,
          heads_out, res_grad, latents, d_keys, d_values),
-        loads=loads, pieces=pieces, core=1,
+        beside=beside,
     )
     parts = [by_dp(grads), latent_parts(g_latent, gain_grad, gain_mlp_grad)]
-    sums, wholes = rest[: len(loads)], rest[len(loads) :]
-    return input_grad.reshape(rows, model), parts, sums, [whole_of(w) for w in wholes]
+    return input_grad.reshape(rows, model), parts, rest
 
 
 def tie(*arrays):
@@ -937,71 +1152,75 @@
     def latent_of(shard):
         return lax.dynamic_slice_in_dim(w_latent[0], group_of(shard) * LH, LH, 1)
 
-    def dp_piece(matrix):
-        rows = matrix.shape[0] // lax.axis_size(DP)
-        return lax.dynamic_slice_in_dim(matrix, at.dp * rows, rows, 0)
-
     def sequence_rows(block):
         return lax.dynamic_slice_in_dim(block, at.sequence * LEN, LEN, 0)
 
-    own_feed = (w_gate[0].T, w_up[0].T, w_down[0])
-    own_packed = pack_attention(w_query[0], w_key_up[0], w_value_up[0], w_out[0])
+    own_feed = [by_dp(w) for w in (w_gate[0].T, w_up[0].T, w_down[0])]
+    own_packed = by_dp(pack_attention(w_query[0], w_key_up[0], w_value_up[0], w_out[0]))
     own_gains = jnp.concatenate([norm_attn, norm_mlp], axis=0)
     own_latent = latent_of(at.z)
-    feed_zero = [at.across(dp_piece(w), 0) for w in own_feed]
-    packed_zero, far_latent, far_gains = fetch(by_dp(own_packed), latent_of(opposite_z), own_gains)
-
-    def attention_weights(mine, far_packed):
-        packed = jnp.where(mine, own_packed, far_packed)
-        gains = jnp.where(mine, own_gains, far_gains)
-        latent = jnp.where(mine, own_latent, far_latent)
-        return unpack_attention(packed, model) + (latent, gains[0], gains[1])
-
-    weights_zero = attention_weights(at.first, whole_of(packed_zero))
-    kept_zero = attend_layer(sequence_rows(inputs), weights_zero)
-    heads_out, own_packed, *feed_zero = tie(kept_zero[6], own_packed, *feed_zero)
-    kept_zero = kept_zero[:6] + (heads_out,) + kept_zero[7:]
-    packed_one = at.across(dp_piece(own_packed), 1)
-    residual_zero, mlp_zero, far_zero = project_layer(0, kept_zero, weights_zero, feed_zero)
-    residual_zero, packed_one, *late_feed = tie(residual_zero, packed_one, *own_feed)
-    feed_one = [at.across(dp_piece(w), 1) for w in late_feed]
-    first_out, feed_kept_zero, (packed_one,) = feed_layer(
-        1, 0, residual_zero, mlp_zero, own_feed, far_zero, [packed_one]
-    )
-
-    weights_one = attention_weights(jnp.logical_not(at.first), packed_one)
-    kept_one = attend_layer(first_out, weights_one)
-    heads_out, *feed_one = tie(kept_one[6], *feed_one)
-    kept_one = kept_one[:6] + (heads_out,) + kept_one[7:]
-    residual_one, mlp_one, far_one = project_layer(2, kept_one, weights_one, feed_one, 0)
-    second_out, feed_kept_one, _ = feed_layer(3, 1, residual_one, mlp_one, own_feed, far_one)
+    zero = forward_layer(
+        0,
+        0,
+        sequence_rows(inputs),
+        dict(own_packed=own_packed, own_gains=own_gains, own_latent=own_latent, pass_latent=latent_of(opposite_z)),
+        dict(own_feed=own_feed),
+    )
+    first_out = zero.output.reshape(LEN, model)
+    one = forward_layer(
+        1,
+        1,
+        first_out,
+        dict(
+            packed=zero.packed_next,
+            own_gains=own_gains,
+            far_gains=zero.far_gains,
+            own_latent=own_latent,
+            far_latent=zero.far_latent,
+            pieces=zero.feed_next,
+        ),
+        dict(own_feed=own_feed, before=first_out),
+    )
+    second_out = one.output.reshape(LEN, model)
+    first_far = one.before_far
+
+    def attention_weights(packed, result):
+        return unpack_attention(whole_of(packed), model) + (result.w_latent, result.gains[0], result.gains[1])
+
+    def kept_of(source, result):
+        attention = (source, result.attn_in, result.queries, result.latents, result.keys, result.values)
+        attention = attention + (result.heads_out, result.norms)
+        return attention, (result.gate, result.up, result.hidden), [whole_of(w) for w in result.feed]
+
+    weights_zero = attention_weights(zero.packed, zero)
+    weights_one = attention_weights(zero.packed_next, one)
+    kept_zero, feed_kept_zero, far_zero = kept_of(sequence_rows(inputs), zero)
+    kept_one, feed_kept_one, far_one = kept_of(first_out, one)
+    residual_zero, mlp_zero = zero.residual, zero.mlp_in.reshape(LEN, model)
+    residual_one, mlp_one = one.residual, one.mlp_in.reshape(LEN, model)
 
     d_residual, res_grad, mlp_gain, feed_one, _ = feed_layer_back(
-        4, 1, sequence_rows(out_grad), feed_kept_one, residual_one, mlp_one, weights_one[6], own_feed, far_one
-    )
-    layer_mine, d_residual = tie(jnp.where(at.first, first_out, second_out), d_residual)
-    layer_far = at.opposite(layer_mine)
-    second_grad, late_one, feed_one, _ = attend_layer_back(
-        5, kept_one, d_residual, res_grad, mlp_gain, weights_one, feed_one
-    )
-    feed_cross = [at.across(part, 0) for part in feed_one]
-    upstream, layer_far = tie(second_grad, layer_far)
-    d_residual, res_grad, mlp_gain, feed_zero, late_one = feed_layer_back(
-        6, 0, upstream, feed_kept_zero, residual_zero, mlp_zero, weights_zero[6], own_feed, far_zero, late_one
-    )
-    d_residual, second_grad, *feed_cross = tie(d_residual, second_grad, *feed_cross)
-    grad_far = at.opposite(second_grad, (1,))
-
-    def total(mine, other):
-        return (mine.astype(F32) + other.astype(F32)).astype(BF16)
-
-    feed_one = [total(mine, other) for mine, other in zip(feed_one, feed_cross)]
-    late_cross = [at.across(part, 0) for part in late_one]
-    first_grad, late_zero, feed_zero, wide_one = attend_layer_back(
-        7, kept_zero, d_residual, res_grad, mlp_gain, weights_zero, feed_zero, feed_one
-    )
-    first_grad, grad_far, *late_cross = tie(first_grad, grad_far, *late_cross)
-    late_one = [total(mine, other) for mine, other in zip(late_one, late_cross)]
+        4, 1, sequence_rows(out_grad), feed_kept_one, residual_one, mlp_one, weights_one[6], far_one, far_one
+    )
+    second_sent, d_residual = tie(second_out, d_residual)
+    second_far = at.opposite(second_sent, (1,))
+    second_grad, late_one, feed_one = attend_layer_back(
+        5, kept_one, d_residual, res_grad, mlp_gain, weights_one, Beside(loads=feed_one)
+    )
+    upstream, second_far = tie(second_grad, second_far)
+    beside = Beside(loads=late_one, crosses=feed_one, sender=0, add=True)
+    d_residual, res_grad, mlp_gain, feed_zero, rest = feed_layer_back(
+        6, 0, upstream, feed_kept_zero, residual_zero, mlp_zero, weights_zero[6], far_zero, far_zero, beside
+    )
+    late_one, feed_one = rest[:2], rest[2:]
+    d_residual, second_sent = tie(d_residual, second_grad)
+    grad_far = at.opposite(second_sent, (1,))
+    beside = Beside(loads=feed_zero, pieces=feed_one, core=1, crosses=late_one, sender=0, add=True)
+    first_grad, late_zero, rest = attend_layer_back(
+        7, kept_zero, d_residual, res_grad, mlp_gain, weights_zero, beside
+    )
+    feed_zero, wide_one, late_one = rest[:3], [whole_of(w) for w in rest[3:6]], rest[6:]
+    first_grad, grad_far = tie(first_grad, grad_far)
     groups = tuple(group_of(shard) for shard in range(at.count))
     shared = first_grad.reshape(at.team, first_grad.shape[0] // at.team, model)
     *wide_zero, packed, latent, first_grad_far = finish(groups, feed_zero, late_zero, late_one, shared)
@@ -1011,7 +1230,9 @@
         both = lax.dynamic_update_slice_in_dim(both, mine[None], at.sequence, 0)
         return both.reshape(1, 2 * other.shape[0], model)
 
-    layer_out = both_sequences(layer_mine, layer_far)
+    layer_out = both_sequences(
+        jnp.where(at.first, first_out, second_out), jnp.where(at.first, first_far, second_far)
+    )
     input_grad = both_sequences(
         jnp.where(at.first, first_grad, second_grad),
         jnp.where(at.first, first_grad_far.reshape(first_grad.shape), grad_far),

time: 682 us -> 623 us (0.913)
  waiting for transfers between devices: 34 us -> 0.01 us
  starting transfers between devices: 34.6 us -> 2.96 us
  Pallas kernels: 527 us -> 557 us
  other arithmetic: 31.7 us -> 17.4 us
    pallas_call x11 -> x6, Pallas kernels: 417 us -> 447 us  [the longest x4 230 us: team_call(): pl.pallas_call(functools.partial(team_kernel, body, counts, beside.counts...]
    ppermute x12 -> x0, starting transfers between devices: 30 us -> none  [across(): return lax.ppermute(block, (SEC, TEN), route)]
    ppermute x2, waiting for transfers between devices: 20.8 us -> 0.01 us  [opposite(): return lax.ppermute(block, (SEC, TEN), route)]
    ppermute x12 -> x0, waiting for transfers between devices: 13.3 us -> none  [across(): return lax.ppermute(block, (SEC, TEN), route)]
    dynamic_slice x7 -> x0, local copies, waits for them, and re-layouts: 8.36 us -> none  [dp_piece(): return lax.dynamic_slice_in_dim(matrix, at.dp * rows, rows, 0)]
    dot_general x14 -> x6, matrix products: 14 us -> 9.25 us  [mm(): return lax.dot_general(left, right, dims, preferred_element_type=F32)]
  transfers between devices with their start and end apart: 14 -> 2, of which waited for: 4 -> 0; matrix products, arithmetic and copies ran while one was open for 5% -> 4% of each run, Pallas kernels for 39% -> 24%
where the time goes in v4:
time: 623 us; the launch traced here: 616 us
  Pallas kernels  557 us (89%)
  local copies, waits for them, and re-layouts  27.8 us (4%)
  other arithmetic  17.4 us (3%)
  matrix products  9.25 us (1%)
    pallas_call x4, Pallas kernels, team_call(): pl.pallas_call(functools.partial(team_kernel, body, counts, beside.counts...  230 us
    pallas_call x2, Pallas kernels, named_call(): pl.pallas_call(body, in_specs=specs, out_specs=[pl.BlockSpec(memory_space...  217 us
    pallas_call x1, Pallas kernels, finish(): pl.pallas_call(functools.partial(finish_kernel, groups), in_specs=[vmem]...  91.6 us
    pallas_call x2, Pallas kernels, attend_backward(): pl.pallas_call(attend_back_kernel, grid=(columns // width,), in_specs=[sp...  17.8 us
  transfers between devices with their start and end apart: 2, of which 0 were waited for; matrix products, arithmetic and copies ran while one was open for 4% of the time, Pallas kernels for 24%

profile of v4, /device:TPU:0, one launch (start us, length us, event | category | flops | bytes accessed | tf_op | source)
XLA Modules:
  0.0 615.7 jit_solution(16488225981689811735)
XLA Ops:
  4.8 4.7 constant_dynamic-slice_fusion
  9.5 112.9 %shard_map.211 = (bf16[1024,1024]{1,0:T(8,128)(2,1)}, bf16[1024,256]{1,0:T(8,128)(2,1)}, bf16[1024,256]{1,0:T(8,128)(2,1)}, bf16[1024,256]{1,0:T(8,128)(2,1)}, b...) custom-call(bf16[4,2,128,1024]{3,2,1,0:T(8,128)(2,1)} %bitcast.125, ...), custom_call_target="tpu_custom_call" | custom-call | flops 4000000000 | bytes 1048576 | tf_op jit(solution)/shard_map/pallas_call | solution.py:663
  122.4 104.3 %shard_map.212 = (bf16[1024,1024]{1,0:T(8,128)(2,1)}, bf16[1024,256]{1,0:T(8,128)(2,1)}, bf16[1024,256]{1,0:T(8,128)(2,1)}, bf16[1024,256]{1,0:T(8,128)(2,1)}, b...) custom-call(bf16[4,2,128,1024]{3,2,1,0:T(8,128)(2,1)} %get-tuple-ele, ...), custom_call_target="tpu_custom_call" | custom-call | flops 4000000000 | bytes 1048576 | tf_op jit(solution)/shard_map/pallas_call | solution.py:663
  226.7 1.4 fusion.32
  228.1 42.8 %shard_map.213 = (f32[4,128,1024]{2,1,0:T(8,128)}, bf16[4,2,128,1024]{3,2,1,0:T(8,128)(2,1)}, f32[1,1024]{1,0:T(1,128)}, bf16[704,1024]{1,0:T(8,128)(2,1)}, bf16...) custom-call(bf16[4,2,128,1024]{3,2,1,0:T(8,128)(2,1)} %bitcast.127, f32[1024,704]{1,0:T(8,128)} %get-tuple-element.124.refs_1_, ...), custom_call_target="tpu_custom_call" | custom-call | flops 4000000000 | bytes 1048576 | tf_op jit(solution)/shard_map/pallas_call | solution.py:553
  270.9 2.2 collective-permute-start
  274.7 1.9 convolution_convert_fusion.1.g_ref
  276.7 8.9 %shard_map.214 = (bf16[1024,256]{1,0:T(8,128)(2,1)S(1)}, bf16[1024,256]{1,0:T(8,128)(2,1)S(1)}, bf16[1024,256]{1,0:T(8,128)(2,1)S(1)}) custom-call(bf16[1024,256]{1,0:T(8,128)(2,1)S(1)} %copy-done.8, bf16[1024,256]{1,0:T(8,128)(2,1)S(1)} %copy-done.9, bf16[1024,256]{1,0:T(8,128)(2,1)S(1)} %copy-done.10, bf16[1024,256]{1,0:T(8,128)(2,1)S(1)} %copy-done.5, ...), custom_call_target="tpu_custom_call" | custom-call | flops 5368709120 | bytes 4194304 | tf_op jit(solution)/shard_map/pallas_call | solution.py:118
  287.1 61.4 %shard_map.215 = (bf16[4,2,128,1024]{3,2,1,0:T(8,128)(2,1)}, f32[1,1024]{1,0:T(1,128)}, bf16[2560,256]{1,0:T(8,128)(2,1)}, bf16[1024,256]{1,0:T(8,128)(2,1)}, bf...) custom-call(bf16[1024,256]{1,0:T(8,128)(2,1)} %copy-done.7, ...), custom_call_target="tpu_custom_call" | custom-call | flops 4000000000 | bytes 1048576 | tf_op jit(solution)/shard_map/pallas_call | solution.py:553
  350.3 2.0 slice.172.refs_2_
  355.0 1.5 broadcast_select_fusion
  356.5 57.4 %shard_map.216 = (f32[4,128,1024]{2,1,0:T(8,128)}, bf16[4,2,128,1024]{3,2,1,0:T(8,128)(2,1)}, f32[1,1024]{1,0:T(1,128)}, bf16[704,1024]{1,0:T(8,128)(2,1)}, bf16...) custom-call(bf16[4,2,128,1024]{3,2,1,0:T(8,128)(2,1)} %get-tuple-ele, ...), custom_call_target="tpu_custom_call" | custom-call | flops 4000000000 | bytes 1048576 | tf_op jit(solution)/shard_map/pallas_call | solution.py:553
  414.9 2.5 convolution_convert_fusion.g_ref
  417.4 8.9 %shard_map.217 = (bf16[1024,256]{1,0:T(8,128)(2,1)S(1)}, bf16[1024,256]{1,0:T(8,128)(2,1)S(1)}, bf16[1024,256]{1,0:T(8,128)(2,1)S(1)}) custom-call(bf16[1024,256]{1,0:T(8,128)(2,1)S(1)} %copy-done.11, bf16[1024,256]{1,0:T(8,128)(2,1)S(1)} %copy-done.12, bf16[1024,256]{1,0:T(8,128)(2,1)S(1)} %copy-done.13, bf16[1024,256]{1,0:T(8,128)(2,1)S(1)} %copy-done.4, ...), custom_call_target="tpu_custom_call" | custom-call | flops 5368709120 | bytes 4194304 | tf_op jit(solution)/shard_map/pallas_call | solution.py:118
  426.3 1.4 fusion.21
  427.7 2.0 fusion.3.refs_1_
  429.7 68.3 %shard_map.218 = (bf16[4,2,128,1024]{3,2,1,0:T(8,128)(2,1)}, f32[1,1024]{1,0:T(1,128)}, bf16[2560,256]{1,0:T(8,128)(2,1)}, bf16[1024,256]{1,0:T(8,128)(2,1)}, bf...) custom-call(bf16[1024,256]{1,0:T(8,128)(2,1)} %copy-done.6, ...), custom_call_target="tpu_custom_call" | custom-call | flops 4000000000 | bytes 1048576 | tf_op jit(solution)/shard_map/pallas_call | solution.py:553
  503.1 2.0 copy-done.21
  505.0 91.6 %shard_map.219 = (bf16[4,176,1024]{2,1,0:T(8,128)(2,1)}, bf16[4,176,1024]{2,1,0:T(8,128)(2,1)}, bf16[4,176,1024]{2,1,0:T(8,128)(2,1)}, bf16[4,640,256]{2,1,0:T(8...) custom-call(bf16[176,1024]{1,0:T(8,128)(2,1)} %get-tuple-element.190.refs_0_, ...), custom_call_target="tpu_custom_call" | custom-call | tf_op jit(solution)/shard_map/pallas_call | solution.py:993
  596.7 1.5 bitcast_convert_fusion.1
  601.2 1.9 bitcast_convert_fusion
  604.2 2.0 convert_bitcast_fusion
  607.1 2.0 convert_bitcast_fusion.1
  611.1 1.3 bitcast_dynamic-update-slice_fusion
  (128 shorter events, 27.0 us)
Async XLA Ops:
  0.7 2.4 copy-start.41
  0.7 3.1 copy-start.32
  3.0 6.5 %copy-start.35 = (bf16[2560,256]{1,0:T(8,128)(2,1)}, bf16[2560,256]{1,0:T(8,128)(2,1)S(1)}, u32[]{:S(2)}) copy-start(bf16[2560,256]{1,0:T(8,128)(2,1)S(1)} %slice_dynamic-update-slice_fusion) | copy-start | bytes 3932164
  228.1 45.0 %copy-start.31 = (bf16[4,640,256]{2,1,0:T(8,128)(2,1)S(1)}, bf16[4,640,256]{2,1,0:T(8,128)(2,1)}, u32[]{:S(2)}) copy-start(bf16[4,640,256]{2,1,0:T(8,128)(2,1)} %get-tuple-element.113.refs_1_) | copy-start | bytes 3932164
  270.9 3.8 copy-start.23
  270.9 85.6 %collective-permute-start = (bf16[1024,1024]{1,0:T(8,128)(2,1)}, bf16[1024,1024]{1,0:T(8,128)(2,1)}, u32[]{:S(2)}, u32[]{:S(2)}) collective-permute-start(bf16[1024,1024]{1,0:T(8,128)(2,1)} %bitcast.23), channel_id=1, source_target_pairs={{16,18},{17,19},{18,16},{19,17},{20,22},{21,23},{22,20},{23,21},{2... | collective-permute-start | bytes 6291464 | tf_op jit(solution)/shard_map/ppermute | solution.py:149
  287.1 62.1 %copy-start.39 = (f32[1,1024]{1,0:T(1,128)S(1)}, f32[1,1024]{1,0:T(1,128)}, u32[]{:S(2)}) copy-start(f32[1,1024]{1,0:T(1,128)} %get-tuple-element.167) | copy-start | bytes 12292
  349.2 4.0 copy-start.37
  350.3 4.7 copy-start.16
  356.5 57.5 %copy-start.19 = (bf16[4,2,128,1024]{3,2,1,0:T(8,128)(2,1)S(1)}, bf16[4,2,128,1024]{3,2,1,0:T(8,128)(2,1)}, u32[]{:S(2)}) copy-start(bf16[4,2,128,1024]{3,2,1,0:T(8,128)(2,1)} %get-tuple-element.147) | copy-start | bytes 6291460
  414.0 89.0 %collective-permute-start.1 = (bf16[1024,1024]{1,0:T(8,128)(2,1)S(1)}, bf16[1024,1024]{1,0:T(8,128)(2,1)S(1)}, u32[]{:S(2)}, u32[]{:S(2)}) collective-permute-start(bf16[1024,1024]{1,0:T(8,128)(2,1)S(1)} %bitcast.130), channel_id=1, source_target_pairs={{16,18},{17,19},{18,16},{19,17},{20,22},{21,23},{22,20},{23,21},{2... | collective-permute-start | bytes 6291464 | tf_op jit(solution)/shard_map/ppermute | solution.py:149
  414.8 2.5 copy-start.4
  414.8 2.5 copy-start.11
  414.8 2.5 copy-start.12
  414.8 2.5 copy-start.13
  414.8 2.5 copy-start.15
  426.3 3.4 copy-start
  426.3 3.4 copy-start.2
  426.3 3.4 copy-start.6
  429.7 69.2 %copy-start.38 = (f32[1,1024]{1,0:T(1,128)S(1)}, f32[1,1024]{1,0:T(1,128)}, u32[]{:S(2)}) copy-start(f32[1,1024]{1,0:T(1,128)} %get-tuple-element.196) | copy-start | bytes 12292
  498.1 2.9 copy-start.22
  601.2 2.8 copy-start.29
  604.2 2.7 copy-start.28
  612.4 3.1 copy-start.20
  (20 other events, 37.4 us)

commit v5 on v4

v5 whole, which is shorter than its diff:
```python
import functools
import math
import types

import jax
import jax.numpy as jnp
from jax import lax
from jax.experimental import pallas as pl
from jax.experimental.pallas import tpu as pltpu
from jax.sharding import PartitionSpec as P

QH = 16
HD = 64
KVH = 2
LH = 256
LEN = 1024
EPS = 1e-05
F32 = jnp.float32
BF16 = jnp.bfloat16
SEC, DP, TEN = "section", "dp", "tensor"
LOG2_SCALE = HD**-0.5 * math.log2(math.e)
KEY_ROWS = 256


def mm(left, right, left_dim=1, right_dim=0):
    dims = (((left_dim,), (right_dim,)), ((), ()))
    return lax.dot_general(left, right, dims, preferred_element_type=F32)


def head_masks(width):
    if width == HD:
        return [None]
    lane = lax.broadcasted_iota(jnp.int32, (1, width), 1)
    return [lane // HD == j for j in range(width // HD)]


def keep_head(block, mask):
    return block if mask is None else jnp.where(mask, block, jnp.zeros_like(block))


def attend_rows(start, q_ref, k_ref, v_ref, o_ref, norm_ref):
    columns = q_ref.shape[1]
    width = min(2 * HD, columns)
    masks = head_masks(width)
    rows = KEY_ROWS
    place_k = lax.broadcasted_iota(jnp.int32, (rows, rows), 0)
    place_q = lax.broadcasted_iota(jnp.int32, (rows, rows), 1)
    for pair in range(columns // width):
        lanes = slice(pair * width, (pair + 1) * width)
        query = q_ref[start : start + rows, lanes]
        total = None
        for j, mask in enumerate(masks):
            query_j = keep_head(query, mask)
            scores = mm(k_ref[start : start + rows, lanes], query_j, 1, 1) * LOG2_SCALE
            scores = jnp.where(place_k <= place_q, scores, -jnp.inf)
            largest = jnp.max(scores, axis=0, keepdims=True)
            if start:
                before = mm(k_ref[0:start, lanes], query_j, 1, 1) * LOG2_SCALE
                largest = jnp.maximum(largest, jnp.max(before, axis=0, keepdims=True))
            weight = jnp.exp2(scores - largest)
            norm = jnp.sum(weight, axis=0, keepdims=True)
            value = keep_head(v_ref[start : start + rows, lanes], mask)
            out = mm(value, weight.astype(BF16), 0, 0)
            if start:
                weight = jnp.exp2(before - largest)
                norm = norm + jnp.sum(weight, axis=0, keepdims=True)
                value = keep_head(v_ref[0:start, lanes], mask)
                out = out + mm(value, weight.astype(BF16), 0, 0)
            out = out / norm
            total = out if total is None else total + out
            norm_ref[pair, j : j + 1, start : start + rows] = largest + jnp.log2(norm)
        o_ref[start : start + rows, lanes] = total.T.astype(BF16)


def attend_rows_back(start, q_ref, k_ref, v_ref, o_ref, g_ref, norm_ref, dq_ref, key_total, value_total):
    columns = q_ref.shape[1]
    width = min(2 * HD, columns)
    masks = head_masks(width)
    rows = KEY_ROWS
    end = start + rows
    place_k = lax.broadcasted_iota(jnp.int32, (rows, rows), 0)
    place_q = lax.broadcasted_iota(jnp.int32, (rows, rows), 1)
    for pair in range(columns // width):
        lanes = slice(pair * width, (pair + 1) * width)
        query, grad = q_ref[start:end, lanes], g_ref[start:end, lanes]
        key, value = k_ref[0:end, lanes], v_ref[0:end, lanes]
        product = (grad.astype(F32) * o_ref[start:end, lanes].astype(F32)).T
        grad_query = grad_key = grad_value = None
        for j, mask in enumerate(masks):
            query_j = keep_head(query, mask)
            grad_j = keep_head(grad, mask)
            delta = jnp.sum(product[j * HD : (j + 1) * HD, :], axis=0, keepdims=True)
            scores = mm(key, query_j, 1, 1) * LOG2_SCALE
            probs = jnp.exp2(scores - norm_ref[pair, j : j + 1, start:end])
            last = jnp.where(place_k <= place_q, probs[start:], 0.0)
            probs = jnp.concatenate([probs[:start], last], axis=0) if start else last
            grad_probs = mm(value, grad_j, 1, 1)
            grad_scores = (probs * (grad_probs - delta)).astype(BF16)
            value_term = mm(probs.astype(BF16), grad_j)
            key_term = mm(grad_scores, query_j)
            query_term = mm(keep_head(key, mask), grad_scores, 0, 0)
            grad_key = key_term if grad_key is None else grad_key + key_term
            grad_value = value_term if grad_value is None else grad_value + value_term
            grad_query = query_term if grad_query is None else grad_query + query_term
        dq_ref[start:end, lanes] = (grad_query.T * HD**-0.5).astype(BF16)
        if end == LEN:
            key_total[:, lanes] = grad_key
            value_total[:, lanes] = grad_value
        else:
            key_total[0:end, lanes] += grad_key
            value_total[0:end, lanes] += grad_value


def rms_scale(features):
    return features * lax.rsqrt(jnp.mean(features * features, axis=-1, keepdims=True) + EPS)


class Place:
    def __init__(self):
        self.count = lax.axis_size(TEN)
        self.team = self.count // 2
        self.z = lax.axis_index(TEN)
        self.core = lax.axis_index(SEC)
        self.dp = lax.axis_index(DP)
        self.sequence = self.z // self.team
        self.first = self.core == 0

    def opposite(self, block, cores=(0, 1)):
        n, t = self.count, self.team
        route = [(core * n + z, core * n + (z + t) % n) for core in cores for z in range(n)]
        return lax.ppermute(block, (SEC, TEN), route)

    def across(self, block, core):
        n, t = self.count, self.team
        route = [(core * n + z, (1 - core) * n + (z + t) % n) for z in range(n)]
        return lax.ppermute(block, (SEC, TEN), route)


def pack_columns(matrix, width):
    return [matrix[:, i : i + width] for i in range(0, matrix.shape[1], width)]


def pack_attention(query, key_up, value_up, out):
    width = query.shape[1]
    return jnp.concatenate([query, key_up, value_up] + pack_columns(out, width), axis=0)


def by_dp(matrix):
    count = lax.axis_size(DP)
    return matrix.reshape(count, matrix.shape[0] // count, matrix.shape[1])


def whole_of(pieces):
    return pieces.reshape(-1, pieces.shape[2])


MESH = pl.DeviceIdType.MESH
PIECES = 4
VMEM_LIMIT = 58 * 2**20
LINK_FLOPS = 4 * 10**9
GAIN_ROWS = 16
FEED = 3
DMA = pltpu.SemaphoreType.DMA


def reciprocal_rms(features):
    return lax.rsqrt(jnp.mean(features * features, axis=-1, keepdims=True) + EPS)


def send_to(source, target, sent, here, device):
    return pltpu.make_async_remote_copy(
        src_ref=source,
        dst_ref=target,
        send_sem=sent,
        recv_sem=here,
        device_id=device,
        device_id_type=MESH,
    )


def greet(partners):
    barrier = pltpu.get_barrier_semaphore()
    for partner in partners:
        pl.semaphore_signal(barrier, inc=1, device_id=partner, device_id_type=MESH)
    pl.semaphore_wait(barrier, len(partners))


class Team:
    def __init__(self):
        count = lax.axis_size(TEN)
        self.size = count // 2
        self.core = lax.axis_index(SEC)
        z = lax.axis_index(TEN)
        self.place = lax.rem(z, self.size)
        self.base = z - self.place
        self.other = {SEC: 1 - self.core}

    def peer(self, step):
        place = lax.rem(self.place + step, self.size)
        return place, {TEN: self.base + place}

    def partners(self):
        return [self.other] + [self.peer(step)[1] for step in range(1, self.size)]


class Plane:
    def __init__(self):
        me = lax.axis_index(DP)
        self.me = me
        self.one = me + 1 - 2 * lax.rem(me, 2)
        self.two = lax.rem(me + 2, 4)
        self.both = lax.rem(self.one + 2, 4)

    def partners(self):
        return [{DP: self.one}, {DP: self.two}]

    def order(self, turn):
        return (self.one, self.two) if turn % 2 == 0 else (self.two, self.one)


def scatter_scratch(load):
    piece = load.shape[1:]
    return [pltpu.VMEM((3,) + piece, BF16), pltpu.VMEM((3,) + piece, BF16), DMA((3,)), DMA((3,)), DMA((2,))]


class Scatter:
    def __init__(self, plane, turn, load, slots, held, sent, here, local):
        near, far = plane.order(turn)
        self.slots, self.held = slots, held
        self.copies = [
            send_to(load.at[near], slots.at[0], sent.at[0], here.at[0], {DP: near}),
            send_to(load.at[plane.both], slots.at[1], sent.at[1], here.at[1], {DP: near}),
            send_to(held.at[2], slots.at[2], sent.at[2], here.at[2], {DP: far}),
        ]
        self.local = [
            pltpu.make_async_copy(load.at[plane.me], held.at[0], local.at[0]),
            pltpu.make_async_copy(load.at[far], held.at[1], local.at[1]),
        ]

    def start(self):
        self.copies[1].start()
        self.copies[0].start()
        for copy in self.local:
            copy.start()

    def middle(self):
        self.local[1].wait()
        self.copies[1].wait_recv()
        self.held[2] = (self.held[1].astype(F32) + self.slots[1].astype(F32)).astype(BF16)
        self.copies[2].start()

    def total(self):
        self.local[0].wait()
        self.copies[0].wait_recv()
        total = self.held[0].astype(F32) + self.slots[0].astype(F32)
        self.copies[2].wait_recv()
        return total + self.slots[2].astype(F32)

    def drain(self):
        for copy in self.copies:
            copy.wait_send()


class Gather:
    def __init__(self, plane, turn, whole, sent, here, active=None, piece=None, local=None):
        self.active = active
        near, far = plane.order(turn)
        me = plane.me
        source = whole.at[me] if piece is None else piece

        def copy(k, source, place, device):
            return send_to(source, whole.at[place], sent.at[k], here.at[place], {DP: device})

        self.first = copy(0, source, me, near)
        self.second = [copy(1, source, me, far), copy(2, whole.at[near], near, far)]
        self.coming = [copy(0, whole.at[place], place, near) for place in (near, far, plane.both)]
        self.local = [] if piece is None else [pltpu.make_async_copy(piece, whole.at[me], local)]

    def when(self, body):
        if self.active is None:
            body()
        else:
            pl.when(self.active)(body)

    def start(self):
        def body():
            for copy in [self.first, self.second[0]] + self.local:
                copy.start()

        self.when(body)

    def middle(self):
        def body():
            self.coming[0].wait_recv()
            self.second[1].start()

        self.when(body)

    def finish(self):
        def body():
            self.coming[1].wait_recv()
            self.coming[2].wait_recv()
            for copy in [self.first] + self.second:
                copy.wait_send()
            for copy in self.local:
                copy.wait()

        self.when(body)


def across_device():
    count = lax.axis_size(TEN)
    opposite = lax.rem(lax.axis_index(TEN) + count // 2, count)
    return {SEC: 1 - lax.axis_index(SEC), TEN: opposite}


class Beside:
    def __init__(self, loads=(), crosses=(), gathered=False, shares=(), spreads=()):
        team = lax.axis_size(TEN) // 2
        self.shared = [[core for _, core in group] for group in (shares, spreads)]
        shares, spreads = ([block for block, _ in group] for group in (shares, spreads))
        self.far = dict(loads=list(loads), crosses=list(crosses), shares=shares, spreads=spreads)
        pieces = [cross.shape for cross in crosses]
        dp = lax.axis_size(DP)
        self.outs = dict(
            sums=[(load.shape[1:], BF16) for load in loads], totals=[(piece, BF16) for piece in pieces]
        )
        self.far_outs = dict(
            wholes=[((dp,) + piece, BF16) for piece in pieces] if gathered else [],
            shares_here=[(block.shape[1:], BF16) for block in shares],
            spreads_here=[((team,) + block.shape, BF16) for block in spreads],
        )
        count = max(1, len(pieces))
        self.scratch = dict(
            scatter=[item for load in loads for item in scatter_scratch(load)],
            comes=[pltpu.VMEM(piece, BF16) for piece in pieces],
            cross_sems=[DMA((count,)), DMA((count,)), DMA((count,)), DMA((count,))],
            gather_sems=[DMA((count, 3)), DMA((count, dp))],
            share_sems=[DMA, DMA] * len(shares),
            spread_sems=[DMA((team,)), DMA((team,)), DMA] * len(spreads),
        )


class BesideRun:
    def __init__(self, r, plane, sender, shared):
        self.outputs = Outputs(r, shared)
        self.totals, self.comes, self.sums = r.totals, r.comes, r.sums
        self.scatters = [
            Scatter(plane, k, load, *r.scatter[5 * k : 5 * k + 5]) for k, load in enumerate(r.loads)
        ]
        self.sends = lax.axis_index(SEC) == sender
        self.takes = jnp.logical_not(self.sends)
        across = across_device()
        sent, here, own, local = r.cross_sems
        self.copies = [
            send_to(cross, r.comes[k], sent.at[k], here.at[k], across) for k, cross in enumerate(r.crosses)
        ]
        self.own = [pltpu.make_async_copy(cross, r.totals[k], own.at[k]) for k, cross in enumerate(r.crosses)]
        self.gathers = [
            Gather(
                plane, k, whole, r.gather_sems[0].at[k], r.gather_sems[1].at[k], self.takes, r.totals[k], local.at[k]
            )
            for k, whole in enumerate(r.wholes)
        ]
        self.partners = (plane.partners() if self.scatters or self.gathers else []) + (
            [across] if self.copies else []
        )
        self.partners = self.partners + self.outputs.partners

    def start(self):
        self.outputs.start()
        for scatter in self.scatters:
            scatter.start()
        for copy, own in zip(self.copies, self.own):
            pl.when(self.sends)(copy.start)
            own.start()

    def add(self):
        for own in self.own:
            own.wait()

        @pl.when(self.takes)
        def _():
            for copy, come, total in zip(self.copies, self.comes, self.totals):
                copy.wait_recv()
                total[...] = (total[...].astype(F32) + come[...].astype(F32)).astype(BF16)

    def middle(self):
        for scatter in self.scatters:
            scatter.middle()
        if self.gathers:
            self.add()
            for gather in self.gathers:
                gather.start()

    def late(self):
        for gather in self.gathers:
            gather.middle()

    def finish(self):
        for scatter, total in zip(self.scatters, self.sums):
            total[...] = scatter.total().astype(BF16)
            scatter.drain()
        if self.copies and not self.gathers:
            self.add()
        for gather in self.gathers:
            gather.finish()
        for copy in self.copies:
            pl.when(self.sends)(copy.wait_send)
        self.outputs.finish()


class Outputs:
    def __init__(self, r, shared):
        team = Team()
        core = lax.axis_index(SEC)
        opposite = {TEN: across_device()[TEN]}
        self.partners = [opposite] if r.shares else []
        self.items = []
        for k, block in enumerate(r.shares):
            copy = send_to(block.at[team.place], r.shares_here[k], *r.share_sems[2 * k : 2 * k + 2], opposite)
            self.items.append((core == shared[0][k], [copy], [copy], []))
        for k, block in enumerate(r.spreads):
            sent, here, own = r.spread_sems[3 * k : 3 * k + 3]
            whole = r.spreads_here[k]
            local = pltpu.make_async_copy(block, whole.at[team.place], own)
            out, come = [], []
            for step in range(1, team.size):
                place, peer = team.peer(step)
                out.append(send_to(block, whole.at[team.place], sent.at[step], here.at[team.place], peer))
                come.append(send_to(block, whole.at[place], sent.at[step], here.at[place], peer))
            self.items.append((core == shared[1][k], out, come, [local]))

    def start(self):
        for active, out, _, local in self.items:

            @pl.when(active)
            def _():
                for copy in out + local:
                    copy.start()

    def finish(self):
        for active, out, come, local in self.items:

            @pl.when(active)
            def _():
                for copy in out:
                    copy.wait_send()
                for copy in come:
                    copy.wait_recv()
                for copy in local:
                    copy.wait()


def exchange_scratch(rows, model):
    team = lax.axis_size(TEN) // 2
    half = rows // PIECES // 2
    return [
        pltpu.VMEM((2, half, model), F32),
        pltpu.VMEM((PIECES, half, model), F32),
        pltpu.VMEM((PIECES, half, model), BF16),
        pltpu.VMEM((PIECES, half, model), BF16),
        pltpu.VMEM((team, PIECES, half, model), BF16),
        DMA((PIECES,)),
        DMA((PIECES,)),
        DMA((team, PIECES)),
        DMA((team, PIECES)),
        DMA((PIECES,)),
        DMA((PIECES,)),
    ]


EXCHANGE = 11


class Exchange:
    def __init__(self, team, refs):
        self.team = team
        (self.part, self.keep, self.out, self.got, self.far) = refs[:5]
        (self.core_sent, self.core_here, self.far_sent, self.far_here) = refs[5:9]
        (self.join_sent, self.join_here) = refs[9:]

    def core_copy(self, i):
        return send_to(
            self.out.at[i], self.got.at[i], self.core_sent.at[i], self.core_here.at[i], self.team.other
        )

    def far_copy(self, i, step, place):
        at = self.far.at[place, i]
        return send_to(
            at, at, self.far_sent.at[step, i], self.far_here.at[place, i], self.team.peer(step)[1]
        )

    def join_copy(self, i, whole):
        at = whole.at[i, self.team.core]
        return send_to(at, at, self.join_sent.at[i], self.join_here.at[i], self.team.other)

    def push(self, i, product):
        core = self.team.core
        self.part[...] = product.reshape(self.part.shape)
        self.out[i] = self.part[1 - core].astype(BF16)
        self.core_copy(i).start()
        self.keep[i] = self.part[core]

    def combine(self, i):
        self.core_copy(i).wait_recv()
        self.far[self.team.place, i] = (self.keep[i] + self.got[i].astype(F32)).astype(BF16)
        for step in range(1, self.team.size):
            self.far_copy(i, step, self.team.place).start()

    def send_all(self, product):
        def send(i):
            self.push(i, product(i))

            @pl.when(i > 0)
            def _():
                self.combine(i - 1)

        each_piece(send)
        self.combine(PIECES - 1)

    def total(self, i):
        for step in range(1, self.team.size):
            self.far_copy(i, step, self.team.peer(step)[0]).wait_recv()
        total = self.far[0, i].astype(F32)
        for place in range(1, self.team.size):
            total = total + self.far[place, i].astype(F32)
        return total

    def join(self, i, whole, half):
        whole[i, self.team.core] = half
        self.join_copy(i, whole).start()

    def finish(self, whole, coming=True):
        def drain(i):
            self.core_copy(i).wait_send()
            for step in range(1, self.team.size):
                self.far_copy(i, step, self.team.place).wait_send()
            self.join_copy(i, whole).wait_send()
            if coming:
                self.join_copy(i, whole).wait_recv()

        each_piece(drain)


def each_piece(body):
    lax.fori_loop(0, PIECES, lambda i, _: (body(i), 0)[1], 0)


def piece_rows(i, rows):
    size = rows // PIECES
    return pl.ds(pl.multiple_of(i * size, size), size)


def rms_back(block, gain, upstream):
    inverse = reciprocal_rms(block)
    normed = block * inverse
    scaled = upstream * gain
    grad = inverse * (scaled - normed * jnp.mean(scaled * normed, axis=-1, keepdims=True))
    return grad, jnp.sum(upstream * normed, axis=0, keepdims=True)


def feed_back(shared, r):
    team, plane = Team(), Plane()
    ex = Exchange(team, r.exchange)
    beside = BesideRun(r, plane, 0, shared)
    greet(team.partners() + beside.partners)
    beside.start()
    rows, model = r.mlp_in.shape
    size = rows // PIECES
    shape = (size, model)
    wide = (r.d_gate.shape[1], model)
    width = r.queries.shape[1]
    last = PIECES - 1
    upstream, gate, up, d_gate, d_up = r.upstream, r.gate, r.up, r.d_gate, r.d_up
    w_gate, w_up, w_down = r.feed
    r.ready(upstream, gate, up, *r.feed)

    def product(i):
        at = piece_rows(i, rows)
        grad_hidden = mm(upstream[i].reshape(shape), w_down[...].reshape(wide), 1, 1)
        gate_block = gate[at, :]
        sigmoid = jax.nn.sigmoid(gate_block)
        silu = gate_block * sigmoid
        d_gate_block = grad_hidden * up[at, :] * (sigmoid + silu * (1.0 - sigmoid))
        d_gate[at, :] = d_gate_block.astype(BF16)
        d_up[at, :] = (grad_hidden * silu).astype(BF16)
        term = mm(d_gate[at, :], w_gate[...].reshape(wide))
        return term + mm(d_up[at, :], w_up[...].reshape(wide))

    def send(step, _):
        i = last - step
        ex.push(i, product(i))

        @pl.when(step > 0)
        def _():
            ex.combine(i + 1)

        return 0

    lax.fori_loop(0, PIECES, send, 0)
    ex.combine(0)
    r.ready(r.mlp_in, r.hidden)
    g_gate, g_up, g_down = r.grads
    g_gate[...] = mm(d_gate[...], r.mlp_in[...], 0, 0).astype(BF16).reshape(g_gate.shape)
    g_up[...] = mm(d_up[...], r.mlp_in[...], 0, 0).astype(BF16).reshape(g_up.shape)
    g_down[...] = mm(r.hidden[...], upstream[...].reshape(rows, model), 0, 0).astype(BF16).reshape(g_down.shape)
    r.flush(*r.grads)
    beside.middle()
    r.ready(r.residual, r.packed, r.queries, r.keys, r.values, r.heads_out, r.norms)
    gain_grad, res_grad = r.gain_grad, r.res_grad
    gain_grad[...] = jnp.zeros_like(gain_grad)
    weights = r.packed[...].reshape(2 * model + 2 * LH, width)
    w_out = weights[model + 2 * LH :]

    def receive(i):
        part, gain_part = rms_back(r.residual[i], r.gain[...], ex.total(i))
        block = upstream[i, ex.team.core].astype(F32) + part
        r.d_residual[i] = block
        gain_grad[...] += gain_part
        ex.join(i, res_grad, block.astype(BF16))

    def attend(i):
        ex.join_copy(i, res_grad).wait_recv()
        at = slice(i * size, (i + 1) * size)
        block = res_grad[i].reshape(shape)
        total = None
        for j in range(model // width):
            columns = slice(j * width, (j + 1) * width)
            term = mm(block[:, columns], w_out[columns], 1, 1)
            total = term if total is None else total + term
        r.d_heads[at, :] = total.astype(BF16)
        attend_rows_back(
            i * size, r.queries, r.keys, r.values, r.heads_out, r.d_heads, r.norms,
            r.d_queries, r.key_total, r.value_total,
        )

    receive(last)
    for i in range(last, 0, -1):
        receive(i - 1)
        if i == 2:
            beside.late()
        attend(i)
    r.flush(r.d_residual)
    attend(0)
    ex.finish(res_grad, False)
    r.flush(res_grad, r.d_queries)
    r.d_keys[...] = (r.key_total[...] * HD**-0.5).astype(BF16)
    r.d_values[...] = r.value_total[...].astype(BF16)
    term = mm(r.d_keys[...], weights[model : model + LH], 1, 1)
    term = term + mm(r.d_values[...], weights[model + LH : model + 2 * LH], 1, 1)
    r.d_latents[...] = term.astype(BF16)
    r.flush(r.d_keys, r.d_values, r.d_latents)
    beside.finish()


def attend_in_back(shared, r):
    team, plane = Team(), Plane()
    ex = Exchange(team, r.exchange)
    beside = BesideRun(r, plane, 0, shared)
    greet(team.partners() + beside.partners)
    beside.start()
    rows, model = r.attn_in.shape
    width = r.d_queries.shape[1]
    r.ready(r.d_queries, r.d_latents, r.packed, r.w_latent)
    w_query = r.packed[...].reshape(2 * model + 2 * LH, width)[:model]

    def product(i):
        at = piece_rows(i, rows)
        return mm(r.d_queries[at, :], w_query, 1, 1) + mm(r.d_latents[at, :], r.w_latent[...], 1, 1)

    ex.send_all(product)
    r.ready(r.attn_in, r.latents, r.heads_out, r.d_keys, r.d_values, r.res_grad)
    half = model + LH
    grads = r.grads
    grads[0:model, :] = mm(r.attn_in[...], r.d_queries[...], 0, 0).astype(BF16)
    count, pieces = lax.axis_size(TEN), r.g_latent.shape[0]
    span = model // count
    depth = span // pieces
    stride = depth + GAIN_ROWS
    g_latent = mm(r.attn_in[...], r.d_latents[...], 0, 0).astype(BF16)
    for piece in range(pieces):
        for chip in range(count):
            start = chip * span + piece * depth
            r.g_latent[piece, chip * stride : chip * stride + depth, :] = g_latent[start : start + depth]
    grads[model:half, :] = mm(r.latents[...], r.d_keys[...], 0, 0).astype(BF16)
    grads[half : half + LH, :] = mm(r.latents[...], r.d_values[...], 0, 0).astype(BF16)
    g_out = mm(r.heads_out[...], r.res_grad[...].reshape(rows, model), 0, 0).astype(BF16)
    for j, block in enumerate(pack_columns(g_out, width)):
        start = half + LH + j * width
        grads[start : start + width, :] = block
    r.g_packed[0][...] = grads[:half].reshape(r.g_packed[0].shape)
    r.g_packed[1][...] = grads[half:].reshape(r.g_packed[1].shape)
    r.flush(*r.g_packed)
    beside.middle()
    r.ready(r.source, r.d_residual)
    r.gain_grad[...] = jnp.zeros_like(r.gain_grad)

    def receive(i):
        part, gain_part = rms_back(r.source[i, team.core].astype(F32), r.gain[...], ex.total(i))
        r.gain_grad[...] += gain_part
        ex.join(i, r.input_grad, (r.d_residual[i] + part).astype(BF16))

    each_piece(receive)
    place = lax.broadcasted_iota(jnp.int32, (GAIN_ROWS, LH), 0)
    nothing = jnp.zeros((GAIN_ROWS, LH), F32)
    for chip in range(count):
        columns = slice(chip * span, (chip + 1) * span)
        rows_of = slice(chip * stride + depth, (chip + 1) * stride)
        gains = [grad[:, columns] for grad in (r.gain_grad, r.mlp_gain)]
        if span < LH:
            gains = [jnp.concatenate([part, jnp.zeros((1, LH - span), F32)], axis=1) for part in gains]
        gains = jnp.where(place == 0, gains[0], jnp.where(place == 1, gains[1], nothing))
        r.g_latent[0, rows_of, :] = gains.astype(BF16)
        for piece in range(1, pieces):
            r.g_latent[piece, rows_of, :] = nothing.astype(BF16)
    r.flush(r.g_latent)
    beside.late()
    ex.finish(r.input_grad)
    r.flush(r.input_grad)
    beside.finish()


def named_call(kernel, number, ins=(), lazy=(), far=(), outs=(), late=(), far_outs=(), scratch=()):
    groups = [dict(group) for group in (ins, lazy, far, outs, late, far_outs, scratch)]

    def listed(group):
        return [(k, v if isinstance(v, list) else [v], isinstance(v, list)) for k, v in group.items()]

    groups = [listed(group) for group in groups]
    ins, lazy, far, outs, late, far_outs, scratch = groups
    vmem, anywhere = pl.BlockSpec(memory_space=pltpu.VMEM), pl.BlockSpec(memory_space=pl.ANY)

    def flat(*parts):
        return [value for part in parts for _, values, _ in part for value in values]

    stages = [pltpu.VMEM(x.shape, x.dtype) for x in flat(lazy)] + [pltpu.VMEM(*x) for x in flat(late)]
    lazy_count, late_count = len(flat(lazy)), len(flat(late))

    def body(*refs):
        refs = list(refs)

        def take(count):
            taken, refs[:] = refs[:count], refs[count:]
            return taken

        named = {}

        def name(part, taken):
            for key, values, is_list in part:
                mine, taken = taken[: len(values)], taken[len(values) :]
                named[key] = mine if is_list else mine[0]

        name(ins, take(len(flat(ins))))
        lazy_refs = take(lazy_count)
        name(far, take(len(flat(far))))
        name(outs, take(len(flat(outs))))
        late_refs = take(late_count)
        name(far_outs, take(len(flat(far_outs))))
        lazy_held, late_held = take(lazy_count), take(late_count)
        in_sem, out_sem = take(1)[0], take(1)[0]
        name(lazy, lazy_held)
        name(late, late_held)
        name(scratch, take(len(flat(scratch))))
        arrive = {
            id(held): pltpu.make_async_copy(ref, held, in_sem.at[k])
            for k, (ref, held) in enumerate(zip(lazy_refs, lazy_held))
        }
        leave = {
            id(held): pltpu.make_async_copy(held, ref, out_sem.at[k])
            for k, (ref, held) in enumerate(zip(late_refs, late_held))
        }
        for copy in arrive.values():
            copy.start()

        def ready(*buffers):
            for buffer in buffers:
                arrive[id(buffer)].wait()

        def flush(*buffers):
            for buffer in buffers:
                leave[id(buffer)].start()

        kernel(types.SimpleNamespace(ready=ready, flush=flush, **named))
        for copy in leave.values():
            copy.wait()

    results = pl.pallas_call(
        body,
        in_specs=[vmem] * len(flat(ins)) + [anywhere] * len(flat(lazy, far)),
        out_specs=[vmem] * len(flat(outs)) + [anywhere] * len(flat(late, far_outs)),
        out_shape=[jax.ShapeDtypeStruct(*x) for x in flat(outs, late, far_outs)],
        scratch_shapes=stages + [DMA((max(1, lazy_count),)), DMA((max(1, late_count),))] + flat(scratch),
        compiler_params=pltpu.CompilerParams(
            collective_id=number, has_side_effects=True, vmem_limit_bytes=VMEM_LIMIT
        ),
        cost_estimate=pl.CostEstimate(flops=LINK_FLOPS, bytes_accessed=2**20, transcendentals=0),
    )(*flat(ins, lazy, far))
    named, results = {}, list(results)
    for key, values, is_list in outs + late + far_outs:
        mine, results = results[: len(values)], results[len(values) :]
        named[key] = mine if is_list else mine[0]
    return types.SimpleNamespace(**named)


def forward_kernel(layer, r):
    team = Team()
    plane = Plane()
    core = lax.axis_index(SEC)
    holder = core == layer
    taker = jnp.logical_not(holder)
    across = across_device()
    ex_a, ex_b = Exchange(team, r.ex_a), Exchange(team, r.ex_b)
    greet(team.partners() + plane.partners() + [across])
    rows, width = r.queries.shape
    model = r.w_latent.shape[0]
    size = rows // PIECES
    feeds = range(3)

    own_copies = [pltpu.make_async_copy(r.own_feed[k], r.feed[k], r.own_sem.at[k]) for k in feeds]
    for copy in own_copies:
        pl.when(holder)(copy.start)
    gathers = [
        Gather(plane, k, r.feed[k], r.gather_sent.at[k], r.gather_here.at[k], taker) for k in feeds
    ]

    def cross(k, source, target):
        return send_to(source, target, r.cross_sent.at[k], r.cross_here.at[k], across)

    come = [cross(1 + k, r.own_feed[k].at[plane.me], r.come[k]) for k in feeds]
    if layer == 0:
        mine = cross(0, r.own_packed.at[plane.me], r.packed.at[plane.me])
        small = [
            send_to(r.pass_latent, r.far_latent, r.small_sent.at[0], r.small_here.at[0], team.other),
            send_to(r.own_gains, r.far_gains, r.small_sent.at[1], r.small_here.at[1], team.other),
        ]
        next_packed = cross(4, r.own_packed.at[plane.me], r.packed_next.at[plane.me])
        packed_gather = Gather(plane, 0, r.packed, r.packed_sent, r.packed_here)
        next_gather = Gather(plane, 1, r.packed_next, r.next_sent, r.next_here)
        own_packed = [
            pltpu.make_async_copy(r.own_packed, target, r.own_sem.at[3]) for target in (r.packed, r.packed_next)
        ]
        pl.when(holder)(mine.start)
        pl.when(holder)(own_packed[0].start)
        pl.when(taker)(own_packed[1].start)
        for copy in small:
            copy.start()
        for copy in small:
            copy.wait()
    else:

        @pl.when(holder)
        def _():
            for copy in come:
                copy.start()

    gains = jnp.where(holder, r.own_gains[...], r.far_gains[...])
    r.gains[...] = gains
    r.w_latent[...] = jnp.where(holder, r.own_latent[...], r.far_latent[...])
    r.flush(r.w_latent)
    r.ready(r.source)

    def norm(i):
        block = r.source[i].reshape(size, model).astype(F32)
        r.attn_in[piece_rows(i, rows), :] = (block * reciprocal_rms(block) * gains[0:1]).astype(BF16)

    each_piece(norm)
    r.flush(r.attn_in)
    if layer == 0:

        @pl.when(taker)
        def _():
            mine.wait_recv()
            packed_gather.start()
            packed_gather.middle()
            packed_gather.finish()

        @pl.when(holder)
        def _():
            own_packed[0].wait()
            mine.wait_send()
            for copy in come:
                copy.start()

        r.flush(r.packed)
    else:
        r.ready(r.packed)
    weights = r.packed[...].reshape(2 * model + 2 * LH, width)

    def project(i):
        at = piece_rows(i, rows)
        block = r.attn_in[at, :]
        r.queries[at, :] = mm(block, weights[:model]).astype(BF16)
        latents = mm(block, r.w_latent[...]).astype(BF16)
        r.latents[at, :] = latents
        r.keys[at, :] = mm(latents, weights[model : model + LH]).astype(BF16)
        r.values[at, :] = mm(latents, weights[model + LH : model + 2 * LH]).astype(BF16)

    each_piece(project)
    r.flush(r.queries, r.latents, r.keys, r.values)
    w_out = [
        weights[model + 2 * LH + start : model + 2 * LH + start + width] for start in range(0, model, width)
    ]
    for i in range(PIECES):
        attend_rows(i * size, r.queries, r.keys, r.values, r.heads_out, r.norms)
        heads = r.heads_out[i * size : (i + 1) * size, :]
        ex_a.push(i, jnp.concatenate([mm(heads, block) for block in w_out], axis=1))
        if i:
            ex_a.combine(i - 1)
    ex_a.combine(PIECES - 1)
    r.flush(r.heads_out, r.norms)
    if layer == 0:

        @pl.when(taker)
        def _():
            next_packed.start()

    @pl.when(taker)
    def _():
        for k in feeds:
            come[k].wait_recv()
            r.feed[k][plane.me] = r.come[k][...]

    for gather in gathers:
        gather.start()

    def receive(i):
        block = r.source[i, core].astype(F32) + ex_a.total(i)
        r.residual[i] = block
        ex_a.join(i, r.mlp_in, (block * reciprocal_rms(block) * gains[1:2]).astype(BF16))

    def feed(i):
        ex_a.join_copy(i, r.mlp_in).wait_recv()
        at = piece_rows(i, rows)
        block = r.mlp_in[i].reshape(size, model)
        shape = (r.hidden.shape[1], model)
        gate = mm(block, r.feed[0][...].reshape(shape), 1, 1)
        up = mm(block, r.feed[1][...].reshape(shape), 1, 1)
        hidden = (jax.nn.silu(gate) * up).astype(BF16)
        r.gate[at, :] = gate
        r.up[at, :] = up
        r.hidden[at, :] = hidden
        ex_b.push(i, mm(hidden, r.feed[2][...].reshape(shape)))

    receive(0)
    for gather in gathers:
        gather.middle()

    @pl.when(holder)
    def _():
        for copy in own_copies:
            copy.wait()

    for gather in gathers:
        gather.finish()
    r.flush(*r.feed)
    receive(1)
    feed(0)
    if layer == 0:

        @pl.when(holder)
        def _():
            next_packed.wait_recv()
            next_gather.start()

    def steady(i, _):
        receive(i)
        feed(i - 1)
        ex_b.combine(i - 2)
        return 0

    lax.fori_loop(2, PIECES, steady, 0)
    feed(PIECES - 1)
    ex_b.combine(PIECES - 2)
    ex_b.combine(PIECES - 1)
    ex_a.finish(r.mlp_in, False)
    r.flush(r.residual, r.mlp_in, r.gate, r.up, r.hidden)
    if layer == 0:

        @pl.when(holder)
        def _():
            next_gather.middle()
            next_gather.finish()

        @pl.when(taker)
        def _():
            own_packed[1].wait()
            next_packed.wait_send()

        r.flush(r.packed_next)
    each_piece(lambda i: ex_b.join(i, r.output, (r.residual[i] + ex_b.total(i)).astype(BF16)))
    ex_b.finish(r.output)
    r.flush(r.output)

    @pl.when(holder)
    def _():
        for copy in come:
            copy.wait_send()


def finish_kernel(groups, r):
    plane = Plane()
    team = Team()
    late = len(r.late)
    scatters = [Scatter(plane, k, r.late[k], *r.scatter[5 * k : 5 * k + 5]) for k in range(late)]
    count = lax.axis_size(TEN)
    z = lax.axis_index(TEN)
    core = lax.axis_index(SEC)
    first, second = core == 0, core == 1
    across = across_device()
    opposite = {TEN: across[TEN]}
    chips = [lax.rem(z + step, count) for step in range(1, count)]
    greet(plane.partners() + [across] + [{TEN: chip} for chip in chips])
    for scatter in scatters:
        scatter.start()
    sources = r.pieces + r.leave
    cross_sent, cross_here = r.cross_sems
    crosses = [
        send_to(source, r.come[k], cross_sent.at[k], cross_here.at[k], across) for k, source in enumerate(sources)
    ]

    @pl.when(second)
    def _():
        for copy in crosses[:FEED]:
            copy.start()

    grad_sent, grad_here = r.grad_sems
    share = r.grad.at[team.place], r.grad_far.at[team.place]
    grad_copies = [send_to(*share, grad_sent.at[0], grad_here.at[team.place], opposite)]
    grad_coming = []
    for step in range(1, team.size):
        place, peer = team.peer(step)
        grad_copies.append(send_to(share[1], share[1], grad_sent.at[step], grad_here.at[team.place], peer))
        theirs = r.grad_far.at[place]
        grad_coming.append(send_to(theirs, theirs, grad_sent.at[step], grad_here.at[place], peer))
    gather_sent, gather_here, gather_own = r.gather_sems
    gathers = [
        Gather(
            plane, k, whole, gather_sent.at[k], gather_here.at[k], first if k < FEED else None,
            r.total[k], gather_own.at[k],
        )
        for k, whole in enumerate(r.wholes)
    ]
    last = FEED + late - 1

    def arrive(k):
        crosses[k].wait_recv()
        return (sources[k][...].astype(F32) + r.come[k][...].astype(F32)).astype(BF16)

    for scatter in scatters:
        scatter.middle()

    @pl.when(first)
    def _():
        r.total[0][...] = arrive(0)

    gathers[0].start()
    for k, scatter in enumerate(scatters):
        r.leave[k][...] = scatter.total().astype(BF16)
        pl.when(second)(crosses[FEED + k].start)
    pl.when(first)(grad_copies[0].start)
    for k in range(1, FEED):

        @pl.when(first)
        def _():
            r.total[k][...] = arrive(k)

        gathers[k].start()
        gathers[k - 1].middle()
    gathers[FEED - 1].middle()

    @pl.when(first)
    def _():
        for k in range(FEED, last):
            r.total[k][...] = arrive(k)
        r.held[...] = arrive(last).reshape(r.held.shape)

    @pl.when(second)
    def _():
        for k in range(FEED, last):
            r.total[k][...] = r.done[k - FEED][...]
        r.held[...] = r.done[late - 1][...].reshape(r.held.shape)

    for k in range(FEED, last):
        gathers[k].start()
    block_sent, block_here = r.block_sems

    def block(step, chip, slot):
        return send_to(r.held.at[chip], r.slots.at[slot], block_sent.at[step], block_here.at[slot], {TEN: chip})

    for step, chip in enumerate(chips):
        block(step, chip, z).start()
    r.slots[z] = r.held[z]
    for step, chip in enumerate(chips):
        block(step, chip, chip).wait_recv()
    shares = [r.slots[shard].astype(F32) for shard in range(count)]
    sums = [sum(s for s, g in zip(shares, groups) if g == group) for group in range(KVH)]
    gain_rows = sums[0]
    for extra in sums[1:]:
        gain_rows = gain_rows + extra
    depth = gain_rows.shape[0] - GAIN_ROWS
    gain_rows = gain_rows * (2.0 / count)
    blocks = [jnp.concatenate([part[:depth], gain_rows[depth:]], axis=0) for part in sums]
    r.total[last][...] = jnp.concatenate(blocks, axis=1).astype(BF16)
    gathers[last].start()
    for k in range(FEED, last + 1):
        gathers[k].middle()

    @pl.when(first)
    def _():
        grad_copies[0].wait_recv()
        for copy in grad_copies[1:]:
            copy.start()

    for gather in gathers:
        gather.finish()
    for scatter in scatters:
        scatter.drain()
    for step, chip in enumerate(chips):
        block(step, chip, z).wait_send()

    @pl.when(second)
    def _():
        for copy in crosses:
            copy.wait_send()

    @pl.when(first)
    def _():
        for copy in grad_copies:
            copy.wait_send()
        for copy in grad_coming:
            copy.wait_recv()


def finish(number, groups, feed, late, done, grad):
    dp, count = lax.axis_size(DP), lax.axis_size(TEN)
    depth = done[-1].shape[0] // count
    shapes = [part.shape for part in list(feed) + list(done)]
    totals = shapes[:-1] + [(depth, KVH * LH)]
    items = len(shapes)
    blocks = pltpu.VMEM((count, depth, LH), BF16)
    return named_call(
        functools.partial(finish_kernel, groups),
        number,
        ins=dict(pieces=list(feed), done=list(done)),
        far=dict(late=list(late), grad=grad),
        far_outs=dict(wholes=[((dp,) + total, BF16) for total in totals], grad_far=(grad.shape, BF16)),
        scratch=dict(
            scatter=[item for load in late for item in scatter_scratch(load)],
            come=[pltpu.VMEM(shape, BF16) for shape in shapes],
            leave=[pltpu.VMEM(part.shape, BF16) for part in done],
            total=[pltpu.VMEM(total, BF16) for total in totals],
            slots=blocks,
            held=blocks,
            cross_sems=[DMA((items,)), DMA((items,))],
            gather_sems=[DMA((items, 3)), DMA((items, dp)), DMA((items,))],
            block_sems=[DMA((count,)), DMA((count,))],
            grad_sems=[DMA((count // 2,)), DMA((count // 2,))],
        ),
    )


def pieces_of(block):
    return block.reshape(PIECES, 2, block.shape[0] // PIECES // 2, block.shape[1])


def shapes_of(rows, model):
    return (PIECES, 2, rows // PIECES // 2, model), (PIECES, rows // PIECES // 2, model)


def forward_layer(layer, number, source, own_feed, own_packed=None, packed=None, **small):
    rows, model = source.shape
    split, own = shapes_of(rows, model)
    pieces, depth, width = (packed if own_packed is None else own_packed).shape
    wide = (rows, pieces * own_feed[0].shape[1])
    pair = min(2 * HD, width)
    narrow = ((rows, width), BF16)
    outs = dict(gains=((2, model), F32))
    late = dict(
        w_latent=((model, LH), BF16),
        attn_in=((rows, model), BF16),
        queries=narrow,
        latents=((rows, LH), BF16),
        keys=narrow,
        values=narrow,
        heads_out=narrow,
        norms=((width // pair, pair // HD, rows), F32),
        residual=(own, F32),
        mlp_in=(split, BF16),
        gate=(wide, F32),
        up=(wide, F32),
        hidden=(wide, BF16),
        output=(split, BF16),
        feed=[(w.shape, BF16) for w in own_feed],
    )
    scratch = dict(
        ex_a=exchange_scratch(rows, model),
        ex_b=exchange_scratch(rows, model),
        come=[pltpu.VMEM(w.shape[1:], BF16) for w in own_feed],
        own_sem=DMA((4,)),
        gather_sent=DMA((3, 3)),
        gather_here=DMA((3, pieces)),
        cross_sent=DMA((5,)),
        cross_here=DMA((5,)),
    )
    lazy, far = dict(source=pieces_of(source)), dict(own_feed=own_feed)
    if layer == 0:
        far.update(own_packed=own_packed)
        outs.update(far_latent=((model, LH), BF16), far_gains=((2, model), F32))
        late.update(packed=((pieces, depth, width), BF16), packed_next=((pieces, depth, width), BF16))
        scratch.update(
            small_sent=DMA((2,)),
            small_here=DMA((2,)),
            packed_sent=DMA((3,)),
            packed_here=DMA((pieces,)),
            next_sent=DMA((3,)),
            next_here=DMA((pieces,)),
        )
    else:
        lazy.update(packed=packed)
    return named_call(
        functools.partial(forward_kernel, layer),
        number,
        ins=small,
        lazy=lazy,
        far=far,
        outs=outs,
        late=late,
        scratch=scratch,
    )


def feed_layer_back(number, upstream, result, beside):
    rows, model = upstream.shape
    split, half = shapes_of(rows, model)
    columns = result.queries.shape[1]
    wide = pltpu.VMEM(result.hidden.shape, BF16)
    narrow = ((rows, columns), BF16)
    total = pltpu.VMEM((rows, columns), F32)
    return named_call(
        functools.partial(feed_back, beside.shared),
        number,
        ins=dict(gain=result.gains[1:2]),
        lazy=dict(
            upstream=pieces_of(upstream),
            feed=result.feed,
            gate=result.gate,
            up=result.up,
            mlp_in=result.mlp_in.reshape(rows, model),
            hidden=result.hidden,
            residual=result.residual,
            packed=result.packed,
            queries=result.queries,
            keys=result.keys,
            values=result.values,
            heads_out=result.heads_out,
            norms=result.norms,
        ),
        far=beside.far,
        outs=dict(gain_grad=((1, model), F32), **beside.outs),
        late=dict(
            d_residual=(half, F32),
            res_grad=(split, BF16),
            grads=[(w.shape, BF16) for w in result.feed],
            d_queries=narrow,
            d_keys=narrow,
            d_values=narrow,
            d_latents=((rows, LH), BF16),
        ),
        far_outs=beside.far_outs,
        scratch=dict(
            exchange=exchange_scratch(rows, model),
            d_gate=wide,
            d_up=wide,
            d_heads=pltpu.VMEM((rows, columns), BF16),
            key_total=total,
            value_total=total,
            **beside.scratch,
        ),
    )


def attend_layer_back(number, source, result, back, beside):
    rows, model = source.shape
    pieces, depth, width = result.packed.shape
    out = named_call(
        functools.partial(attend_in_back, beside.shared),
        number,
        ins=dict(gain=result.gains[0:1], mlp_gain=back.gain_grad),
        lazy=dict(
            d_queries=back.d_queries,
            d_latents=back.d_latents,
            packed=result.packed,
            w_latent=result.w_latent,
            attn_in=result.attn_in,
            latents=result.latents,
            heads_out=result.heads_out,
            d_keys=back.d_keys,
            d_values=back.d_values,
            res_grad=back.res_grad,
            source=pieces_of(source),
            d_residual=back.d_residual,
        ),
        far=beside.far,
        outs=beside.outs,
        late=dict(
            input_grad=(shapes_of(rows, model)[0], BF16),
            g_packed=[((pieces, depth // 2, width), BF16)] * 2,
            g_latent=((pieces, model // pieces + lax.axis_size(TEN) * GAIN_ROWS, LH), BF16),
        ),
        far_outs=beside.far_outs,
        scratch=dict(
            exchange=exchange_scratch(rows, model),
            grads=pltpu.VMEM((pieces * depth, width), BF16),
            gain_grad=pltpu.VMEM((1, model), F32),
            **beside.scratch,
        ),
    )
    out.parts = out.g_packed + [out.g_latent]
    out.input_grad = out.input_grad.reshape(rows, model)
    return out


def tie(*arrays):
    return lax.optimization_barrier(arrays)


def local(
    inputs,
    out_grad,
    w_query,
    w_latent,
    w_key_up,
    w_value_up,
    w_out,
    w_gate,
    w_up,
    w_down,
    norm_attn,
    norm_mlp,
):
    at = Place()
    model = inputs.shape[1]
    heads = w_query.shape[2] // HD

    def group_of(shard):
        return shard * heads // (QH // KVH)

    opposite_z = (at.z + at.team) % at.count

    def latent_of(shard):
        return lax.dynamic_slice_in_dim(w_latent[0], group_of(shard) * LH, LH, 1)

    def sequence_rows(block):
        return lax.dynamic_slice_in_dim(block, at.sequence * LEN, LEN, 0)

    own_feed = [by_dp(w) for w in (w_gate[0].T, w_up[0].T, w_down[0])]
    own_packed = by_dp(pack_attention(w_query[0], w_key_up[0], w_value_up[0], w_out[0]))
    own_gains = jnp.concatenate([norm_attn, norm_mlp], axis=0)
    own_latent = latent_of(at.z)
    source = sequence_rows(inputs)
    zero = forward_layer(
        0,
        0,
        source,
        own_feed,
        own_packed=own_packed,
        own_gains=own_gains,
        own_latent=own_latent,
        pass_latent=latent_of(opposite_z),
    )
    first_out = zero.output.reshape(LEN, model)
    one = forward_layer(
        1,
        1,
        first_out,
        own_feed,
        packed=zero.packed_next,
        own_gains=own_gains,
        far_gains=zero.far_gains,
        own_latent=own_latent,
        far_latent=zero.far_latent,
    )
    one.packed = zero.packed_next
    second_out = one.output.reshape(LEN, model)

    def shared(block):
        return block.reshape(at.team, LEN // at.team, model)

    back = feed_layer_back(2, sequence_rows(out_grad), one, Beside(shares=[(shared(first_out), 0)]))
    beside = Beside(back.grads, shares=[(shared(second_out), 1)], spreads=[(back.shares_here[0], 0)])
    above = attend_layer_back(3, first_out, one, back, beside)
    first_far = above.spreads_here[0]
    second_grad = above.input_grad
    beside = Beside(
        above.parts, above.sums, True, [(shared(second_grad), 1)], [(above.shares_here[0], 1)]
    )
    back = feed_layer_back(4, second_grad, zero, beside)
    wide_one = back.wholes
    second_far = back.spreads_here[0]
    beside = Beside(back.grads, back.sums, spreads=[(back.shares_here[0], 1)])
    below = attend_layer_back(5, source, zero, back, beside)
    grad_far = below.spreads_here[0]
    first_grad = below.input_grad
    first_far, second_far, grad_far = (far.reshape(LEN, model) for far in (first_far, second_far, grad_far))
    groups = tuple(group_of(shard) for shard in range(at.count))
    last = finish(6, groups, below.sums, below.parts, below.totals, shared(first_grad))
    *wide_zero, low_part, high_part, latent = last.wholes

    def both_sequences(mine, other):
        both = jnp.broadcast_to(other[None], (2,) + other.shape)
        both = lax.dynamic_update_slice_in_dim(both, mine[None], at.sequence, 0)
        return both.reshape(1, 2 * other.shape[0], model)

    layer_out = both_sequences(
        jnp.where(at.first, first_out, second_out), jnp.where(at.first, first_far, second_far)
    )
    input_grad = both_sequences(
        jnp.where(at.first, first_grad, second_grad),
        jnp.where(at.first, last.grad_far.reshape(first_grad.shape), grad_far),
    )
    g_gate, g_up, g_down = [
        jnp.where(at.first, whole_of(zero), whole_of(one)).astype(F32) for zero, one in zip(wide_zero, wide_one)
    ]
    low_part, high_part = whole_of(low_part).astype(F32), whole_of(high_part).astype(F32)
    g_query, g_key_up = low_part[:model], low_part[model:]
    g_value_up = high_part[:LH]
    columns = high_part.shape[1]
    g_out = [high_part[start : start + columns] for start in range(LH, LH + model, columns)]
    g_out = jnp.concatenate(g_out, axis=1)
    width = model // at.count
    depth = latent.shape[1] - GAIN_ROWS
    g_latent = latent[:, :depth].reshape(width, KVH * LH).astype(F32)
    gains = latent[0, depth : depth + 2, :width].astype(F32)
    return (
        layer_out,
        input_grad,
        g_query[None],
        g_latent[None],
        g_key_up[None],
        g_value_up[None],
        g_out[None],
        g_gate.T[None],
        g_up.T[None],
        g_down[None],
        gains[0:1],
        gains[1:2],
    )


def solution(mesh):
    columns = P(SEC, None, TEN)
    rows = P(SEC, TEN, None)
    return jax.shard_map(
        local,
        mesh=mesh,
        in_specs=(
            P(DP, None),
            P(DP, None),
            columns,
            P(SEC, None, None),
            columns,
            columns,
            rows,
            columns,
            columns,
            rows,
            P(SEC, None),
            P(SEC, None),
        ),
        out_specs=(
            P(SEC, DP, None),
            P(SEC, DP, None),
            columns,
            rows,
            columns,
            columns,
            rows,
            columns,
            columns,
            rows,
            P(SEC, TEN),
            P(SEC, TEN),
        ),
        check_vma=False,
    )
```

time: 623 us -> 559 us (0.90)
  Pallas kernels: 557 us -> 502 us
  matrix products: 9.25 us -> 0 us
    pallas_call x9 -> x7, Pallas kernels: 557 us -> 502 us  [named_call(): pl.pallas_call(body, in_specs=[vmem] * len(flat(ins)) + [anywhere] * len(...]
    dot_general x6 -> x0, matrix products: 9.25 us -> none  [mm(): return lax.dot_general(left, right, dims, preferred_element_type=F32)]
    unnamed x90 -> x50, local copies, waits for them, and re-layouts: 8.73 us -> 14.8 us
  transfers between devices with their start and end apart: 2 -> 0, of which waited for: 0 -> 0; matrix products, arithmetic and copies ran while one was open for 4% -> 0% of each run, Pallas kernels for 24% -> 0%
where the time goes in v5:
time: 559 us; the launch traced here: 551 us
  Pallas kernels  502 us (90%)
  local copies, waits for them, and re-layouts  30.2 us (5%)
  other arithmetic  16.7 us (3%)
    pallas_call x7, Pallas kernels, named_call(): pl.pallas_call(body, in_specs=[vmem] * len(flat(ins)) + [anywhere] * len(...  502 us
    unnamed x50, local copies, waits for them, and re-layouts  14.8 us

profile of v5, /device:TPU:0, one launch (start us, length us, event | category | flops | bytes accessed | tf_op | source)
XLA Modules:
  0.0 550.9 jit_solution(2349248488513452107)
XLA Ops:
  0.7 1.4 pad_maximum_fusion.refs_0_
  2.1 2.4 dynamic-slice_bitcast_fusion
  9.2 4.6 constant_dynamic-slice_fusion
  13.7 103.6 %shard_map.211 = (f32[2,1024]{1,0:T(2,128)}, bf16[1024,256]{1,0:T(8,128)(2,1)}, f32[2,1024]{1,0:T(2,128)}, bf16[1024,256]{1,0:T(8,128)(2,1)}, bf16[1024,1024]{1,...) custom-call(f32[2,1024]{1,0:T(2,128)} %pad_maximum_fusion.refs_0_, ...), custom_call_target="tpu_custom_call" | custom-call | flops 4000000000 | bytes 1048576 | tf_op jit(solution)/shard_map/pallas_call | solution.py:788
  117.4 1.4 fusion.1
  118.7 81.8 %shard_map.212 = (f32[2,1024]{1,0:T(2,128)}, bf16[1024,256]{1,0:T(8,128)(2,1)}, bf16[1024,1024]{1,0:T(8,128)(2,1)}, bf16[1024,256]{1,0:T(8,128)(2,1)}, bf16[1024...) custom-call(f32[2,1024]{1,0:T(2,128)} %pad_maximum_fusion.refs_0_, ...), custom_call_target="tpu_custom_call" | custom-call | flops 4000000000 | bytes 1048576 | tf_op jit(solution)/shard_map/pallas_call | solution.py:788
  200.5 1.4 fusion.2
  201.9 53.3 %shard_map.213 = (f32[1,1024]{1,0:T(1,128)}, f32[4,128,1024]{2,1,0:T(8,128)}, bf16[4,2,128,1024]{3,2,1,0:T(8,128)(2,1)}, bf16[4,176,1024]{2,1,0:T(8,128)(2,1)}, ...) custom-call(f32[1,1024]{1,0:T(1,128)} %get-tuple-element.213.refs_0_, ...), custom_call_target="tpu_custom_call" | custom-call | flops 4000000000 | bytes 1048576 | tf_op jit(solution)/shard_map/pallas_call | solution.py:788
  255.3 54.2 %shard_map.214 = (bf16[176,1024]{1,0:T(8,128)(2,1)}, bf16[176,1024]{1,0:T(8,128)(2,1)}, bf16[176,1024]{1,0:T(8,128)(2,1)}, bf16[4,2,128,1024]{3,2,1,0:T(8,128)(2...) custom-call(f32[1,1024]{1,0:T(1,128)} %get-tuple-element.214.refs_0_, ...), custom_call_target="tpu_custom_call" | custom-call | flops 4000000000 | bytes 1048576 | tf_op jit(solution)/shard_map/pallas_call | solution.py:788
  309.5 1.5 broadcast_select_fusion.1
  311.0 74.3 %shard_map.215 = (f32[1,1024]{1,0:T(1,128)}, bf16[320,256]{1,0:T(8,128)(2,1)}, bf16[320,256]{1,0:T(8,128)(2,1)}, bf16[320,256]{1,0:T(8,128)(2,1)}, bf16[176,1024...) custom-call(f32[1,1024]{1,0:T(1,128)} %get-tuple-element.212.refs_0_, ...), custom_call_target="tpu_custom_call" | custom-call | flops 4000000000 | bytes 1048576 | tf_op jit(solution)/shard_map/pallas_call | solution.py:788
  385.5 49.9 %shard_map.216 = (bf16[176,1024]{1,0:T(8,128)(2,1)}, bf16[176,1024]{1,0:T(8,128)(2,1)}, bf16[176,1024]{1,0:T(8,128)(2,1)}, bf16[320,256]{1,0:T(8,128)(2,1)}, bf1...) custom-call(f32[1,1024]{1,0:T(1,128)} %get-tuple-element.211.refs_0_, ...), custom_call_target="tpu_custom_call" | custom-call | flops 4000000000 | bytes 1048576 | tf_op jit(solution)/shard_map/pallas_call | solution.py:788
  435.4 3.1 broadcast_select_fusion
  439.1 1.1 copy-done.3
  440.4 2.0 copy-done.6
  442.5 85.4 %shard_map.217 = (bf16[4,176,1024]{2,1,0:T(8,128)(2,1)}, bf16[4,176,1024]{2,1,0:T(8,128)(2,1)}, bf16[4,176,1024]{2,1,0:T(8,128)(2,1)}, bf16[4,320,256]{2,1,0:T(8...) custom-call(bf16[176,1024]{1,0:T(8,128)(2,1)} %get-tuple-element.183.refs_0_, ...), custom_call_target="tpu_custom_call" | custom-call | flops 4000000000 | bytes 1048576 | tf_op jit(solution)/shard_map/pallas_call | solution.py:788
  527.9 1.7 broadcast_select_fusion.4
  530.3 1.2 copy-done.10
  532.1 1.4 copy-done.8
  539.5 1.1 maximum_bitcast_fusion
  540.6 2.0 convert_bitcast_fusion.1
  542.6 2.0 convert_bitcast_fusion
  544.6 1.9 bitcast_convert_fusion
  548.5 2.0 copy-done.5
  (63 shorter events, 14.8 us)
Async XLA Ops:
  0.6 3.8 copy-start.18
  0.7 3.8 copy-start.21
  2.1 7.1 %copy-start.15 = (bf16[2048,1024]{1,0:T(8,128)(2,1)S(1)}, bf16[2048,1024]{1,0:T(8,128)(2,1)}, u32[]{:S(2)}) copy-start(bf16[2048,1024]{1,0:T(8,128)(2,1)} %param.13) | copy-start | bytes 12582916
  9.2 4.6 copy-start.20
  255.3 54.2 %copy-start = (bf16[4,2,128,1024]{3,2,1,0:T(8,128)(2,1)S(1)}, bf16[4,2,128,1024]{3,2,1,0:T(8,128)(2,1)}, u32[]{:S(2)}) copy-start(bf16[4,2,128,1024]{3,2,1,0:T(8,128)(2,1)} %get-tuple-element.110.refs_4_.refs_12_) | copy-start | bytes 6291460
  255.3 54.2 %copy-start.2 = (bf16[4,2,128,1024]{3,2,1,0:T(8,128)(2,1)S(1)}, bf16[4,2,128,1024]{3,2,1,0:T(8,128)(2,1)}, u32[]{:S(2)}) copy-start(bf16[4,2,128,1024]{3,2,1,0:T(8,128)(2,1)} %get-tuple-element.139) | copy-start | bytes 6291460
  311.0 74.3 %copy-start.7 = (bf16[2,512,1024]{2,1,0:T(8,128)(2,1)S(1)}, bf16[2,512,1024]{2,1,0:T(8,128)(2,1)}, u32[]{:S(2)}) copy-start(bf16[2,512,1024]{2,1,0:T(8,128)(2,1)} %get-tuple-element.141) | copy-start | bytes 6291460
  385.5 49.9 %copy-start.1 = (bf16[4,2,128,1024]{3,2,1,0:T(8,128)(2,1)S(1)}, bf16[4,2,128,1024]{3,2,1,0:T(8,128)(2,1)}, u32[]{:S(2)}) copy-start(bf16[4,2,128,1024]{3,2,1,0:T(8,128)(2,1)} %get-tuple-element.143.refs_1_) | copy-start | bytes 6291460
  438.6 1.6 copy-start.3
  440.4 2.0 copy-start.6
  442.5 85.4 %copy-start.12 = (bf16[4,176,1024]{2,1,0:T(8,128)(2,1)S(1)}, bf16[4,176,1024]{2,1,0:T(8,128)(2,1)}, u32[]{:S(2)}) copy-start(bf16[4,176,1024]{2,1,0:T(8,128)(2,1)} %get-tuple-element.203) | copy-start | bytes 4325380
  527.9 1.8 copy-start.11
  527.9 2.2 copy-start.14
  530.1 1.4 copy-start.10
  530.1 1.8 copy-start.13
  531.9 1.6 copy-start.8
  531.9 2.2 copy-start.9
  534.1 1.0 copy-start.19
  534.4 2.2 copy-start.17
  536.7 1.8 copy-start.16
  546.6 1.6 copy-start.4
  548.5 2.0 copy-start.5

commit v6 on v5

--- a/solution.py
+++ b/solution.py
@@ -327,8 +327,8 @@
         )
         self.far_outs = dict(
             wholes=[((dp,) + piece, BF16) for piece in pieces] if gathered else [],
-            shares_here=[(block.shape[1:], BF16) for block in shares],
-            spreads_here=[((team,) + block.shape, BF16) for block in spreads],
+            shares_here=[(block.shape, BF16) for block in shares],
+            spreads_here=[(block.shape, BF16) for block in spreads],
         )
         count = max(1, len(pieces))
         self.scratch = dict(
@@ -336,8 +336,8 @@
             comes=[pltpu.VMEM(piece, BF16) for piece in pieces],
             cross_sems=[DMA((count,)), DMA((count,)), DMA((count,)), DMA((count,))],
             gather_sems=[DMA((count, 3)), DMA((count, dp))],
-            share_sems=[DMA, DMA] * len(shares),
-            spread_sems=[DMA((team,)), DMA((team,)), DMA] * len(spreads),
+            share_sems=[DMA((PIECES,))] * (2 * len(shares)),
+            spread_sems=[DMA((team, PIECES)), DMA((PIECES,))] * len(spreads),
         )
 
 
@@ -410,46 +410,46 @@
         self.outputs.finish()
 
 
+def owner(piece):
+    return piece * (lax.axis_size(TEN) // 2) // PIECES
+
+
 class Outputs:
     def __init__(self, r, shared):
         team = Team()
         core = lax.axis_index(SEC)
         opposite = {TEN: across_device()[TEN]}
         self.partners = [opposite] if r.shares else []
-        self.items = []
-        for k, block in enumerate(r.shares):
-            copy = send_to(block.at[team.place], r.shares_here[k], *r.share_sems[2 * k : 2 * k + 2], opposite)
-            self.items.append((core == shared[0][k], [copy], [copy], []))
-        for k, block in enumerate(r.spreads):
-            sent, here, own = r.spread_sems[3 * k : 3 * k + 3]
-            whole = r.spreads_here[k]
-            local = pltpu.make_async_copy(block, whole.at[team.place], own)
-            out, come = [], []
-            for step in range(1, team.size):
-                place, peer = team.peer(step)
-                out.append(send_to(block, whole.at[team.place], sent.at[step], here.at[team.place], peer))
-                come.append(send_to(block, whole.at[place], sent.at[step], here.at[place], peer))
-            self.items.append((core == shared[1][k], out, come, [local]))
+        self.out, self.come = [], []
+        for piece in range(PIECES):
+            mine = team.place == owner(piece)
+            for k, block in enumerate(r.shares):
+                sent, here = r.share_sems[2 * k : 2 * k + 2]
+                target = r.shares_here[k].at[piece]
+                copy = send_to(block.at[piece], target, sent.at[piece], here.at[piece], opposite)
+                active = jnp.logical_and(core == shared[0][k], mine)
+                self.out.append((active, copy))
+                self.come.append((active, copy))
+            for k, block in enumerate(r.spreads):
+                sent, here = r.spread_sems[2 * k : 2 * k + 2]
+                for step in range(1, team.size):
+                    copy = send_to(
+                        block.at[piece], r.spreads_here[k].at[piece], sent.at[step, piece], here.at[piece],
+                        team.peer(step)[1],
+                    )
+                    self.out.append((jnp.logical_and(core == shared[1][k], mine), copy))
+                theirs = jnp.logical_and(core == shared[1][k], jnp.logical_not(mine))
+                self.come.append((theirs, copy))
 
     def start(self):
-        for active, out, _, local in self.items:
-
-            @pl.when(active)
-            def _():
-                for copy in out + local:
-                    copy.start()
+        for active, copy in self.out:
+            pl.when(active)(copy.start)
 
     def finish(self):
-        for active, out, come, local in self.items:
-
-            @pl.when(active)
-            def _():
-                for copy in out:
-                    copy.wait_send()
-                for copy in come:
-                    copy.wait_recv()
-                for copy in local:
-                    copy.wait()
+        for active, copy in self.out:
+            pl.when(active)(copy.wait_send)
+        for active, copy in self.come:
+            pl.when(active)(copy.wait_recv)
 
 
 def exchange_scratch(rows, model):
@@ -654,11 +654,12 @@
     beside.finish()
 
 
-def attend_in_back(shared, r):
+def attend_in_back(shared, early, r):
     team, plane = Team(), Plane()
+    opposite = {TEN: across_device()[TEN]}
     ex = Exchange(team, r.exchange)
     beside = BesideRun(r, plane, 0, shared)
-    greet(team.partners() + beside.partners)
+    greet(team.partners() + beside.partners + ([opposite] if early else []))
     beside.start()
     rows, model = r.attn_in.shape
     width = r.d_queries.shape[1]
@@ -701,7 +702,19 @@
         r.gain_grad[...] += gain_part
         ex.join(i, r.input_grad, (r.d_residual[i] + part).astype(BF16))
 
-    each_piece(receive)
+    def leave(i):
+        ex.join_copy(i, r.input_grad).wait_recv()
+        if early:
+            copy = send_to(r.input_grad.at[i], r.grad_here.at[i], r.early_sems[0].at[i], r.early_sems[1].at[i], opposite)
+            copies.append((jnp.logical_and(team.core == 0, team.place == owner(i)), copy))
+            pl.when(copies[-1][0])(copy.start)
+
+    copies = []
+    receive(0)
+    for i in range(1, PIECES):
+        receive(i)
+        leave(i - 1)
+    leave(PIECES - 1)
     place = lax.broadcasted_iota(jnp.int32, (GAIN_ROWS, LH), 0)
     nothing = jnp.zeros((GAIN_ROWS, LH), F32)
     for chip in range(count):
@@ -716,9 +729,17 @@
             r.g_latent[piece, rows_of, :] = nothing.astype(BF16)
     r.flush(r.g_latent)
     beside.late()
-    ex.finish(r.input_grad)
+    ex.finish(r.input_grad, False)
     r.flush(r.input_grad)
     beside.finish()
+    for active, copy in copies:
+        pl.when(active)(copy.wait)
+
+
+class Part:
+    def __init__(self, block):
+        self.block = block.reshape((2,) + pieces_of(block[: block.shape[0] // 2]).shape)
+        self.shape, self.dtype = self.block.shape[1:], block.dtype
 
 
 def named_call(kernel, number, ins=(), lazy=(), far=(), outs=(), late=(), far_outs=(), scratch=()):
@@ -762,6 +783,9 @@
         name(lazy, lazy_held)
         name(late, late_held)
         name(scratch, take(len(flat(scratch))))
+        sequence = lax.axis_index(TEN) // (lax.axis_size(TEN) // 2)
+        parts = [isinstance(value, Part) for value in flat(lazy)]
+        lazy_refs = [ref.at[sequence] if part else ref for ref, part in zip(lazy_refs, parts)]
         arrive = {
             id(held): pltpu.make_async_copy(ref, held, in_sem.at[k])
             for k, (ref, held) in enumerate(zip(lazy_refs, lazy_held))
@@ -792,10 +816,10 @@
         out_shape=[jax.ShapeDtypeStruct(*x) for x in flat(outs, late, far_outs)],
         scratch_shapes=stages + [DMA((max(1, lazy_count),)), DMA((max(1, late_count),))] + flat(scratch),
         compiler_params=pltpu.CompilerParams(
-            collective_id=number, has_side_effects=True, vmem_limit_bytes=VMEM_LIMIT
+            collective_id=number, has_side_effects=number is not None, vmem_limit_bytes=VMEM_LIMIT
         ),
         cost_estimate=pl.CostEstimate(flops=LINK_FLOPS, bytes_accessed=2**20, transcendentals=0),
-    )(*flat(ins, lazy, far))
+    )(*[value.block if isinstance(value, Part) else value for value in flat(ins, lazy, far)])
     named, results = {}, list(results)
     for key, values, is_list in outs + late + far_outs:
         mine, results = results[: len(values)], results[len(values) :]
@@ -848,11 +872,21 @@
         for copy in small:
             copy.wait()
     else:
-
+        pl.when(holder)(come[0].start)
+
+    def next_come(k):
         @pl.when(holder)
         def _():
-            for copy in come:
-                copy.start()
+            come[k - 1].wait_send()
+            come[k].start()
+
+    def take_come(k):
+        @pl.when(taker)
+        def _():
+            come[k].wait_recv()
+            r.feed[k][plane.me] = r.come[k][...]
+
+        gathers[k].start()
 
     gains = jnp.where(holder, r.own_gains[...], r.far_gains[...])
     r.gains[...] = gains
@@ -864,9 +898,8 @@
         block = r.source[i].reshape(size, model).astype(F32)
         r.attn_in[piece_rows(i, rows), :] = (block * reciprocal_rms(block) * gains[0:1]).astype(BF16)
 
-    each_piece(norm)
-    r.flush(r.attn_in)
     if layer == 0:
+        each_piece(norm)
 
         @pl.when(taker)
         def _():
@@ -879,10 +912,10 @@
         def _():
             own_packed[0].wait()
             mine.wait_send()
-            for copy in come:
-                copy.start()
+            come[0].start()
 
         r.flush(r.packed)
+        take_come(0)
     else:
         r.ready(r.packed)
     weights = r.packed[...].reshape(2 * model + 2 * LH, width)
@@ -896,33 +929,38 @@
         r.keys[at, :] = mm(latents, weights[model : model + LH]).astype(BF16)
         r.values[at, :] = mm(latents, weights[model + LH : model + 2 * LH]).astype(BF16)
 
-    each_piece(project)
-    r.flush(r.queries, r.latents, r.keys, r.values)
     w_out = [
         weights[model + 2 * LH + start : model + 2 * LH + start + width] for start in range(0, model, width)
     ]
     for i in range(PIECES):
+        if layer == 1:
+            norm(i)
+        project(i)
         attend_rows(i * size, r.queries, r.keys, r.values, r.heads_out, r.norms)
         heads = r.heads_out[i * size : (i + 1) * size, :]
         ex_a.push(i, jnp.concatenate([mm(heads, block) for block in w_out], axis=1))
+        if i == layer:
+            next_come(1)
+        if i == 0 and layer == 1:
+            take_come(0)
         if i:
             ex_a.combine(i - 1)
+        if i == 1:
+            gathers[0].middle()
+        if i == 2:
+            next_come(2)
+            if layer == 0:
+                take_come(1)
     ex_a.combine(PIECES - 1)
-    r.flush(r.heads_out, r.norms)
+    if layer == 1:
+        take_come(1)
+    r.flush(r.attn_in, r.queries, r.latents, r.keys, r.values, r.heads_out, r.norms)
     if layer == 0:
 
         @pl.when(taker)
         def _():
             next_packed.start()
 
-    @pl.when(taker)
-    def _():
-        for k in feeds:
-            come[k].wait_recv()
-            r.feed[k][plane.me] = r.come[k][...]
-
-    for gather in gathers:
-        gather.start()
 
     def receive(i):
         block = r.source[i, core].astype(F32) + ex_a.total(i)
@@ -943,8 +981,10 @@
         ex_b.push(i, mm(hidden, r.feed[2][...].reshape(shape)))
 
     receive(0)
-    for gather in gathers:
-        gather.middle()
+    gathers[1].middle()
+    take_come(2)
+    receive(1)
+    gathers[2].middle()
 
     @pl.when(holder)
     def _():
@@ -954,7 +994,6 @@
     for gather in gathers:
         gather.finish()
     r.flush(*r.feed)
-    receive(1)
     feed(0)
     if layer == 0:
 
@@ -992,10 +1031,7 @@
     ex_b.finish(r.output)
     r.flush(r.output)
 
-    @pl.when(holder)
-    def _():
-        for copy in come:
-            copy.wait_send()
+    pl.when(holder)(come[2].wait_send)
 
 
 def finish_kernel(groups, r):
@@ -1019,20 +1055,16 @@
         send_to(source, r.come[k], cross_sent.at[k], cross_here.at[k], across) for k, source in enumerate(sources)
     ]
 
-    @pl.when(second)
-    def _():
-        for copy in crosses[:FEED]:
-            copy.start()
-
-    grad_sent, grad_here = r.grad_sems
-    share = r.grad.at[team.place], r.grad_far.at[team.place]
-    grad_copies = [send_to(*share, grad_sent.at[0], grad_here.at[team.place], opposite)]
-    grad_coming = []
-    for step in range(1, team.size):
-        place, peer = team.peer(step)
-        grad_copies.append(send_to(share[1], share[1], grad_sent.at[step], grad_here.at[team.place], peer))
-        theirs = r.grad_far.at[place]
-        grad_coming.append(send_to(theirs, theirs, grad_sent.at[step], grad_here.at[place], peer))
+    pl.when(second)(crosses[0].start)
+
+    def next_cross(k):
+        @pl.when(second)
+        def _():
+            crosses[k - 1].wait_send()
+            crosses[k].start()
+
+    outputs = Outputs(r, [[], [0]])
+    outputs.start()
     gather_sent, gather_here, gather_own = r.gather_sems
     gathers = [
         Gather(
@@ -1047,27 +1079,28 @@
         crosses[k].wait_recv()
         return (sources[k][...].astype(F32) + r.come[k][...].astype(F32)).astype(BF16)
 
-    for scatter in scatters:
-        scatter.middle()
-
-    @pl.when(first)
-    def _():
-        r.total[0][...] = arrive(0)
-
-    gathers[0].start()
-    for k, scatter in enumerate(scatters):
-        r.leave[k][...] = scatter.total().astype(BF16)
-        pl.when(second)(crosses[FEED + k].start)
-    pl.when(first)(grad_copies[0].start)
-    for k in range(1, FEED):
-
+    def take_cross(k):
         @pl.when(first)
         def _():
             r.total[k][...] = arrive(k)
 
         gathers[k].start()
-        gathers[k - 1].middle()
-    gathers[FEED - 1].middle()
+
+    scatters[0].middle()
+    next_cross(1)
+    take_cross(0)
+    for scatter in scatters[1:]:
+        scatter.middle()
+    for k, scatter in enumerate(scatters):
+        r.leave[k][...] = scatter.total().astype(BF16)
+        if k == 0:
+            next_cross(2)
+            gathers[0].middle()
+        pl.when(second)(crosses[FEED + k].start)
+    take_cross(1)
+    take_cross(2)
+    gathers[1].middle()
+    gathers[2].middle()
 
     @pl.when(first)
     def _():
@@ -1106,12 +1139,6 @@
     for k in range(FEED, last + 1):
         gathers[k].middle()
 
-    @pl.when(first)
-    def _():
-        grad_copies[0].wait_recv()
-        for copy in grad_copies[1:]:
-            copy.start()
-
     for gather in gathers:
         gather.finish()
     for scatter in scatters:
@@ -1121,15 +1148,10 @@
 
     @pl.when(second)
     def _():
-        for copy in crosses:
+        for copy in crosses[2:]:
             copy.wait_send()
 
-    @pl.when(first)
-    def _():
-        for copy in grad_copies:
-            copy.wait_send()
-        for copy in grad_coming:
-            copy.wait_recv()
+    outputs.finish()
 
 
 def finish(number, groups, feed, late, done, grad):
@@ -1143,8 +1165,8 @@
         functools.partial(finish_kernel, groups),
         number,
         ins=dict(pieces=list(feed), done=list(done)),
-        far=dict(late=list(late), grad=grad),
-        far_outs=dict(wholes=[((dp,) + total, BF16) for total in totals], grad_far=(grad.shape, BF16)),
+        far=dict(late=list(late), shares=[], spreads=[grad]),
+        far_outs=dict(wholes=[((dp,) + total, BF16) for total in totals], spreads_here=[(grad.shape, BF16)]),
         scratch=dict(
             scatter=[item for load in late for item in scatter_scratch(load)],
             come=[pltpu.VMEM(shape, BF16) for shape in shapes],
@@ -1155,12 +1177,104 @@
             cross_sems=[DMA((items,)), DMA((items,))],
             gather_sems=[DMA((items, 3)), DMA((items, dp)), DMA((items,))],
             block_sems=[DMA((count,)), DMA((count,))],
-            grad_sems=[DMA((count // 2,)), DMA((count // 2,))],
+            spread_sems=[DMA((count // 2, PIECES)), DMA((PIECES,))],
         ),
     )
 
 
+def emit_kernel(r):
+    core = lax.axis_index(SEC)
+    sequence = lax.axis_index(TEN) // (lax.axis_size(TEN) // 2)
+    placed = []
+    place = lax.rem(lax.axis_index(TEN), lax.axis_size(TEN) // 2)
+    for k, (mine, share, spread, out) in enumerate(
+        ((r.outs, r.outs_share, r.outs_spread, r.layer_out), (r.grads, r.grads_share, r.grads_spread, r.input_grad))
+    ):
+        for piece in range(PIECES):
+            passed = place == owner(piece)
+            for side, to in enumerate((sequence, 1 - sequence)):
+                at = (2 * k + side, piece)
+                held = r.held.at[at]
+                for layer in range(2):
+                    sources = [(mine, True)] if side == 0 else [(share, passed), (spread, jnp.logical_not(passed))]
+                    for blocks, active in sources:
+                        come = pltpu.make_async_copy(blocks[layer].at[piece], held, r.held_here.at[at])
+                        pl.when(jnp.logical_and(core == layer, active))(come.start)
+                placed.append((come, pltpu.make_async_copy(held, out.at[to, piece], r.placed.at[at])))
+    wide = []
+    for k in range(FEED):
+        for layer, source in enumerate((r.zero[k], r.one[k])):
+            copy = pltpu.make_async_copy(source, r.wide[k], r.wide_here.at[k])
+            pl.when(core == layer)(copy.start)
+            if layer == 0:
+                wide.append(copy)
+    for come, leave in placed:
+        come.wait()
+        leave.start()
+    r.ready(r.low, r.high, r.latent)
+    model = r.g_query.shape[0]
+    columns = r.g_query.shape[1]
+    low = r.low[...].reshape(-1, columns).astype(F32)
+    high = r.high[...].reshape(-1, columns).astype(F32)
+    r.g_query[...] = low[:model]
+    r.g_key_up[...] = low[model:]
+    r.g_value_up[...] = high[:LH]
+    r.g_out[...] = jnp.concatenate(
+        [high[start : start + columns] for start in range(LH, LH + model, columns)], axis=1
+    )
+    depth = r.latent.shape[1] - GAIN_ROWS
+    r.g_latent[...] = r.latent[:, :depth, :].astype(F32).reshape(r.g_latent.shape)
+    r.gains[...] = r.latent[0, depth:, :LH].astype(F32)
+    r.flush(r.g_query, r.g_key_up, r.g_value_up, r.g_out, r.g_latent, r.gains)
+    for k in range(FEED):
+        wide[k].wait()
+        r.g_wide[k][...] = r.wide[k][...].reshape(r.g_wide[k].shape).astype(F32)
+        r.flush(r.g_wide[k])
+    for come, leave in placed:
+        leave.wait()
+
+
+def emit(outs, outs_share, outs_spread, grads, grads_share, grads_spread, zero, one, parts):
+    low, high, latent = parts
+    pieces, depth, model = zero[0].shape
+    columns = low.shape[2]
+    split = pieces * (latent.shape[1] - GAIN_ROWS)
+    both = ((2,) + outs[0].shape, BF16)
+    out = named_call(
+        emit_kernel,
+        None,
+        lazy=dict(low=low, high=high, latent=latent),
+        far=dict(
+            outs=outs, outs_share=outs_share, outs_spread=outs_spread,
+            grads=grads, grads_share=grads_share, grads_spread=grads_spread,
+            zero=zero, one=one,
+        ),
+        late=dict(
+            g_query=((model, columns), F32),
+            g_key_up=((LH, columns), F32),
+            g_value_up=((LH, columns), F32),
+            g_out=((columns, model), F32),
+            g_latent=((split, KVH * LH), F32),
+            gains=((GAIN_ROWS, LH), F32),
+            g_wide=[((pieces * depth, model), F32)] * FEED,
+        ),
+        far_outs=dict(layer_out=both, input_grad=both),
+        scratch=dict(
+            placed=DMA((4, PIECES)),
+            held_here=DMA((4, PIECES)),
+            held=pltpu.VMEM((4,) + outs[0].shape, BF16),
+            wide_here=DMA((FEED,)),
+            wide=[pltpu.VMEM((pieces, depth, model), BF16)] * FEED,
+        ),
+    )
+    wide = [part for part in out.g_wide]
+    rest = (out.g_query, out.g_key_up, out.g_value_up, out.g_out, out.g_latent, out.gains)
+    return (out.layer_out, out.input_grad, *wide, *rest)
+
+
 def pieces_of(block):
+    if isinstance(block, Part) or len(block.shape) == 4:
+        return block
     return block.reshape(PIECES, 2, block.shape[0] // PIECES // 2, block.shape[1])
 
 
@@ -1169,7 +1283,7 @@
 
 
 def forward_layer(layer, number, source, own_feed, own_packed=None, packed=None, **small):
-    rows, model = source.shape
+    rows, model = LEN, own_feed[0].shape[2]
     split, own = shapes_of(rows, model)
     pieces, depth, width = (packed if own_packed is None else own_packed).shape
     wide = (rows, pieces * own_feed[0].shape[1])
@@ -1231,7 +1345,7 @@
 
 
 def feed_layer_back(number, upstream, result, beside):
-    rows, model = upstream.shape
+    rows, model = result.attn_in.shape
     split, half = shapes_of(rows, model)
     columns = result.queries.shape[1]
     wide = pltpu.VMEM(result.hidden.shape, BF16)
@@ -1280,11 +1394,11 @@
     )
 
 
-def attend_layer_back(number, source, result, back, beside):
-    rows, model = source.shape
+def attend_layer_back(number, source, result, back, beside, early=False):
+    rows, model = result.attn_in.shape
     pieces, depth, width = result.packed.shape
     out = named_call(
-        functools.partial(attend_in_back, beside.shared),
+        functools.partial(attend_in_back, beside.shared, early),
         number,
         ins=dict(gain=result.gains[0:1], mlp_gain=back.gain_grad),
         lazy=dict(
@@ -1308,16 +1422,16 @@
             g_packed=[((pieces, depth // 2, width), BF16)] * 2,
             g_latent=((pieces, model // pieces + lax.axis_size(TEN) * GAIN_ROWS, LH), BF16),
         ),
-        far_outs=beside.far_outs,
+        far_outs=dict(grad_here=(shapes_of(rows, model)[0], BF16), **beside.far_outs) if early else beside.far_outs,
         scratch=dict(
             exchange=exchange_scratch(rows, model),
             grads=pltpu.VMEM((pieces * depth, width), BF16),
             gain_grad=pltpu.VMEM((1, model), F32),
+            early_sems=[DMA((PIECES,)), DMA((PIECES,))],
             **beside.scratch,
         ),
     )
     out.parts = out.g_packed + [out.g_latent]
-    out.input_grad = out.input_grad.reshape(rows, model)
     return out
 
 
@@ -1351,14 +1465,11 @@
     def latent_of(shard):
         return lax.dynamic_slice_in_dim(w_latent[0], group_of(shard) * LH, LH, 1)
 
-    def sequence_rows(block):
-        return lax.dynamic_slice_in_dim(block, at.sequence * LEN, LEN, 0)
-
     own_feed = [by_dp(w) for w in (w_gate[0].T, w_up[0].T, w_down[0])]
     own_packed = by_dp(pack_attention(w_query[0], w_key_up[0], w_value_up[0], w_out[0]))
     own_gains = jnp.concatenate([norm_attn, norm_mlp], axis=0)
     own_latent = latent_of(at.z)
-    source = sequence_rows(inputs)
+    source = Part(inputs)
     zero = forward_layer(
         0,
         0,
@@ -1369,7 +1480,7 @@
         own_latent=own_latent,
         pass_latent=latent_of(opposite_z),
     )
-    first_out = zero.output.reshape(LEN, model)
+    first_out = zero.output
     one = forward_layer(
         1,
         1,
@@ -1382,56 +1493,36 @@
         far_latent=zero.far_latent,
     )
     one.packed = zero.packed_next
-    second_out = one.output.reshape(LEN, model)
-
-    def shared(block):
-        return block.reshape(at.team, LEN // at.team, model)
-
-    back = feed_layer_back(2, sequence_rows(out_grad), one, Beside(shares=[(shared(first_out), 0)]))
-    beside = Beside(back.grads, shares=[(shared(second_out), 1)], spreads=[(back.shares_here[0], 0)])
+    second_out = one.output
+
+    back = feed_layer_back(2, Part(out_grad), one, Beside(shares=[(first_out, 0)]))
+    first_share = back.shares_here[0]
+    beside = Beside(back.grads, shares=[(second_out, 1)], spreads=[(first_share, 0)])
     above = attend_layer_back(3, first_out, one, back, beside)
-    first_far = above.spreads_here[0]
-    second_grad = above.input_grad
-    beside = Beside(
-        above.parts, above.sums, True, [(shared(second_grad), 1)], [(above.shares_here[0], 1)]
+    second_share, second_grad = above.shares_here[0], above.input_grad
+    beside = Beside(above.parts, above.sums, True, [(second_grad, 1)], [(second_share, 1)])
+    back = feed_layer_back(4, second_grad, zero, beside)
+    wide_one, grad_share = back.wholes, back.shares_here[0]
+    beside = Beside(back.grads, back.sums, spreads=[(grad_share, 1)])
+    below = attend_layer_back(5, source, zero, back, beside, True)
+    first_grad = below.input_grad
+    groups = tuple(group_of(shard) for shard in range(at.count))
+    last = finish(6, groups, below.sums, below.parts, below.totals, below.grad_here)
+    *wide_zero, low_part, high_part, latent = last.wholes
+    out = emit(
+        [first_out, second_out],
+        [first_share, second_share],
+        [above.spreads_here[0], back.spreads_here[0]],
+        [first_grad, second_grad],
+        [below.grad_here, grad_share],
+        [last.spreads_here[0], below.spreads_here[0]],
+        wide_zero,
+        wide_one,
+        [low_part, high_part, latent],
     )
-    back = feed_layer_back(4, second_grad, zero, beside)
-    wide_one = back.wholes
-    second_far = back.spreads_here[0]
-    beside = Beside(back.grads, back.sums, spreads=[(back.shares_here[0], 1)])
-    below = attend_layer_back(5, source, zero, back, beside)
-    grad_far = below.spreads_here[0]
-    first_grad = below.input_grad
-    first_far, second_far, grad_far = (far.reshape(LEN, model) for far in (first_far, second_far, grad_far))
-    groups = tuple(group_of(shard) for shard in range(at.count))
-    last = finish(6, groups, below.sums, below.parts, below.totals, shared(first_grad))
-    *wide_zero, low_part, high_part, latent = last.wholes
-
-    def both_sequences(mine, other):
-        both = jnp.broadcast_to(other[None], (2,) + other.shape)
-        both = lax.dynamic_update_slice_in_dim(both, mine[None], at.sequence, 0)
-        return both.reshape(1, 2 * other.shape[0], model)
-
-    layer_out = both_sequences(
-        jnp.where(at.first, first_out, second_out), jnp.where(at.first, first_far, second_far)
-    )
-    input_grad = both_sequences(
-        jnp.where(at.first, first_grad, second_grad),
-        jnp.where(at.first, last.grad_far.reshape(first_grad.shape), grad_far),
-    )
-    g_gate, g_up, g_down = [
-        jnp.where(at.first, whole_of(zero), whole_of(one)).astype(F32) for zero, one in zip(wide_zero, wide_one)
-    ]
-    low_part, high_part = whole_of(low_part).astype(F32), whole_of(high_part).astype(F32)
-    g_query, g_key_up = low_part[:model], low_part[model:]
-    g_value_up = high_part[:LH]
-    columns = high_part.shape[1]
-    g_out = [high_part[start : start + columns] for start in range(LH, LH + model, columns)]
-    g_out = jnp.concatenate(g_out, axis=1)
-    width = model // at.count
-    depth = latent.shape[1] - GAIN_ROWS
-    g_latent = latent[:, :depth].reshape(width, KVH * LH).astype(F32)
-    gains = latent[0, depth : depth + 2, :width].astype(F32)
+    layer_out, input_grad, g_gate, g_up, g_down, g_query, g_key_up, g_value_up, g_out, g_latent, gains = out
+    gains = gains[:, : model // at.count]
+    layer_out, input_grad = (both.reshape(1, 2 * LEN, model) for both in (layer_out, input_grad))
     return (
         layer_out,
         input_grad,

time: 559 us -> 519 us (0.928)
  local copies, waits for them, and re-layouts: 30.2 us -> 7.6 us
  other arithmetic: 16.7 us -> 1.36 us
    unnamed x50 -> x16, local copies, waits for them, and re-layouts: 14.8 us -> 1.18 us
    select_n x7 -> x0, other arithmetic: 7.14 us -> none  [the longest x1 3.14 us: local(): jnp.where(at.first, first_grad, second_grad)]
    pallas_call x7 -> x8, Pallas kernels: 502 us -> 500 us  [named_call(): pl.pallas_call(body, in_specs=[vmem] * len(flat(ins)) + [anywhere] * len(...]
where the time goes in v6:
time: 519 us; the launch traced here: 510 us
  Pallas kernels  500 us (96%)
  local copies, waits for them, and re-layouts  7.6 us (1%)
    pallas_call x8, Pallas kernels, named_call(): pl.pallas_call(body, in_specs=[vmem] * len(flat(ins)) + [anywhere] * len(...  500 us

profile of v6, /device:TPU:0, one launch (start us, length us, event | category | flops | bytes accessed | tf_op | source)
XLA Modules:
  0.0 510.0 jit_solution(699730358172221598)
XLA Ops:
  0.6 0.0 copy-start
  0.7 1.4 pad_maximum_fusion.refs_0_
  2.1 0.0 copy-start.3
  2.1 0.0 copy-start.4
  2.1 0.0 copy-start.1
  2.1 2.3 dynamic-slice_bitcast_fusion
  4.4 0.0 copy-done
  4.4 0.0 copy-done.3
  4.5 0.0 copy-done.4
  4.5 0.0 copy-done.1
  4.6 0.0 copy-start.2
  4.6 1.0 copy-done.2
  5.7 101.5 %shard_map.211 = (f32[2,1024]{1,0:T(2,128)}, bf16[1024,256]{1,0:T(8,128)(2,1)}, f32[2,1024]{1,0:T(2,128)}, bf16[1024,256]{1,0:T(8,128)(2,1)}, bf16[1024,1024]{1,...) custom-call(f32[2,1024]{1,0:T(2,128)} %pad_maximum_fusion.refs_0_, ...), custom_call_target="tpu_custom_call" | custom-call | flops 4000000000 | bytes 1048576 | tf_op jit(solution)/shard_map/pallas_call | solution.py:812
  107.2 1.4 fusion.2
  108.6 81.5 %shard_map.212 = (f32[2,1024]{1,0:T(2,128)}, bf16[1024,256]{1,0:T(8,128)(2,1)}, bf16[1024,1024]{1,0:T(8,128)(2,1)}, bf16[1024,256]{1,0:T(8,128)(2,1)}, bf16[1024...) custom-call(f32[2,1024]{1,0:T(2,128)} %pad_maximum_fusion.refs_0_, ...), custom_call_target="tpu_custom_call" | custom-call | flops 4000000000 | bytes 1048576 | tf_op jit(solution)/shard_map/pallas_call | solution.py:812
  190.1 1.4 fusion.1
  191.5 52.9 %shard_map.213 = (f32[1,1024]{1,0:T(1,128)}, f32[4,128,1024]{2,1,0:T(8,128)}, bf16[4,2,128,1024]{3,2,1,0:T(8,128)(2,1)}, bf16[4,176,1024]{2,1,0:T(8,128)(2,1)}, ...) custom-call(f32[1,1024]{1,0:T(1,128)} %get-tuple-element.232.refs_0_, ...), custom_call_target="tpu_custom_call" | custom-call | flops 4000000000 | bytes 1048576 | tf_op jit(solution)/shard_map/pallas_call | solution.py:812
  244.5 54.1 %shard_map.214 = (bf16[176,1024]{1,0:T(8,128)(2,1)}, bf16[176,1024]{1,0:T(8,128)(2,1)}, bf16[176,1024]{1,0:T(8,128)(2,1)}, bf16[4,2,128,1024]{3,2,1,0:T(8,128)(2...) custom-call(f32[1,1024]{1,0:T(1,128)} %get-tuple-element.233.refs_0_, ...), custom_call_target="tpu_custom_call" | custom-call | flops 4000000000 | bytes 1048576 | tf_op jit(solution)/shard_map/pallas_call | solution.py:812
  298.6 75.0 %shard_map.215 = (f32[1,1024]{1,0:T(1,128)}, bf16[320,256]{1,0:T(8,128)(2,1)}, bf16[320,256]{1,0:T(8,128)(2,1)}, bf16[320,256]{1,0:T(8,128)(2,1)}, bf16[176,1024...) custom-call(f32[1,1024]{1,0:T(1,128)} %get-tuple-element.234.refs_0_, ...), custom_call_target="tpu_custom_call" | custom-call | flops 4000000000 | bytes 1048576 | tf_op jit(solution)/shard_map/pallas_call | solution.py:812
  373.6 61.9 %shard_map.216 = (bf16[176,1024]{1,0:T(8,128)(2,1)}, bf16[176,1024]{1,0:T(8,128)(2,1)}, bf16[176,1024]{1,0:T(8,128)(2,1)}, bf16[320,256]{1,0:T(8,128)(2,1)}, bf1...) custom-call(f32[1,1024]{1,0:T(1,128)} %get-tuple-element.235.refs_0_, ...), custom_call_target="tpu_custom_call" | custom-call | flops 4000000000 | bytes 1048576 | tf_op jit(solution)/shard_map/pallas_call | solution.py:812
  435.5 60.0 %shard_map.217 = (bf16[4,176,1024]{2,1,0:T(8,128)(2,1)}, bf16[4,176,1024]{2,1,0:T(8,128)(2,1)}, bf16[4,176,1024]{2,1,0:T(8,128)(2,1)}, bf16[4,320,256]{2,1,0:T(8...) custom-call(bf16[176,1024]{1,0:T(8,128)(2,1)} %get-tuple-element.193.refs_0, ...), custom_call_target="tpu_custom_call" | custom-call | flops 4000000000 | bytes 1048576 | tf_op jit(solution)/shard_map/pallas_call | solution.py:812
  495.5 12.7 %shard_map.218 = (f32[1024,256]{1,0:T(8,128)}, f32[256,256]{1,0:T(8,128)}, f32[256,256]{1,0:T(8,128)}, f32[256,1024]{1,0:T(8,128)}, f32[256,512]{1,0:T(8,128)}, ...) custom-call(bf16[4,320,256]{2,1,0:T(8,128)(2,1)} %get-tuple-element., ...), custom_call_target="tpu_custom_call" | custom-call | flops 4000000000 | bytes 1048576 | tf_op jit(solution)/shard_map/pallas_call | solution.py:812
  508.2 1.3 fusion
  (7 shorter events, 0.1 us)
Async XLA Ops:
  0.6 3.7 copy-start
  2.1 2.4 copy-start.3
  2.1 2.4 copy-start.4
  2.1 2.4 copy-start.1
  4.6 1.1 copy-start.2

commit v7 on v6

--- a/solution.py
+++ b/solution.py
@@ -262,18 +262,22 @@
 
 
 class Gather:
-    def __init__(self, plane, turn, whole, sent, here, active=None, piece=None, local=None):
+    def __init__(self, plane, turn, whole, sent, here, active=None, piece=None, local=None, rows=slice(None)):
         self.active = active
         near, far = plane.order(turn)
         me = plane.me
-        source = whole.at[me] if piece is None else piece
+
+        def part(place):
+            return whole.at[place, rows]
+
+        source = part(me) if piece is None else piece
 
         def copy(k, source, place, device):
-            return send_to(source, whole.at[place], sent.at[k], here.at[place], {DP: device})
+            return send_to(source, part(place), sent.at[k], here.at[place], {DP: device})
 
         self.first = copy(0, source, me, near)
-        self.second = [copy(1, source, me, far), copy(2, whole.at[near], near, far)]
-        self.coming = [copy(0, whole.at[place], place, near) for place in (near, far, plane.both)]
+        self.second = [copy(1, source, me, far), copy(2, part(near), near, far)]
+        self.coming = [copy(0, part(place), place, near) for place in (near, far, plane.both)]
         self.local = [] if piece is None else [pltpu.make_async_copy(piece, whole.at[me], local)]
 
     def when(self, body):
@@ -457,7 +461,7 @@
     half = rows // PIECES // 2
     return [
         pltpu.VMEM((2, half, model), F32),
-        pltpu.VMEM((PIECES, half, model), F32),
+        pltpu.VMEM((2, half, model), F32),
         pltpu.VMEM((PIECES, half, model), BF16),
         pltpu.VMEM((PIECES, half, model), BF16),
         pltpu.VMEM((team, PIECES, half, model), BF16),
@@ -500,11 +504,11 @@
         self.part[...] = product.reshape(self.part.shape)
         self.out[i] = self.part[1 - core].astype(BF16)
         self.core_copy(i).start()
-        self.keep[i] = self.part[core]
+        self.keep[i % 2] = self.part[core]
 
     def combine(self, i):
         self.core_copy(i).wait_recv()
-        self.far[self.team.place, i] = (self.keep[i] + self.got[i].astype(F32)).astype(BF16)
+        self.far[self.team.place, i] = (self.keep[i % 2] + self.got[i].astype(F32)).astype(BF16)
         for step in range(1, self.team.size):
             self.far_copy(i, step, self.team.place).start()
 
@@ -728,7 +732,6 @@
         for piece in range(1, pieces):
             r.g_latent[piece, rows_of, :] = nothing.astype(BF16)
     r.flush(r.g_latent)
-    beside.late()
     ex.finish(r.input_grad, False)
     r.flush(r.input_grad)
     beside.finish()
@@ -835,7 +838,7 @@
     taker = jnp.logical_not(holder)
     across = across_device()
     ex_a, ex_b = Exchange(team, r.ex_a), Exchange(team, r.ex_b)
-    greet(team.partners() + plane.partners() + [across])
+    greet(team.partners() + plane.partners() + ([across] if layer == 0 else []))
     rows, width = r.queries.shape
     model = r.w_latent.shape[0]
     size = rows // PIECES
@@ -845,22 +848,33 @@
     for copy in own_copies:
         pl.when(holder)(copy.start)
     gathers = [
-        Gather(plane, k, r.feed[k], r.gather_sent.at[k], r.gather_here.at[k], taker) for k in feeds
+        Gather(
+            plane, k, r.feed[k], r.gather_sent.at[k], r.gather_here.at[k], taker,
+            r.pieces[k] if layer else None, r.piece_sem.at[k],
+        )
+        for k in feeds
     ]
 
     def cross(k, source, target):
         return send_to(source, target, r.cross_sent.at[k], r.cross_here.at[k], across)
 
-    come = [cross(1 + k, r.own_feed[k].at[plane.me], r.come[k]) for k in feeds]
     if layer == 0:
+        come = [cross(1 + k, r.own_feed[k].at[plane.me], r.come[k]) for k in feeds]
+        next_feed = [cross(5 + k, r.own_feed[k].at[plane.me], r.feed_next[k]) for k in feeds]
         mine = cross(0, r.own_packed.at[plane.me], r.packed.at[plane.me])
         small = [
             send_to(r.pass_latent, r.far_latent, r.small_sent.at[0], r.small_here.at[0], team.other),
             send_to(r.own_gains, r.far_gains, r.small_sent.at[1], r.small_here.at[1], team.other),
         ]
         next_packed = cross(4, r.own_packed.at[plane.me], r.packed_next.at[plane.me])
-        packed_gather = Gather(plane, 0, r.packed, r.packed_sent, r.packed_here)
-        next_gather = Gather(plane, 1, r.packed_next, r.next_sent, r.next_here)
+        depth = r.packed.shape[1] // 2
+        halves = [slice(0, depth), slice(depth, 2 * depth)]
+        packed_gathers, next_gathers = (
+            [Gather(plane, k, whole, sent.at[k], here.at[k], rows=half) for k, half in enumerate(halves)]
+            for whole, sent, here in (
+                (r.packed, r.packed_sent, r.packed_here), (r.packed_next, r.next_sent, r.next_here)
+            )
+        )
         own_packed = [
             pltpu.make_async_copy(r.own_packed, target, r.own_sem.at[3]) for target in (r.packed, r.packed_next)
         ]
@@ -872,7 +886,8 @@
         for copy in small:
             copy.wait()
     else:
-        pl.when(holder)(come[0].start)
+        for gather in gathers:
+            gather.start()
 
     def next_come(k):
         @pl.when(holder)
@@ -904,9 +919,12 @@
         @pl.when(taker)
         def _():
             mine.wait_recv()
-            packed_gather.start()
-            packed_gather.middle()
-            packed_gather.finish()
+            for gather in packed_gathers:
+                gather.start()
+            for gather in packed_gathers:
+                gather.middle()
+            for gather in packed_gathers:
+                gather.finish()
 
         @pl.when(holder)
         def _():
@@ -939,21 +957,16 @@
         attend_rows(i * size, r.queries, r.keys, r.values, r.heads_out, r.norms)
         heads = r.heads_out[i * size : (i + 1) * size, :]
         ex_a.push(i, jnp.concatenate([mm(heads, block) for block in w_out], axis=1))
-        if i == layer:
+        if i == 0 and layer == 0:
             next_come(1)
-        if i == 0 and layer == 1:
-            take_come(0)
         if i:
             ex_a.combine(i - 1)
         if i == 1:
             gathers[0].middle()
-        if i == 2:
+        if i == 2 and layer == 0:
             next_come(2)
-            if layer == 0:
-                take_come(1)
+            take_come(1)
     ex_a.combine(PIECES - 1)
-    if layer == 1:
-        take_come(1)
     r.flush(r.attn_in, r.queries, r.latents, r.keys, r.values, r.heads_out, r.norms)
     if layer == 0:
 
@@ -982,7 +995,8 @@
 
     receive(0)
     gathers[1].middle()
-    take_come(2)
+    if layer == 0:
+        take_come(2)
     receive(1)
     gathers[2].middle()
 
@@ -994,13 +1008,21 @@
     for gather in gathers:
         gather.finish()
     r.flush(*r.feed)
+    if layer == 0:
+
+        @pl.when(taker)
+        def _():
+            for copy in next_feed:
+                copy.start()
+
     feed(0)
     if layer == 0:
 
         @pl.when(holder)
         def _():
             next_packed.wait_recv()
-            next_gather.start()
+            for gather in next_gathers:
+                gather.start()
 
     def steady(i, _):
         receive(i)
@@ -1018,8 +1040,10 @@
 
         @pl.when(holder)
         def _():
-            next_gather.middle()
-            next_gather.finish()
+            for gather in next_gathers:
+                gather.middle()
+            for gather in next_gathers:
+                gather.finish()
 
         @pl.when(taker)
         def _():
@@ -1031,7 +1055,18 @@
     ex_b.finish(r.output)
     r.flush(r.output)
 
-    pl.when(holder)(come[2].wait_send)
+    if layer == 0:
+
+        @pl.when(holder)
+        def _():
+            come[2].wait_send()
+            for copy in next_feed:
+                copy.wait_recv()
+
+        @pl.when(taker)
+        def _():
+            for copy in next_feed:
+                copy.wait_send()
 
 
 def finish_kernel(groups, r):
@@ -1063,7 +1098,7 @@
             crosses[k - 1].wait_send()
             crosses[k].start()
 
-    outputs = Outputs(r, [[], [0]])
+    outputs = Outputs(r, [[], [0, 1]])
     outputs.start()
     gather_sent, gather_here, gather_own = r.gather_sems
     gathers = [
@@ -1154,7 +1189,7 @@
     outputs.finish()
 
 
-def finish(number, groups, feed, late, done, grad):
+def finish(number, groups, feed, late, done, grads):
     dp, count = lax.axis_size(DP), lax.axis_size(TEN)
     depth = done[-1].shape[0] // count
     shapes = [part.shape for part in list(feed) + list(done)]
@@ -1165,8 +1200,8 @@
         functools.partial(finish_kernel, groups),
         number,
         ins=dict(pieces=list(feed), done=list(done)),
-        far=dict(late=list(late), shares=[], spreads=[grad]),
-        far_outs=dict(wholes=[((dp,) + total, BF16) for total in totals], spreads_here=[(grad.shape, BF16)]),
+        far=dict(late=list(late), shares=[], spreads=grads),
+        far_outs=dict(wholes=[((dp,) + total, BF16) for total in totals], spreads_here=[(grad.shape, BF16) for grad in grads]),
         scratch=dict(
             scatter=[item for load in late for item in scatter_scratch(load)],
             come=[pltpu.VMEM(shape, BF16) for shape in shapes],
@@ -1177,7 +1212,7 @@
             cross_sems=[DMA((items,)), DMA((items,))],
             gather_sems=[DMA((items, 3)), DMA((items, dp)), DMA((items,))],
             block_sems=[DMA((count,)), DMA((count,))],
-            spread_sems=[DMA((count // 2, PIECES)), DMA((PIECES,))],
+            spread_sems=[DMA((count // 2, PIECES)), DMA((PIECES,))] * len(grads),
         ),
     )
 
@@ -1282,7 +1317,7 @@
     return (PIECES, 2, rows // PIECES // 2, model), (PIECES, rows // PIECES // 2, model)
 
 
-def forward_layer(layer, number, source, own_feed, own_packed=None, packed=None, **small):
+def forward_layer(layer, number, source, own_feed, own_packed=None, packed=None, pieces_in=(), **small):
     rows, model = LEN, own_feed[0].shape[2]
     split, own = shapes_of(rows, model)
     pieces, depth, width = (packed if own_packed is None else own_packed).shape
@@ -1310,28 +1345,32 @@
     scratch = dict(
         ex_a=exchange_scratch(rows, model),
         ex_b=exchange_scratch(rows, model),
-        come=[pltpu.VMEM(w.shape[1:], BF16) for w in own_feed],
         own_sem=DMA((4,)),
+        piece_sem=DMA((3,)),
         gather_sent=DMA((3, 3)),
         gather_here=DMA((3, pieces)),
-        cross_sent=DMA((5,)),
-        cross_here=DMA((5,)),
+        cross_sent=DMA((8,)),
+        cross_here=DMA((8,)),
     )
+    far_outs = dict()
     lazy, far = dict(source=pieces_of(source)), dict(own_feed=own_feed)
     if layer == 0:
         far.update(own_packed=own_packed)
+        far_outs.update(feed_next=[(w.shape[1:], BF16) for w in own_feed])
         outs.update(far_latent=((model, LH), BF16), far_gains=((2, model), F32))
         late.update(packed=((pieces, depth, width), BF16), packed_next=((pieces, depth, width), BF16))
         scratch.update(
+            come=[pltpu.VMEM(w.shape[1:], BF16) for w in own_feed],
             small_sent=DMA((2,)),
             small_here=DMA((2,)),
-            packed_sent=DMA((3,)),
-            packed_here=DMA((pieces,)),
-            next_sent=DMA((3,)),
-            next_here=DMA((pieces,)),
+            packed_sent=DMA((2, 3)),
+            packed_here=DMA((2, pieces)),
+            next_sent=DMA((2, 3)),
+            next_here=DMA((2, pieces)),
         )
     else:
         lazy.update(packed=packed)
+        small.update(pieces=list(pieces_in))
     return named_call(
         functools.partial(forward_kernel, layer),
         number,
@@ -1340,6 +1379,7 @@
         far=far,
         outs=outs,
         late=late,
+        far_outs=far_outs,
         scratch=scratch,
     )
 
@@ -1487,6 +1527,7 @@
         first_out,
         own_feed,
         packed=zero.packed_next,
+        pieces_in=zero.feed_next,
         own_gains=own_gains,
         far_gains=zero.far_gains,
         own_latent=own_latent,
@@ -1499,23 +1540,23 @@
     first_share = back.shares_here[0]
     beside = Beside(back.grads, shares=[(second_out, 1)], spreads=[(first_share, 0)])
     above = attend_layer_back(3, first_out, one, back, beside)
-    second_share, second_grad = above.shares_here[0], above.input_grad
-    beside = Beside(above.parts, above.sums, True, [(second_grad, 1)], [(second_share, 1)])
+    second_share, second_grad, first_spread = above.shares_here[0], above.input_grad, above.spreads_here[0]
+    beside = Beside(above.parts, above.sums, True, spreads=[(second_share, 1)])
     back = feed_layer_back(4, second_grad, zero, beside)
-    wide_one, grad_share = back.wholes, back.shares_here[0]
-    beside = Beside(back.grads, back.sums, spreads=[(grad_share, 1)])
+    wide_one, second_spread = back.wholes, back.spreads_here[0]
+    beside = Beside(back.grads, back.sums, shares=[(second_grad, 1)])
     below = attend_layer_back(5, source, zero, back, beside, True)
-    first_grad = below.input_grad
+    first_grad, grad_share = below.input_grad, below.shares_here[0]
     groups = tuple(group_of(shard) for shard in range(at.count))
-    last = finish(6, groups, below.sums, below.parts, below.totals, below.grad_here)
+    last = finish(6, groups, below.sums, below.parts, below.totals, [below.grad_here, grad_share])
     *wide_zero, low_part, high_part, latent = last.wholes
     out = emit(
         [first_out, second_out],
         [first_share, second_share],
-        [above.spreads_here[0], back.spreads_here[0]],
+        [first_spread, second_spread],
         [first_grad, second_grad],
         [below.grad_here, grad_share],
-        [last.spreads_here[0], below.spreads_here[0]],
+        last.spreads_here,
         wide_zero,
         wide_one,
         [low_part, high_part, latent],

time: 519 us -> 502 us (0.967)
  Pallas kernels: 500 us -> 485 us
    pallas_call x8, Pallas kernels: 500 us -> 485 us  [named_call(): pl.pallas_call(body, in_specs=[vmem] * len(flat(ins)) + [anywhere] * len(...]
where the time goes in v7:
time: 502 us; the launch traced here: 495 us
  Pallas kernels  485 us (97%)
  local copies, waits for them, and re-layouts  7.6 us (2%)
    pallas_call x8, Pallas kernels, named_call(): pl.pallas_call(body, in_specs=[vmem] * len(flat(ins)) + [anywhere] * len(...  485 us

profile of v7, /device:TPU:0, one launch (start us, length us, event | category | flops | bytes accessed | tf_op | source)
XLA Modules:
  0.0 494.7 jit_solution(973371052582760664)
XLA Ops:
  0.6 0.0 copy-start
  0.7 1.4 pad_maximum_fusion.refs_0_
  2.1 0.0 copy-start.3
  2.1 0.0 copy-start.4
  2.1 0.0 copy-start.1
  2.1 2.3 dynamic-slice_bitcast_fusion
  4.4 0.0 copy-done
  4.4 0.0 copy-done.3
  4.5 0.0 copy-done.4
  4.5 0.0 copy-done.1
  4.6 0.0 copy-start.2
  4.6 1.0 copy-done.2
  5.7 110.6 %shard_map.211 = (f32[2,1024]{1,0:T(2,128)}, bf16[1024,256]{1,0:T(8,128)(2,1)}, f32[2,1024]{1,0:T(2,128)}, bf16[1024,256]{1,0:T(8,128)(2,1)}, bf16[1024,1024]{1,...) custom-call(f32[2,1024]{1,0:T(2,128)} %pad_maximum_fusion.refs_0_, ...), custom_call_target="tpu_custom_call" | custom-call | flops 4000000000 | bytes 1048576 | tf_op jit(solution)/shard_map/pallas_call | solution.py:815
  116.3 1.4 fusion.2
  117.6 70.9 %shard_map.212 = (f32[2,1024]{1,0:T(2,128)}, bf16[1024,256]{1,0:T(8,128)(2,1)}, bf16[1024,1024]{1,0:T(8,128)(2,1)}, bf16[1024,256]{1,0:T(8,128)(2,1)}, bf16[1024...) custom-call(f32[2,1024]{1,0:T(2,128)} %pad_maximum_fusion.refs_0_, ...), custom_call_target="tpu_custom_call" | custom-call | flops 4000000000 | bytes 1048576 | tf_op jit(solution)/shard_map/pallas_call | solution.py:815
  188.6 1.4 fusion.1
  190.0 52.7 %shard_map.213 = (f32[1,1024]{1,0:T(1,128)}, f32[4,128,1024]{2,1,0:T(8,128)}, bf16[4,2,128,1024]{3,2,1,0:T(8,128)(2,1)}, bf16[4,176,1024]{2,1,0:T(8,128)(2,1)}, ...) custom-call(f32[1,1024]{1,0:T(1,128)} %get-tuple-element.238.refs_0_, ...), custom_call_target="tpu_custom_call" | custom-call | flops 4000000000 | bytes 1048576 | tf_op jit(solution)/shard_map/pallas_call | solution.py:815
  242.6 54.1 %shard_map.214 = (bf16[176,1024]{1,0:T(8,128)(2,1)}, bf16[176,1024]{1,0:T(8,128)(2,1)}, bf16[176,1024]{1,0:T(8,128)(2,1)}, bf16[4,2,128,1024]{3,2,1,0:T(8,128)(2...) custom-call(f32[1,1024]{1,0:T(1,128)} %get-tuple-element.239.refs_0_, ...), custom_call_target="tpu_custom_call" | custom-call | flops 4000000000 | bytes 1048576 | tf_op jit(solution)/shard_map/pallas_call | solution.py:815
  296.7 57.8 %shard_map.215 = (f32[1,1024]{1,0:T(1,128)}, bf16[320,256]{1,0:T(8,128)(2,1)}, bf16[320,256]{1,0:T(8,128)(2,1)}, bf16[320,256]{1,0:T(8,128)(2,1)}, bf16[176,1024...) custom-call(f32[1,1024]{1,0:T(1,128)} %get-tuple-element.240.refs_0_, ...), custom_call_target="tpu_custom_call" | custom-call | flops 4000000000 | bytes 1048576 | tf_op jit(solution)/shard_map/pallas_call | solution.py:815
  354.5 64.1 %shard_map.216 = (bf16[176,1024]{1,0:T(8,128)(2,1)}, bf16[176,1024]{1,0:T(8,128)(2,1)}, bf16[176,1024]{1,0:T(8,128)(2,1)}, bf16[320,256]{1,0:T(8,128)(2,1)}, bf1...) custom-call(f32[1,1024]{1,0:T(1,128)} %get-tuple-element.241.refs_0_, ...), custom_call_target="tpu_custom_call" | custom-call | flops 4000000000 | bytes 1048576 | tf_op jit(solution)/shard_map/pallas_call | solution.py:815
  418.6 61.7 %shard_map.217 = (bf16[4,176,1024]{2,1,0:T(8,128)(2,1)}, bf16[4,176,1024]{2,1,0:T(8,128)(2,1)}, bf16[4,176,1024]{2,1,0:T(8,128)(2,1)}, bf16[4,320,256]{2,1,0:T(8...) custom-call(bf16[176,1024]{1,0:T(8,128)(2,1)} %get-tuple-element.198, ...), custom_call_target="tpu_custom_call" | custom-call | flops 4000000000 | bytes 1048576 | tf_op jit(solution)/shard_map/pallas_call | solution.py:815
  480.3 12.7 %shard_map.218 = (f32[1024,256]{1,0:T(8,128)}, f32[256,256]{1,0:T(8,128)}, f32[256,256]{1,0:T(8,128)}, f32[256,1024]{1,0:T(8,128)}, f32[256,512]{1,0:T(8,128)}, ...) custom-call(bf16[4,320,256]{2,1,0:T(8,128)(2,1)} %get-tuple-element., ...), custom_call_target="tpu_custom_call" | custom-call | flops 4000000000 | bytes 1048576 | tf_op jit(solution)/shard_map/pallas_call | solution.py:815
  493.1 1.3 fusion
  (7 shorter events, 0.1 us)
Async XLA Ops:
  0.6 3.7 copy-start
  2.1 2.4 copy-start.3
  2.1 2.4 copy-start.4
  2.1 2.4 copy-start.1
  4.6 1.1 copy-start.2

commit v8 on v7

--- a/solution.py
+++ b/solution.py
@@ -618,7 +618,7 @@
     w_out = weights[model + 2 * LH :]
 
     def receive(i):
-        part, gain_part = rms_back(r.residual[i], r.gain[...], ex.total(i))
+        part, gain_part = rms_back(r.residual[i], r.gain[1:2, :], ex.total(i))
         block = upstream[i, ex.team.core].astype(F32) + part
         r.d_residual[i] = block
         gain_grad[...] += gain_part
@@ -702,7 +702,7 @@
     r.gain_grad[...] = jnp.zeros_like(r.gain_grad)
 
     def receive(i):
-        part, gain_part = rms_back(r.source[i, team.core].astype(F32), r.gain[...], ex.total(i))
+        part, gain_part = rms_back(r.source[i, team.core].astype(F32), r.gain[0:1, :], ex.total(i))
         r.gain_grad[...] += gain_part
         ex.join(i, r.input_grad, (r.d_residual[i] + part).astype(BF16))
 
@@ -997,6 +997,12 @@
     gathers[1].middle()
     if layer == 0:
         take_come(2)
+
+        @pl.when(taker)
+        def _():
+            for copy in next_feed:
+                copy.start()
+
     receive(1)
     gathers[2].middle()
 
@@ -1008,13 +1014,6 @@
     for gather in gathers:
         gather.finish()
     r.flush(*r.feed)
-    if layer == 0:
-
-        @pl.when(taker)
-        def _():
-            for copy in next_feed:
-                copy.start()
-
     feed(0)
     if layer == 0:
 
@@ -1090,13 +1089,10 @@
         send_to(source, r.come[k], cross_sent.at[k], cross_here.at[k], across) for k, source in enumerate(sources)
     ]
 
-    pl.when(second)(crosses[0].start)
-
-    def next_cross(k):
-        @pl.when(second)
-        def _():
-            crosses[k - 1].wait_send()
-            crosses[k].start()
+    @pl.when(second)
+    def _():
+        for copy in crosses[:FEED]:
+            copy.start()
 
     outputs = Outputs(r, [[], [0, 1]])
     outputs.start()
@@ -1122,14 +1118,12 @@
         gathers[k].start()
 
     scatters[0].middle()
-    next_cross(1)
     take_cross(0)
     for scatter in scatters[1:]:
         scatter.middle()
     for k, scatter in enumerate(scatters):
         r.leave[k][...] = scatter.total().astype(BF16)
         if k == 0:
-            next_cross(2)
             gathers[0].middle()
         pl.when(second)(crosses[FEED + k].start)
     take_cross(1)
@@ -1183,7 +1177,7 @@
 
     @pl.when(second)
     def _():
-        for copy in crosses[2:]:
+        for copy in crosses:
             copy.wait_send()
 
     outputs.finish()
@@ -1220,6 +1214,13 @@
 def emit_kernel(r):
     core = lax.axis_index(SEC)
     sequence = lax.axis_index(TEN) // (lax.axis_size(TEN) // 2)
+    wide = []
+    for k in range(FEED):
+        for layer, source in enumerate((r.zero[k], r.one[k])):
+            copy = pltpu.make_async_copy(source, r.wide[k], r.wide_here.at[k])
+            pl.when(core == layer)(copy.start)
+            if layer == 0:
+                wide.append(copy)
     placed = []
     place = lax.rem(lax.axis_index(TEN), lax.axis_size(TEN) // 2)
     for k, (mine, share, spread, out) in enumerate(
@@ -1236,13 +1237,10 @@
                         come = pltpu.make_async_copy(blocks[layer].at[piece], held, r.held_here.at[at])
                         pl.when(jnp.logical_and(core == layer, active))(come.start)
                 placed.append((come, pltpu.make_async_copy(held, out.at[to, piece], r.placed.at[at])))
-    wide = []
     for k in range(FEED):
-        for layer, source in enumerate((r.zero[k], r.one[k])):
-            copy = pltpu.make_async_copy(source, r.wide[k], r.wide_here.at[k])
-            pl.when(core == layer)(copy.start)
-            if layer == 0:
-                wide.append(copy)
+        wide[k].wait()
+        r.g_wide[k][...] = r.wide[k][...].reshape(r.g_wide[k].shape).astype(F32)
+        r.flush(r.g_wide[k])
     for come, leave in placed:
         come.wait()
         leave.start()
@@ -1261,10 +1259,6 @@
     r.g_latent[...] = r.latent[:, :depth, :].astype(F32).reshape(r.g_latent.shape)
     r.gains[...] = r.latent[0, depth:, :LH].astype(F32)
     r.flush(r.g_query, r.g_key_up, r.g_value_up, r.g_out, r.g_latent, r.gains)
-    for k in range(FEED):
-        wide[k].wait()
-        r.g_wide[k][...] = r.wide[k][...].reshape(r.g_wide[k].shape).astype(F32)
-        r.flush(r.g_wide[k])
     for come, leave in placed:
         leave.wait()
 
@@ -1394,7 +1388,7 @@
     return named_call(
         functools.partial(feed_back, beside.shared),
         number,
-        ins=dict(gain=result.gains[1:2]),
+        ins=dict(gain=result.gains),
         lazy=dict(
             upstream=pieces_of(upstream),
             feed=result.feed,
@@ -1440,7 +1434,7 @@
     out = named_call(
         functools.partial(attend_in_back, beside.shared, early),
         number,
-        ins=dict(gain=result.gains[0:1], mlp_gain=back.gain_grad),
+        ins=dict(gain=result.gains, mlp_gain=back.gain_grad),
         lazy=dict(
             d_queries=back.d_queries,
             d_latents=back.d_latents,

time: 502 us -> 488 us (0.972)
  Pallas kernels: 485 us -> 477 us
    pallas_call x8, Pallas kernels: 485 us -> 477 us  [named_call(): pl.pallas_call(body, in_specs=[vmem] * len(flat(ins)) + [anywhere] * len(...]
where the time goes in v8:
time: 488 us; the launch traced here: 484 us
  Pallas kernels  477 us (98%)
    pallas_call x8, Pallas kernels, named_call(): pl.pallas_call(body, in_specs=[vmem] * len(flat(ins)) + [anywhere] * len(...  477 us

profile of v8, /device:TPU:0, one launch (start us, length us, event | category | flops | bytes accessed | tf_op | source)
XLA Modules:
  0.0 484.3 jit_solution(13501387693114306066)
XLA Ops:
  0.6 0.0 copy-start
  0.7 1.4 pad_maximum_fusion.refs_0_
  2.1 0.0 copy-start.3
  2.1 0.0 copy-start.4
  2.1 0.0 copy-start.1
  2.1 2.3 dynamic-slice_bitcast_fusion
  4.4 0.0 copy-done
  4.4 0.0 copy-done.3
  4.5 0.0 copy-done.4
  4.5 0.0 copy-done.1
  4.6 0.0 copy-start.2
  4.6 1.0 copy-done.2
  5.7 104.7 %shard_map.211 = (f32[2,1024]{1,0:T(2,128)}, bf16[1024,256]{1,0:T(8,128)(2,1)}, f32[2,1024]{1,0:T(2,128)}, bf16[1024,256]{1,0:T(8,128)(2,1)}, bf16[1024,1024]{1,...) custom-call(f32[2,1024]{1,0:T(2,128)} %pad_maximum_fusion.refs_0_, ...), custom_call_target="tpu_custom_call" | custom-call | flops 4000000000 | bytes 1048576 | tf_op jit(solution)/shard_map/pallas_call | solution.py:815
  110.4 71.0 %shard_map.212 = (f32[2,1024]{1,0:T(2,128)}, bf16[1024,256]{1,0:T(8,128)(2,1)}, bf16[1024,1024]{1,0:T(8,128)(2,1)}, bf16[1024,256]{1,0:T(8,128)(2,1)}, bf16[1024...) custom-call(f32[2,1024]{1,0:T(2,128)} %pad_maximum_fusion.refs_0_, ...), custom_call_target="tpu_custom_call" | custom-call | flops 4000000000 | bytes 1048576 | tf_op jit(solution)/shard_map/pallas_call | solution.py:815
  181.4 53.4 %shard_map.213 = (f32[1,1024]{1,0:T(1,128)}, f32[4,128,1024]{2,1,0:T(8,128)}, bf16[4,2,128,1024]{3,2,1,0:T(8,128)(2,1)}, bf16[4,176,1024]{2,1,0:T(8,128)(2,1)}, ...) custom-call(f32[2,1024]{1,0:T(2,128)} %get-tuple-element.131.refs_0_, ...), custom_call_target="tpu_custom_call" | custom-call | flops 4000000000 | bytes 1048576 | tf_op jit(solution)/shard_map/pallas_call | solution.py:815
  234.8 54.1 %shard_map.214 = (bf16[176,1024]{1,0:T(8,128)(2,1)}, bf16[176,1024]{1,0:T(8,128)(2,1)}, bf16[176,1024]{1,0:T(8,128)(2,1)}, bf16[4,2,128,1024]{3,2,1,0:T(8,128)(2...) custom-call(f32[2,1024]{1,0:T(2,128)} %get-tuple-element.131.refs_0_, ...), custom_call_target="tpu_custom_call" | custom-call | flops 4000000000 | bytes 1048576 | tf_op jit(solution)/shard_map/pallas_call | solution.py:815
  288.9 58.3 %shard_map.215 = (f32[1,1024]{1,0:T(1,128)}, bf16[320,256]{1,0:T(8,128)(2,1)}, bf16[320,256]{1,0:T(8,128)(2,1)}, bf16[320,256]{1,0:T(8,128)(2,1)}, bf16[176,1024...) custom-call(f32[2,1024]{1,0:T(2,128)} %get-tuple-element.123.refs_0_, ...), custom_call_target="tpu_custom_call" | custom-call | flops 4000000000 | bytes 1048576 | tf_op jit(solution)/shard_map/pallas_call | solution.py:815
  347.2 64.0 %shard_map.216 = (bf16[176,1024]{1,0:T(8,128)(2,1)}, bf16[176,1024]{1,0:T(8,128)(2,1)}, bf16[176,1024]{1,0:T(8,128)(2,1)}, bf16[320,256]{1,0:T(8,128)(2,1)}, bf1...) custom-call(f32[2,1024]{1,0:T(2,128)} %get-tuple-element.123.refs_0_, ...), custom_call_target="tpu_custom_call" | custom-call | flops 4000000000 | bytes 1048576 | tf_op jit(solution)/shard_map/pallas_call | solution.py:815
  411.2 60.3 %shard_map.217 = (bf16[4,176,1024]{2,1,0:T(8,128)(2,1)}, bf16[4,176,1024]{2,1,0:T(8,128)(2,1)}, bf16[4,176,1024]{2,1,0:T(8,128)(2,1)}, bf16[4,320,256]{2,1,0:T(8...) custom-call(bf16[176,1024]{1,0:T(8,128)(2,1)} %get-tuple-element.198, ...), custom_call_target="tpu_custom_call" | custom-call | flops 4000000000 | bytes 1048576 | tf_op jit(solution)/shard_map/pallas_call | solution.py:815
  471.5 11.2 %shard_map.218 = (f32[1024,256]{1,0:T(8,128)}, f32[256,256]{1,0:T(8,128)}, f32[256,256]{1,0:T(8,128)}, f32[256,1024]{1,0:T(8,128)}, f32[256,512]{1,0:T(8,128)}, ...) custom-call(bf16[4,320,256]{2,1,0:T(8,128)(2,1)} %get-tuple-element., ...), custom_call_target="tpu_custom_call" | custom-call | flops 4000000000 | bytes 1048576 | tf_op jit(solution)/shard_map/pallas_call | solution.py:815
  482.8 1.3 fusion
  (7 shorter events, 0.1 us)
Async XLA Ops:
  0.6 3.7 copy-start
  2.1 2.4 copy-start.3
  2.1 2.4 copy-start.4
  2.1 2.4 copy-start.1
  4.6 1.1 copy-start.2
